TPU v7x, 128 devices: a whole 4x4x4 slice. The times are simulated.
128 devices in a mesh: stream: 32 (over x, y, core), span: 4 (over z).
Axes of the slice: x: 4, y: 4, z: 4, core: 2. Of those that a mesh axis runs over, the one named last changes fastest.
Arguments:
- rhs: float32 [512, 32, 5, 128], P('stream', 'span'), may hold values from -0.8 to 0.8
- adjoint: float32 [512, 32, 5, 128], P('stream', 'span'), may hold values from -6 to 6
- diag_x: float32 [512, 32, 5, 5, 128], P('stream', 'span'), may hold values from -0.3 to 0.6
- lower_x: float32 [512, 32, 5, 5, 128], P('stream', 'span'), may hold values from -1 to 1
- upper_x: float32 [512, 32, 5, 5, 128], P('stream', 'span'), may hold values from -1 to 1
- diag_y: float32 [512, 32, 5, 5, 128], P('stream', 'span'), may hold values from -0.3 to 0.6
- lower_y: float32 [512, 32, 5, 5, 128], P('stream', 'span'), may hold values from -1 to 1
- upper_y: float32 [512, 32, 5, 5, 128], P('stream', 'span'), may hold values from -1 to 1
- metric: bfloat16 [512, 32, 3, 5, 128], P('stream', 'span'), may hold values from -0.25 to 0.25
- node_cell: int32 [32, 4, 128], P('stream', 'span'), may hold values from 0 to 127, each once within a row
- node_owner: int32 [32, 4, 128], P('stream', 'span'), may hold values from 0 to 2047
- node_weight: float32 [32, 4, 128], P('stream', 'span'), may hold values from 0.2 to 1
- node_count: int32 [32, 4], P('stream', 'span'), may hold values from 16 to 128, as said below
Outputs:
- adjoint_new: float32 [512, 32, 5, 128], P('stream', 'span')
- control_grad: float32 [3, 2048], P(None, ('stream', 'span'))
Inputs may be any that keep to these rules, and one draw needn't show every extreme that they name: `node_cell`: each block's list names every one of its wall cells once. Only the first node_count slots of a block are surface nodes.
All inputs are finite; a program needn't handle non-finite values.
Results may differ from a plain program's by a relative error of at most 0.0003.
Values sent between devices are 32-bit elements; how exact they have to be, the bound alone decides.
No kernel may reach another device: no remote copies, remote signals or barrier semaphores. Data moves between devices by JAX's collectives and lax.ppermute only.
A program may use at most 64 MiB of HBM per device.

v0:
```python
import jax
import jax.numpy as jnp
from jax import lax
from jax.sharding import PartitionSpec as P

CP_DEV = 16


def entering(value, axis, combine, identity, reverse):
    count, index = (lax.axis_size(axis), lax.axis_index(axis))
    everything = jax.tree.map(lambda part: lax.all_gather(part, axis), value)
    start = jax.tree.map(
        lambda part, zero: jnp.broadcast_to(jnp.asarray(zero, part.dtype), part.shape),
        value,
        identity,
    )

    def lap(k, before):
        at = count - 1 - k if reverse else k
        reached = at > index if reverse else at < index
        new = combine(before, jax.tree.map(lambda part: part[at], everything))
        return jax.tree.map(lambda a, b: jnp.where(reached, a, b), new, before)

    return lax.fori_loop(0, count, lap, start)


def act_on(matrix, vector):
    return jnp.sum(matrix * vector[..., None, :, :], axis=-2)


def compose(later, earlier):
    return jnp.sum(later[..., :, :, None, :] * earlier[..., None, :, :, :], axis=-3)


def without(dims, split_axis):
    return tuple((extent for place, extent in enumerate(dims) if place != split_axis))


def block_map(driving, coupling, split_axis, reverse):
    matrix_shape = without(coupling.shape, split_axis)
    start = (
        jnp.broadcast_to(jnp.eye(5, dtype=jnp.float32)[:, :, None], matrix_shape),
        jnp.zeros(without(driving.shape, split_axis), jnp.float32),
    )

    def advance(current, source, magnitude_multiplier):
        return (
            compose(-magnitude_multiplier, current[0]),
            source - act_on(magnitude_multiplier, current[1]),
        )

    if split_axis == 0:
        result, _ = lax.scan(
            lambda current, inputs: (advance(current, inputs[0], inputs[1]), None),
            start,
            (driving, coupling),
            reverse=reverse,
        )
        return result
    sequence = list(range(driving.shape[1]))
    if reverse:
        sequence = sequence[::-1]
    current = start
    for lattice_coordinate in sequence:
        current = advance(current, driving[:, lattice_coordinate], coupling[:, lattice_coordinate])
    return current


def replay(driving, coupling, incoming, split_axis, reverse):

    def advance(previous, source, magnitude_multiplier):
        return source - act_on(magnitude_multiplier, previous)

    if split_axis == 0:

        def scanned(previous, inputs):
            fresh = advance(previous, inputs[0], inputs[1])
            return (fresh, fresh)

        _, states = lax.scan(scanned, incoming, (driving, coupling), reverse=reverse)
        return states
    length = driving.shape[1]
    sequence = list(range(length))
    if reverse:
        sequence = sequence[::-1]
    states = [None] * length
    previous = incoming
    for lattice_coordinate in sequence:
        previous = advance(
            previous, driving[:, lattice_coordinate], coupling[:, lattice_coordinate]
        )
        states[lattice_coordinate] = previous
    return jnp.stack(states, axis=1)


def carried(matrices, vectors, direction):
    identity = (
        jnp.broadcast_to(jnp.eye(5, dtype=jnp.float32)[:, :, None], matrices.shape),
        jnp.zeros_like(vectors),
    )

    def combine(earlier, later):
        return (compose(later[0], earlier[0]), act_on(later[0], earlier[1]) + later[1])

    if direction == "stream_fore":
        result = entering((matrices, vectors), "stream", combine, identity, False)[1]
    elif direction == "stream_back":
        result = entering((matrices, vectors), "stream", combine, identity, True)[1]
    elif direction == "span_fore":
        result = entering((matrices, vectors), "span", combine, identity, False)[1]
    else:
        result = entering((matrices, vectors), "span", combine, identity, True)[1]
    return result


def shards(
    rhs,
    adjoint,
    diag_x,
    lower_x,
    upper_x,
    diag_y,
    lower_y,
    upper_y,
    metric,
    node_cell,
    node_owner,
    node_weight,
    node_count,
):
    driven = act_on(diag_x, rhs)
    matrices, vectors = block_map(driven, lower_x, 0, False)
    forward = replay(driven, lower_x, carried(matrices, vectors, "stream_fore"), 0, False)
    matrices, vectors = block_map(forward, upper_x, 0, True)
    stream_done = replay(forward, upper_x, carried(matrices, vectors, "stream_back"), 0, True)
    driven = act_on(diag_y, stream_done)
    matrices, vectors = block_map(driven, lower_y, 1, False)
    span_forward = replay(driven, lower_y, carried(matrices, vectors, "span_fore"), 1, False)
    matrices, vectors = block_map(span_forward, upper_y, 1, True)
    update = replay(span_forward, upper_y, carried(matrices, vectors, "span_back"), 1, True)
    adjoint_new = adjoint + update
    points = CP_DEV * lax.axis_size("stream") * lax.axis_size("span")
    surface = jnp.sum(metric.astype(jnp.float32) * adjoint_new[:, :, None], axis=(3, 4))
    flat_surface = surface.transpose(2, 0, 1).reshape(3, -1)
    wall_cells = node_cell.reshape(-1)
    picked = flat_surface[:, wall_cells]
    in_use = (jnp.arange(wall_cells.shape[0], dtype=jnp.int32) < node_count.reshape(())).astype(
        jnp.float32
    )
    weighted = picked * (node_weight.reshape(-1) * in_use)[None, :]
    owners = (
        node_owner.reshape(-1)[:, None] == jnp.arange(points, dtype=jnp.int32)[None, :]
    ).astype(jnp.float32)
    node_terms = jnp.dot(
        weighted, owners, precision=lax.Precision.HIGHEST, preferred_element_type=jnp.float32
    )
    control = lax.psum_scatter(node_terms, ("stream", "span"), scatter_dimension=1, tiled=True)
    return (adjoint_new, control)


def solution(mesh):
    placed = (
        P("stream", "span", None, None),
        P("stream", "span", None, None),
        P("stream", "span", None, None, None),
        P("stream", "span", None, None, None),
        P("stream", "span", None, None, None),
        P("stream", "span", None, None, None),
        P("stream", "span", None, None, None),
        P("stream", "span", None, None, None),
        P("stream", "span", None, None, None),
        P("stream", "span", None),
        P("stream", "span", None),
        P("stream", "span", None),
        P("stream", "span"),
    )
    return jax.shard_map(
        shards,
        mesh=mesh,
        in_specs=placed,
        out_specs=(P("stream", "span", None, None), P(None, ("stream", "span"))),
        check_vma=False,
    )
```

profile of v0, /device:TPU:1, one launch (start us, length us, event | category | flops | bytes accessed | tf_op | source)
XLA Modules:
  0.0 996.0 jit_solution(8943422585114054519)
XLA Ops:
  7.2 1.7 multiply_reduce_fusion.3
  9.0 16.4 %while.120 = (s32[]{:T(128)}, f32[8,5,5,128]{3,0,2,1:T(8,128)S(1)}, f32[8,5,128]{2,0,1:T(8,128)S(1)}, f32[16,8,5,5,128]{4,1,3,2,0:T(8,128)}, f32[16,8,5,128]{3,1,2,0:T(8,128)S(1)}, /*index=5*/s32[]{:T(128)}, s32[]{:T(128)}) while((s32[]{:T(128)}, f32[8,5,5,128]{3,0,2,1:T(8,128)S(1)}, f32[8,5,128]{2,0,1:T(8,128)S(1)}, ...), condition=%wide.region_4.5_spmd.clone, body=%wide.region_1.4_spmd.clone.sunk | while | flops 312323 | bytes 860255 | solution.py:53
  9.0 0.9 fusion.94
  10.0 0.9 fusion.94
  11.1 0.9 fusion.94
  12.1 0.9 fusion.94
  13.1 0.9 fusion.94
  14.2 0.9 fusion.94
  15.2 0.9 fusion.94
  16.2 0.9 fusion.94
  17.2 0.9 fusion.94
  18.3 0.9 fusion.94
  19.3 0.9 fusion.94
  20.3 0.9 fusion.94
  21.3 0.9 fusion.94
  22.4 0.9 fusion.94
  23.4 0.9 fusion.94
  24.4 0.9 fusion.94
  26.2 26.7 %all-gather.1 = f32[256,5,128]{2,0,1:T(8,128)S(1)} all-gather(f32[8,5,128]{2,0,1:T(8,128)S(1)} %get-tuple-element.717), channel_id=3, replica_groups=mesh['stream'=32,'span'=4] {'stream'}, dimensions={0}, use_global_device_ids=true | all-gather | bytes 675840 | tf_op jit(solution)/shard_map/all_gather | solution.py:11
  52.8 24.6 %all-gather.9.cloned.1.call-done = f32[256,5,5,128]{3,0,2,1:T(8,128)} async-done(((f32[8,5,5,128]{3,0,2,1:T(8,128)}), f32[256,5,5,128]{3,0,2,1:T(8,128)}) %all-gather.9.cloned.1.call-update) | async-done | bytes 3276816 | tf_op jit(solution)/shard_map/all_gather | solution.py:11
  77.4 33.9 %while.121 = (s32[]{:T(128)}, f32[8,5,128]{2,1,0:T(8,128)S(1)}, s32[]{:T(128)}, f32[32,8,5,5,128]{4,1,0,3,2:T(8,128)}, f32[32,8,5,128]{3,1,0,2:T(8,128)S(1)}, /*index=5*/s32[]{:T(128)}, s32[]{:T(128)}) while((s32[]{:T(128)}, f32[8,5,128]{2,1,0:T(8,128)S(1)}, s32[]{:T(128)}, f32[32,8,5,5,128]{4,1,0,3,2:T(8,128)}, ...), condition=%wide.region_7.8_spmd.clone, body=%wide.region_5.7_spmd.clone.sunk | while | flops 66564 | bytes 512106 | solution.py:24
  111.4 15.5 %while.118 = (s32[]{:T(128)}, f32[8,5,128]{2,0,1:T(8,128)S(1)}, f32[16,8,5,128]{3,1,2,0:T(8,128)S(1)}, f32[16,8,5,128]{3,1,2,0:T(8,128)S(1)}, f32[16,8,5,5,128]{4,1,3,2,0:T(8,128)}, /*index=5*/s32[]{:T(128)}) while((s32[]{:T(128)}, f32[8,5,128]{2,0,1:T(8,128)S(1)}, f32[16,8,5,128]{3,1,2,0:T(8,128)S(1)}, f32[16,8,5,128]{3,1,2,0:T(8,128)S(1)}, ...), condition=%wide.region_10.11_spmd, body=%wide.region_8.10_spmd.sunk | while | flops 56322 | bytes 266321 | solution.py:80
  111.4 0.9 fusion.90
  112.4 0.9 fusion.90
  114.3 0.9 fusion.90
  116.3 0.9 fusion.90
  127.0 16.5 %while.122 = (s32[]{:T(128)}, f32[8,5,5,128]{3,0,2,1:T(8,128)S(1)}, f32[8,5,128]{2,0,1:T(8,128)S(1)}, f32[16,8,5,5,128]{4,1,3,2,0:T(8,128)}, f32[16,8,5,128]{3,1...) while((s32[]{:T(128)}, f32[8,5,5,128]{3,0,2,1:T(8,128)S(1)}, ...), condition=%wide.region_14.15_spmd.clone, body=%wide.region_11.14_spmd.clone.sunk | while | flops 312324 | bytes 860275 | solution.py:53
  127.0 0.9 fusion.97
  128.1 0.9 fusion.97
  129.1 0.9 fusion.97
  130.1 0.9 fusion.97
  131.2 0.9 fusion.97
  132.2 0.9 fusion.97
  133.2 0.9 fusion.97
  134.2 0.9 fusion.97
  135.3 0.9 fusion.97
  136.3 0.9 fusion.97
  137.3 0.9 fusion.97
  138.4 0.9 fusion.97
  139.4 0.9 fusion.97
  140.4 0.9 fusion.97
  141.5 0.9 fusion.97
  142.5 0.9 fusion.97
  145.5 7.8 fusion.73
  153.3 1.8 fusion.74
  155.9 1.0 multiply_reduce_fusion.11
  157.4 26.6 %all-gather.3 = f32[256,5,128]{2,0,1:T(8,128)} all-gather(f32[8,5,128]{2,0,1:T(8,128)S(1)} %get-tuple-element.721), channel_id=5, replica_groups=mesh['stream'=32,'span'=4] {'stream'}, dimensions={0}, use_global_device_ids=true | all-gather | bytes 675840 | tf_op jit(solution)/shard_map/all_gather | solution.py:11
  184.0 7.0 all-gather.11.cloned.1.call-done
  191.0 56.7 %while.123 = (s32[]{:T(128)}, f32[8,5,128]{2,1,0:T(8,128)S(1)}, s32[]{:T(128)}, f32[32,8,5,5,128]{4,1,0,3,2:T(8,128)}, f32[32,8,5,128]{3,1,0,2:T(8,128)}, /*index=5*/s32[]{:T(128)}, s32[]{:T(128)}, s32[]{:T(128)}, s32[]{:T(128)}) while((s32[]{:T(128)}, f32[8,5,128]{2,1,0:T(8,128)S(1)}, s32[]{:T(128)}, ...), condition=%wide.region_17.18_spmd.clone, body=%wide.region_15.17_spmd.clone.sunk | while | flops 66568 | bytes 512168 | solution.py:24
  247.7 38.1 %while.119 = (s32[]{:T(128)}, f32[8,5,128]{2,0,1:T(8,128)S(1)}, f32[16,8,5,128]{3,1,2,0:T(8,128)S(1)}, f32[16,8,5,128]{3,1,2,0:T(8,128)}, f32[16,8,5,5,128]{4,1,3,2,0:T(8,128)}, /*index=5*/s32[]{:T(128)}, s32[]{:T(128)}) while((s32[]{:T(128)}, f32[8,5,128]{2,0,1:T(8,128)S(1)}, f32[16,8,5,128]{3,1,2,0:T(8,128)S(1)}, ...), condition=%wide.region_20.21_spmd, body=%wide.region_18.20_spmd.sunk | while | flops 56323 | bytes 266341 | solution.py:80
  247.7 0.9 fusion.92
  285.8 1.7 multiply_reduce_fusion.2
  288.5 10.5 %all_gather.54 = f32[4,16,5,128]{3,1,2,0:T(8,128)} all-gather(f32[1,16,5,128]{3,1,2,0:T(8,128)S(1)} %bitcast_subtract_fusion.31), channel_id=1, replica_groups=mesh['stream'=32,'span'=4] {'span'}, dimensions={0}, use_global_device_ids=true | all-gather | bytes 204800 | tf_op jit(solution)/shard_map/all_gather | solution.py:11
  299.6 10.9 %all-gather.4 = f32[64,5,5,128]{3,0,2,1:T(8,128)S(1)} all-gather(f32[16,5,5,128]{3,0,2,1:T(8,128)S(1)} %multiply_reduce_fusion.12), channel_id=6, replica_groups=mesh['stream'=32,'span'=4] {'span'}, dimensions={0}, use_global_device_ids=true | all-gather | bytes 1024000 | tf_op jit(solution)/shard_map/all_gather | solution.py:11
  310.5 4.2 while.124
  314.8 1.0 fusion.70
  315.8 0.9 multiply_reduce_fusion.43
  317.5 0.9 multiply_reduce_fusion.42
  320.4 9.7 all_gather.57
  330.7 11.1 %all-gather.5 = f32[64,5,5,128]{3,0,2,1:T(8,128)S(1)} all-gather(f32[16,5,5,128]{3,0,2,1:T(8,128)S(1)} %multiply_reduce_fusion.4), channel_id=7, replica_groups=mesh['stream'=32,'span'=4] {'span'}, dimensions={0}, use_global_device_ids=true | all-gather | bytes 1024000 | tf_op jit(solution)/shard_map/all_gather | solution.py:11
  341.8 1.2 while.125
  345.6 2.1 convolution_bitcast_fusion
  347.7 640.5 %reduce-scatter.4.cloned.1.call-done = f32[16,3]{1,0:T(8,128)} async-done(((f32[2048,3]{1,0:T(8,128)}), f32[16,3]{1,0:T(8,128)}) %reduce-scatter.4.cloned.1.call-update) | async-done | bytes 208
  988.1 1.3 copy.429
  (759 shorter events, 153.8 us)
Async XLA Ops:
  7.2 70.3 %all-gather.9.cloned.1.call-start = ((), (), s32[]{:S(2)}) async-start(), calls=%async_computation.1 | async-start | bytes 3379200 | tf_op jit(solution)/shard_map/all_gather | solution.py:11
  25.4 0.6 copy-start
  26.1 164.9 %all-gather.11.cloned.1.call-start = ((), (), s32[]{:S(2)}) async-start(), calls=%async_computation.2 | async-start | bytes 3379200 | tf_op jit(solution)/shard_map/all_gather | solution.py:11
  127.0 17.9 %copy-start.33 = (s32[1,1,128]{2,1,0:T(1,128)S(1)}, s32[1,1,128]{2,1,0:T(1,128)}, u32[]{:S(2)}) copy-start(s32[1,1,128]{2,1,0:T(1,128)} %param.38) | copy-start | bytes 1540
  143.5 0.7 copy-start.1
  143.5 1.4 copy-start.10
  144.2 844.0 %reduce-scatter.4.cloned.1.call-start = ((), (), s32[]{:S(2)}) async-start(), calls=%async_computation.3 | async-start | bytes 1056768
  145.5 7.8 copy-start.8
  155.1 132.8 %copy-start.6 = (f32[16,1,5,5,128]{4,1,3,2,0:T(1,128)}, f32[16,1,5,5,128]{4,1,3,2,0:T(1,128)S(1)}, u32[]{:S(2)}) copy-start(f32[16,1,5,5,128]{4,1,3,2,0:T(1,128)S(1)} %get-tuple-element.1074) | copy-start | bytes 614404
  155.1 132.9 %copy-start.4 = (f32[16,1,5,5,128]{4,1,3,2,0:T(1,128)}, f32[16,1,5,5,128]{4,1,3,2,0:T(1,128)S(1)}, u32[]{:S(2)}) copy-start(f32[16,1,5,5,128]{4,1,3,2,0:T(1,128)S(1)} %get-tuple-element.1076) | copy-start | bytes 614404
  155.1 133.0 %copy-start.2 = (f32[16,1,5,5,128]{4,1,3,2,0:T(1,128)}, f32[16,1,5,5,128]{4,1,3,2,0:T(1,128)S(1)}, u32[]{:S(2)}) copy-start(f32[16,1,5,5,128]{4,1,3,2,0:T(1,128)S(1)} %get-tuple-element.1077) | copy-start | bytes 614404
  155.1 1.7 copy-start.34
  285.8 2.0 copy-start.30
  285.8 2.0 copy-start.7
  287.8 0.6 copy-start.11
  287.8 0.6 copy-start.20
  287.8 0.6 copy-start.22
  287.8 0.6 copy-start.24
  287.8 0.6 copy-start.26
  287.8 0.6 copy-start.27
  287.8 0.6 copy-start.18
  288.0 11.0 %copy-start.14 = (f32[16,5,5,128]{3,0,2,1:T(8,128)S(1)}, f32[16,5,5,128]{3,0,2,1:T(8,128)}, u32[]{:S(2)}) copy-start(f32[16,5,5,128]{3,0,2,1:T(8,128)} %get-tuple-element.979) | copy-start | bytes 614404
  314.7 4.6 copy-start.25
  314.7 4.6 copy-start.5
  314.7 4.6 copy-start.23
  314.7 4.6 copy-start.3
  314.8 4.7 copy-start.21
  314.8 4.7 copy-start.19
  314.8 4.8 copy-start.29
  314.8 5.1 copy-start.15
  319.6 0.8 copy-start.12
  319.7 10.5 %copy-start.13 = (f32[16,5,5,128]{3,0,2,1:T(8,128)S(1)}, f32[16,5,5,128]{3,0,2,1:T(8,128)}, u32[]{:S(2)}) copy-start(f32[16,5,5,128]{3,0,2,1:T(8,128)} %get-tuple-element.978) | copy-start | bytes 614404
  343.1 0.8 copy-start.16
  343.2 1.0 copy-start.28
  343.4 1.1 copy-start.17
  343.9 1.7 copy-start.31
  343.9 1.7 copy-start.32
  344.4 645.1 %copy-start.9 = (f32[16,8,5,128]{3,1,2,0:T(8,128)}, f32[16,8,5,128]{3,1,2,0:T(8,128)S(1)}, u32[]{:S(2)}) copy-start(f32[16,8,5,128]{3,1,2,0:T(8,128)S(1)} %copy.427) | copy-start | bytes 983044
Sparse Core Ops, SparseCore 0:
  26.2 51.1 all-gather.8
  144.3 46.6 all-gather.10
  347.8 640.3 reduce-scatter.3
where the time goes:
time: 1010 us; the launch traced here: 996 us
  waiting for transfers between devices  672 us (67%)
  other arithmetic  105 us (10%)
  local copies, waits for them, and re-layouts  101 us (10%)
  blocking collectives  95.4 us (9%)
  between operations  15.5 us (2%)
    unnamed x4, waiting for transfers between devices  641 us
    all_gather x6, blocking collectives, entering(): everything = jax.tree.map(lambda part: lax.all_gather(part, axis), value)  95.4 us
    dynamic_slice x144, local copies, waits for them, and re-layouts, lap(): new = combine(before, jax.tree.map(lambda part: part[at], everything))  85.4 us
    reduce_sum x169, other arithmetic, act_on(): return jnp.sum(matrix * vector[..., None, :, :], axis=-2)  70.8 us
    all_gather x2, waiting for transfers between devices, entering(): everything = jax.tree.map(lambda part: lax.all_gather(part, axis), value)  31.6 us
  transfers between devices with their start and end apart: 3, of which 3 were waited for; matrix products, arithmetic and copies ran while one was open for 1% of the time, Pallas kernels for 0%

commit v1 on v0

v1 whole, which is shorter than its diff:
```python
import jax
import jax.numpy as jnp
from jax import lax
from jax.experimental import pallas as pl
from jax.experimental.pallas import tpu as pltpu
from jax.sharding import PartitionSpec as P

SX, SY, NN = 16, 8, 128
XS = 32
ROWS = 24
VMEM = 56 * 1024 * 1024


def act(m, v):
    out = []
    for a in range(5):
        t = m[5 * a] * v[0]
        for b in range(1, 5):
            t = t + m[5 * a + b] * v[b]
        out.append(t)
    return out


def act_cols(m, f):
    cols = [act(m, [f[5 * b + c] for b in range(5)]) for c in range(5)]
    return [cols[c][a] for a in range(5) for c in range(5)]


def add(p, q):
    return [x + y for x, y in zip(p, q)]


def sub(p, q):
    return [x - y for x, y in zip(p, q)]


def lanes_quarter(shape):
    return lax.shift_right_logical(lax.broadcasted_iota(jnp.int32, shape, 1), 5)


def maps_kernel(z_ref, rhs, dx, lx, ux, ly, uy, msg, driven, mats, matsel, fs, gs, fy):
    def tiles(ref, i, n=25):
        return [ref[i, k] for k in range(n)]

    def put(ref, i, vals):
        for k, v in enumerate(vals):
            ref[i, k] = v

    d = act(tiles(dx, 0), tiles(rhs, 0, 5))
    put(driven, 0, d)
    put(gs, 0, d)
    f = tiles(lx, 0)
    put(fs, 0, f)

    def fore(i, carry):
        g, f = carry
        l = tiles(lx, i)
        d = act(tiles(dx, i), tiles(rhs, i, 5))
        put(driven, i, d)
        g = sub(d, act(l, g))
        put(gs, i, g)
        f = act_cols(l, f)
        put(fs, i, f)
        return g, f

    g, f = lax.fori_loop(1, SX, fore, (d, f))

    def back(k, carry):
        i = SX - 2 - k
        b, c = carry
        u = tiles(ux, i)
        b = sub(tiles(gs, i, 5), act(u, b))
        c = add(tiles(fs, i), act_cols(u, c))
        return b, c

    b, c = lax.fori_loop(0, SX - 1, back, (g, f))

    def back_map(k, bm):
        return act_cols(tiles(ux, SX - 2 - k), bm)

    bm = lax.fori_loop(0, SX - 1, back_map, tiles(ux, SX - 1))
    zero = jnp.zeros((SY, NN), jnp.float32)
    values = f + g + bm + b + [-x for x in c] + [zero] * 3
    quarter = lanes_quarter((SY, NN))
    for r in range(22):
        four = values[4 * r : 4 * r + 4]
        for nq in range(4):
            out = None
            for kk in range(4):
                shift = (32 * (kk - nq)) % 128
                part = four[kk] if shift == 0 else pltpu.roll(four[kk], shift, 1)
                out = part if out is None else jnp.where(quarter == kk, part, out)
            msg[pl.ds(nq * 8 * ROWS + r, 8, ROWS), :] = out
    for r in range(22, ROWS):
        for nq in range(4):
            msg[pl.ds(nq * 8 * ROWS + r, 8, ROWS), :] = zero

    last = z_ref[0] == 3
    for h in range(2):
        def turned(ref, y):
            return [ref[pl.ds(h * 1600 + k * 8 + y, 8, 200), :] for k in range(25)]

        f = turned(ly, 0)
        put(fy, 0, f)

        def fore_y(y, f):
            f = act_cols(turned(ly, y), f)
            put(fy, y, f)
            return f

        f = lax.fori_loop(1, SY, fore_y, f)
        for k in range(25):
            mats[k, pl.ds(h * 8, 8), :] = f[k]

        def back_y(k, c):
            y = SY - 2 - k
            return add(tiles(fy, y), act_cols(turned(uy, y), c))

        c = lax.fori_loop(0, SY - 1, back_y, f)
        for k in range(25):
            mats[50 + k, pl.ds(h * 8, 8), :] = -c[k]
            matsel[k, pl.ds(h * 8, 8), :] = jnp.where(last, -c[k], mats[k, pl.ds(h * 8, 8), :])

        def back_map_y(k, bm):
            return act_cols(turned(uy, SY - 2 - k), bm)

        bm = lax.fori_loop(0, SY - 1, back_map_y, turned(uy, SY - 1))
        for k in range(25):
            mats[25 + k, pl.ds(h * 8, 8), :] = bm[k]


def solve_kernel(got, out, un, fin, sin):
    un[0] = got[...]
    for q in range(1, 4):
        for p in range(XS):
            un[q, p] = pltpu.roll(got[p], 128 - 32 * q, 1)

    def val(p, k):
        return un[k % 4, p, (k // 4) : (k // 4) + 1, :]

    zero = [jnp.zeros((1, NN), jnp.float32)] * 5

    def fore(p, f):
        for j in range(5):
            fin[p, j : j + 1, :] = f[j]
        return add(act([val(p, k) for k in range(25)], f), [val(p, 25 + j) for j in range(5)])

    lax.fori_loop(0, XS, fore, zero)

    def back(k, s):
        p = XS - 1 - k
        for j in range(5):
            sin[p, j : j + 1, :] = s[j]
        f = [fin[p, j : j + 1, :] for j in range(5)]
        known = add(act([val(p, 60 + k) for k in range(25)], f), [val(p, 55 + j) for j in range(5)])
        return add(known, act([val(p, 30 + k) for k in range(25)], s))

    lax.fori_loop(0, XS, back, zero)
    quarter = lanes_quarter((8, NN))
    for p in range(XS):
        out[p] = jnp.where(quarter == 0, fin[p], pltpu.roll(sin[p], 32, 1))


def replay_kernel(got, driven, lx, ux, dy, ly, uy, dturn, vec, fs, sd, gt):
    quarter = lanes_quarter((SY, NN))

    def entering(j, at):
        out = None
        for nq in range(4):
            part = got[pl.ds(nq * 64 + j, 8, 8), :]
            shift = (32 * nq - 32 * at) % 128
            part = part if shift == 0 else pltpu.roll(part, shift, 1)
            out = part if out is None else jnp.where(quarter == nq, part, out)
        return out

    def tiles(ref, i, n=25):
        return [ref[i, k] for k in range(n)]

    def fore(i, f):
        f = sub(tiles(driven, i, 5), act(tiles(lx, i), f))
        for a in range(5):
            fs[i, a] = f[a]
        return f

    lax.fori_loop(0, SX, fore, [entering(j, 0) for j in range(5)])

    def back(k, s):
        i = SX - 1 - k
        s = sub(tiles(fs, i, 5), act(tiles(ux, i), s))
        d = act(tiles(dy, i), s)
        for a in range(5):
            sd[pl.ds(pl.multiple_of((i * 5 + a) * 8, 8), 8), :] = d[a]
        return s

    lax.fori_loop(0, SX, back, [entering(j, 1) for j in range(5)])

    for h in range(2):
        def turned(ref, y):
            return [ref[pl.ds(h * 1600 + k * 8 + y, 8, 200), :] for k in range(25)]

        g = None
        for y in range(SY):
            d = [sd[pl.ds(h * 320 + a * 8 + y, 8, 40), :] for a in range(5)]
            for a in range(5):
                dturn[y, a, pl.ds(h * 8, 8), :] = d[a]
            g = d if g is None else sub(d, act(turned(ly, y), g))
            for a in range(5):
                gt[y, a] = g[a]
        for a in range(5):
            vec[a, pl.ds(h * 8, 8), :] = g[a]
        b = g
        for y in range(SY - 2, -1, -1):
            b = sub([gt[y, a] for a in range(5)], act(turned(uy, y), b))
        for a in range(5):
            vec[5 + a, pl.ds(h * 8, 8), :] = b[a]


def finish_kernel(z_ref, count, v1, v2, v3, m1, m2, m3, dturn, ly, uy, adjoint, metric, cell, owner,
                  weight, new, part, fin, sin, ft, ut, pk):
    z = z_ref[0]
    halves = [pl.ds(0, 8), pl.ds(8, 8)]
    zero = jnp.zeros((8, NN), jnp.float32)

    def a_of(v, h):
        return [v[j, halves[h], :] for j in range(5)]

    def b_of(v, h):
        return [v[5 + j, halves[h], :] for j in range(5)]

    def mat(m, at, h):
        return [m[25 * at + k, halves[h], :] for k in range(25)]

    def put_in(h, f):
        for j in range(5):
            fin[j, halves[h], :] = f[j]

    for h in range(2):
        @pl.when(z == 0)
        def _():
            put_in(h, [zero] * 5)

        @pl.when(z == 1)
        def _():
            put_in(h, a_of(v3, h))

        @pl.when(z == 2)
        def _():
            put_in(h, add(a_of(v3, h), act(mat(m3, 0, h), a_of(v2, h))))

        @pl.when(z == 3)
        def _():
            f = add(a_of(v2, h), act(mat(m2, 0, h), a_of(v1, h)))
            put_in(h, add(a_of(v3, h), act(mat(m3, 0, h), f)))

    def turned(ref, y, h):
        return [ref[pl.ds(h * 1600 + k * 8 + y, 8, 200), :] for k in range(25)]

    for h in range(2):
        f = [fin[j, halves[h], :] for j in range(5)]
        for y in range(SY):
            f = sub([dturn[y, a, halves[h], :] for a in range(5)], act(turned(ly, y, h), f))
            for a in range(5):
                ft[y, a, halves[h], :] = f[a]

    def put_back(h, s):
        for j in range(5):
            sin[j, halves[h], :] = s[j]

    for h in range(2):
        def own(h=h):
            return [ft[SY - 1, a, halves[h], :] for a in range(5)]

        @pl.when(z == 0)
        def _():
            f1 = own()
            f2 = add(a_of(v1, h), act(mat(m1, 0, h), f1))
            f3 = add(a_of(v2, h), act(mat(m2, 0, h), f2))
            s3 = add(b_of(v3, h), act(mat(m3, 0, h), f3))
            s2 = add(add(b_of(v2, h), act(mat(m2, 2, h), f2)), act(mat(m2, 1, h), s3))
            put_back(h, add(add(b_of(v1, h), act(mat(m1, 2, h), f1)), act(mat(m1, 1, h), s2)))

        @pl.when(z == 1)
        def _():
            f2 = own()
            f3 = add(a_of(v1, h), act(mat(m1, 0, h), f2))
            s3 = add(b_of(v2, h), act(mat(m2, 2, h), f3))
            put_back(h, add(add(b_of(v1, h), act(mat(m1, 2, h), f2)), act(mat(m1, 1, h), s3)))

        @pl.when(z == 2)
        def _():
            put_back(h, add(b_of(v1, h), act(mat(m1, 2, h), own())))

        @pl.when(z == 3)
        def _():
            put_back(h, [zero] * 5)

    for h in range(2):
        s = [sin[j, halves[h], :] for j in range(5)]
        for y in range(SY - 1, -1, -1):
            s = sub([ft[y, a, halves[h], :] for a in range(5)], act(turned(uy, y, h), s))
            for a in range(5):
                ut[pl.ds((y * 5 + a) * 16 + h * 8, 8), :] = s[a]

    for x in range(SX):
        fresh = []
        for a in range(5):
            fresh.append(adjoint[x, a] + ut[pl.ds(a * 16 + x, 8, 80), :])
            new[x, a] = fresh[a]
        for k in range(3):
            t = metric[x, 5 * k].astype(jnp.float32) * fresh[0]
            for a in range(1, 5):
                t = t + metric[x, 5 * k + a].astype(jnp.float32) * fresh[a]
            pk[k, pl.ds(x * 8, 8), :] = t

    row = lax.broadcasted_iota(jnp.int32, (128, 128), 0)
    lane = lax.broadcasted_iota(jnp.int32, (128, 128), 1)
    here = cell[...] == row
    used = jnp.logical_and(here, lane < count[0])
    w = jnp.sum(jnp.where(used, weight[...], 0.0), axis=1, keepdims=True)
    who = jnp.sum(jnp.where(here, owner[...].astype(jnp.float32), 0.0), axis=1, keepdims=True)
    who = who.astype(jnp.int32)
    surface = [jnp.sum(pk[k], axis=1, keepdims=True) * w for k in range(3)]
    which = lax.shift_right_logical(lane, 4)
    picked = jnp.where(which == 0, surface[0], jnp.where(which == 1, surface[1], surface[2]))
    picked = jnp.where(jnp.logical_and(lane < 48, (lane & 15) == (who & 15)), picked, 0.0)
    target = (lax.shift_right_logical(who, 4) == lane).astype(jnp.float32)
    part[...] = lax.dot_general(target, picked, (((0,), (0,)), ((), ())),
                                precision=lax.Precision.HIGHEST, preferred_element_type=jnp.float32)


def call(kernel, outs, scratch, smem=0, n_in=0):
    f32 = jnp.float32
    return pl.pallas_call(
        kernel,
        out_shape=[jax.ShapeDtypeStruct(s, f32) for s in outs],
        in_specs=[pl.BlockSpec(memory_space=pltpu.SMEM)] * smem
        + [pl.BlockSpec(memory_space=pltpu.VMEM)] * (n_in - smem),
        out_specs=[pl.BlockSpec(memory_space=pltpu.VMEM)] * len(outs),
        scratch_shapes=[pltpu.VMEM(s, f32) for s in scratch],
        compiler_params=pltpu.CompilerParams(vmem_limit_bytes=VMEM),
    )


def shards(rhs, adjoint, diag_x, lower_x, upper_x, diag_y, lower_y, upper_y, metric, node_cell,
           node_owner, node_weight, node_count):
    def blocks(m):
        return m.transpose(0, 2, 3, 1, 4).reshape(SX, -1, SY, NN)

    rhs = rhs.transpose(0, 2, 1, 3)
    adjoint = adjoint.transpose(0, 2, 1, 3)
    dx, lx, ux, dy = blocks(diag_x), blocks(lower_x), blocks(upper_x), blocks(diag_y)
    ly = blocks(lower_y).reshape(-1, NN)
    uy = blocks(upper_y).reshape(-1, NN)
    metric = blocks(metric)
    z = lax.axis_index("span").astype(jnp.int32).reshape(1)

    tile = (SX, 25, SY, NN)
    msg, driven, mats, matsel = call(
        maps_kernel,
        [(XS * ROWS, NN), (SX, 5, SY, NN), (75, SX, NN), (25, SX, NN)],
        [tile, (SX, 5, SY, NN), (SY, 25, 8, NN)],
        smem=1, n_in=7,
    )(z, rhs, dx, lx, ux, ly, uy)
    m1 = lax.ppermute(mats, "span", [(1, 0), (2, 1), (3, 2)])
    m2 = lax.ppermute(mats, "span", [(2, 0), (3, 1), (1, 3)])
    m3 = lax.ppermute(matsel, "span", [(3, 0), (1, 2), (2, 3)])
    got = lax.all_to_all(msg.reshape(XS, ROWS, NN), "stream", 0, 0, tiled=True)
    (back,) = call(
        solve_kernel, [(XS, 8, NN)],
        [(4, XS, ROWS, NN), (XS, 8, NN), (XS, 8, NN)], n_in=1,
    )(got)
    back = lax.all_to_all(back, "stream", 0, 0, tiled=True)
    dturn, vec = call(
        replay_kernel,
        [(SY, 5, SX, NN), (10, SX, NN)],
        [(SX, 5, SY, NN), (SX * 5 * SY, NN), (SY, 5, 8, NN)],
        n_in=7,
    )(back.reshape(XS * 8, NN), driven, lx, ux, dy, ly, uy)
    v = [lax.ppermute(vec, "span", [((i + s) % 4, i) for i in range(4)]) for s in (1, 2, 3)]
    new, part = call(
        finish_kernel,
        [(SX, 5, SY, NN), (128, NN)],
        [(5, SX, NN), (5, SX, NN), (SY, 5, SX, NN), (SY * 5 * SX, NN), (3, 128, NN)],
        smem=2, n_in=16,
    )(z, node_count.reshape(1), *v, m1, m2, m3, dturn, ly, uy, adjoint, metric,
      node_cell.reshape(1, -1), node_owner.reshape(1, -1), node_weight.reshape(1, -1))
    parts = lax.all_to_all(part, ("stream", "span"), 0, 0, tiled=True)
    control = jnp.sum(parts, axis=0)[:48].reshape(3, 16)
    return new.transpose(0, 2, 1, 3), control


def solution(mesh):
    cells, mats = P("stream", "span", None, None), P("stream", "span", None, None, None)
    slots = P("stream", "span", None)
    return jax.shard_map(
        shards,
        mesh=mesh,
        in_specs=(cells,) * 2 + (mats,) * 7 + (slots,) * 3 + (P("stream", "span"),),
        out_specs=(cells, P(None, ("stream", "span"))),
        check_vma=False,
    )
```

time: 1010 us -> 87.6 us (0.09); the launches traced: 996 us -> 87.2 us
  waiting for transfers between devices: 672 us -> 13.4 us
  other arithmetic: 105 us -> 0.15 us
  local copies, waits for them, and re-layouts: 101 us -> 2.45 us
  blocking collectives: 95.4 us -> 27.1 us
  Pallas kernels: 0 us -> 22.2 us
  starting transfers between devices: 0.12 us -> 20.5 us
  between operations: 15.5 us -> 1.37 us
    unnamed x4 -> x0, waiting for transfers between devices: 641 us -> none
    all_gather x6 -> x0, blocking collectives: 95.4 us -> none  [entering(): everything = jax.tree.map(lambda part: lax.all_gather(part, axis), value)]
    dynamic_slice x144 -> x0, local copies, waits for them, and re-layouts: 85.4 us -> none  [lap(): new = combine(before, jax.tree.map(lambda part: part[at], everything))]
    reduce_sum x217 -> x1, other arithmetic: 74.3 us -> 0.15 us  [shards(): control = jnp.sum(parts, axis=0)[:48].reshape(3, 16)]
    all_gather x2 -> x0, waiting for transfers between devices: 31.6 us -> none  [entering(): everything = jax.tree.map(lambda part: lax.all_gather(part, axis), value)]
    all_to_all x0 -> x2, blocking collectives: none -> 27.1 us  [the longest x1 15.2 us: shards(): parts = lax.all_to_all(part, ('stream', 'span'), 0, 0, tiled=True)]
    pallas_call x0 -> x4, Pallas kernels: none -> 22.2 us  [the longest x1 9.13 us: shards(): call(maps_kernel, [(XS * ROWS, NN), (SX, 5, SY, NN), (75, SX, NN), (25, S...]
    sub x72 -> x0, other arithmetic: 14 us -> none  [the longest x38 13.5 us: advance(): return source - act_on(magnitude_multiplier, previous)]
  transfers between devices with their start and end apart: 3 -> 7, of which waited for: 3 -> 4; matrix products, arithmetic and copies ran while one was open for 1% -> 0% of each run, Pallas kernels for 0% -> 10%
where the time goes in v1:
time: 87.6 us; the launch traced here: 87.2 us
  blocking collectives  27.1 us (31%)
  Pallas kernels  22.2 us (25%)
  starting transfers between devices  20.5 us (23%)
  waiting for transfers between devices  13.4 us (15%)
  local copies, waits for them, and re-layouts  2.45 us (3%)
  between operations  1.37 us (2%)
    all_to_all x1, blocking collectives, shards(): parts = lax.all_to_all(part, ('stream', 'span'), 0, 0, tiled=True)  15.2 us
    all_to_all x1, blocking collectives, shards(): back = lax.all_to_all(back, 'stream', 0, 0, tiled=True)  11.9 us
    pallas_call x1, Pallas kernels, shards(): call(maps_kernel, [(XS * ROWS, NN), (SX, 5, SY, NN), (75, SX, NN), (25, S...  9.13 us
    all_to_all x1, waiting for transfers between devices, shards(): got = lax.all_to_all(msg.reshape(XS, ROWS, NN), 'stream', 0, 0, tiled=True)  9 us
    all_to_all x1, starting transfers between devices, shards(): got = lax.all_to_all(msg.reshape(XS, ROWS, NN), 'stream', 0, 0, tiled=True)  8.6 us
    ppermute x3, starting transfers between devices, shards(): lax.ppermute(vec, 'span', [((i + s) % 4, i) for i in range(4)])  8.07 us
    pallas_call x1, Pallas kernels, shards(): call(replay_kernel, [(SY, 5, SX, NN), (10, SX, NN)], [(SX, 5, SY, NN), (S...  5.37 us
    pallas_call x1, Pallas kernels, shards(): call(finish_kernel, [(SX, 5, SY, NN), (128, NN)], [(5, SX, NN), (5, SX, N...  4.59 us
  transfers between devices with their start and end apart: 7, of which 4 were waited for; matrix products, arithmetic and copies ran while one was open for 0% of the time, Pallas kernels for 10%

profile of v1, /device:TPU:1, one launch (start us, length us, event | category | flops | bytes accessed | tf_op | source)
XLA Modules:
  0.0 87.2 jit_solution(6642643117397929046)
XLA Ops:
  0.6 9.1 %shard_map.140 = (f32[768,128]{1,0:T(8,128)}, f32[16,5,8,128]{3,2,1,0:T(8,128)}, f32[75,16,128]{2,1,0:T(8,128)}, f32[25,16,128]{2,1,0:T(8,128)}) custom-call(s32[1]{0:T(128)} %bitcast.z_ref, f32[16,5,8,128]{3,2,1,0:T(8,128)} %bitcast.51, f32[16,25,8,128]{3,2,1,0:T(8,128)} %bitcast.46, f32[16,25,8,128]{3,2,1,0:T(8,128)} %bitcast.42, ...), custom_call_target="tpu_custom_call" | custom-call | tf_op jit(solution)/shard_map/pallas_call | solution.py:358
  9.8 1.3 %collective-permute-start.3 = (f32[75,16,128]{2,1,0:T(8,128)}, f32[75,16,128]{2,1,0:T(8,128)S(1)}, u32[]{:S(2)}, u32[]{:S(2)}) collective-permute-start(f32[75,16,128]{2,1,0:T(8,128)} %get-tuple-element.13), channel_id=1, source_target_pairs={{1,0},{2,1},{3,2},{5,4},{6,5},{7,6},{9,8},{10,9},{11,10},{13,12},{... | collective-permute-start | bytes 1843208 | tf_op jit(solution)/shard_map/ppermute | solution.py:364
  11.0 1.3 %collective-permute-start.4 = (f32[75,16,128]{2,1,0:T(8,128)}, f32[75,16,128]{2,1,0:T(8,128)S(1)}, u32[]{:S(2)}, u32[]{:S(2)}) collective-permute-start(f32[75,16,128]{2,1,0:T(8,128)} %get-tuple-element.13), channel_id=1, source_target_pairs={{2,0},{3,1},{1,3},{6,4},{7,5},{5,7},{10,8},{11,9},{9,11},{14,12},{... | collective-permute-start | bytes 1843208 | tf_op jit(solution)/shard_map/ppermute | solution.py:365
  12.3 8.6 %all-to-all-start = ((f32[32,24,128]{2,1,0:T(8,128)}), f32[32,24,128]{2,1,0:T(8,128)S(1)}, u32[]{:S(2)}, u32[]{:S(2)}) async-start(f32[32,24,128]{2,1,0:T(8,128)} %bitcast.50), calls=%async_computation | async-start | bytes 786432 | tf_op jit(solution)/shard_map/all_to_all | solution.py:367
  21.0 1.3 %collective-permute-start.5 = (f32[25,16,128]{2,1,0:T(8,128)}, f32[25,16,128]{2,1,0:T(8,128)S(1)}, u32[]{:S(2)}, u32[]{:S(2)}) collective-permute-start(f32[25,16,128]{2,1,0:T(8,128)} %get-tuple-element.14), channel_id=1, source_target_pairs={{3,0},{1,2},{2,3},{7,4},{5,6},{6,7},{11,8},{9,10},{10,11},{15,12},... | collective-permute-start | bytes 614408 | tf_op jit(solution)/shard_map/ppermute | solution.py:366
  22.3 9.0 %all-to-all-done.got = f32[32,24,128]{2,1,0:T(8,128)S(1)} async-done(((f32[32,24,128]{2,1,0:T(8,128)}), f32[32,24,128]{2,1,0:T(8,128)S(1)}, u32[]{:S(2)}, u32[]{:S(2)}) %all-to-all-start) | async-done | bytes 393248 | tf_op jit(solution)/shard_map/all_to_all | solution.py:367
  31.3 0.0 copy-start
  31.3 0.7 copy-done
  32.0 3.1 %shard_map.141 = f32[32,8,128]{2,1,0:T(8,128)} custom-call(f32[32,24,128]{2,1,0:T(8,128)} %copy-done), custom_call_target="tpu_custom_call" | custom-call | tf_op jit(solution)/shard_map/pallas_call | solution.py:368
  35.1 11.9 %all_to_all.19 = f32[32,8,128]{2,1,0:T(8,128)} all-to-all(f32[32,8,128]{2,1,0:T(8,128)} %shard_map.141), channel_id=1, replica_groups=mesh['stream'=32,'span'=4] {'stream'}, dimensions={0} | all-to-all | bytes 262144 | tf_op jit(solution)/shard_map/all_to_all | solution.py:372
  47.0 5.4 %shard_map.142 = (f32[8,5,16,128]{3,2,1,0:T(8,128)}, f32[10,16,128]{2,1,0:T(8,128)}) custom-call(f32[256,128]{1,0:T(8,128)} %bitcast.48, f32[16,5,8,128]{3,2,1,0:T(8,128)} %get-tuple-element.11.driven, f32[16,25,8,128]{3,2,1,0:T(8,128)} %bitcast.43, f32[16,25,8,128]{3,2,1,0:T(8,128)} %bitcast.45, f32[16,25,8,128]{3,2,1,0:T(8,128)} %bitcast.47, ...), custom_call_target="tpu_custom_call" | custom-call | tf_op jit(solution)/shard_map/pallas_call | solution.py:373
  52.3 5.7 %collective-permute-start = (f32[10,16,128]{2,1,0:T(8,128)}, f32[10,16,128]{2,1,0:T(8,128)S(1)}, u32[]{:S(2)}, u32[]{:S(2)}) collective-permute-start(f32[10,16,128]{2,1,0:T(8,128)} %get-tuple-element.12), channel_id=1, source_target_pairs={{1,0},{2,1},{3,2},{0,3},{5,4},{6,5},{7,6},{4,7},{9,8},{10,9},{11,1... | collective-permute-start | bytes 245768 | tf_op jit(solution)/shard_map/ppermute | solution.py:379
  58.0 2.4 %collective-permute-start.1 = (f32[10,16,128]{2,1,0:T(8,128)}, f32[10,16,128]{2,1,0:T(8,128)S(1)}, u32[]{:S(2)}, u32[]{:S(2)}) collective-permute-start(f32[10,16,128]{2,1,0:T(8,128)} %get-tuple-element.12), channel_id=1, source_target_pairs={{2,0},{3,1},{0,2},{1,3},{6,4},{7,5},{4,6},{5,7},{10,8},{11,9},{8,1... | collective-permute-start | bytes 245768 | tf_op jit(solution)/shard_map/ppermute | solution.py:379
  60.4 0.0 collective-permute-done.5.m3
  60.4 0.0 copy-start.3
  60.4 0.0 collective-permute-start.2
  61.1 0.2 collective-permute-done.v1
  61.3 0.0 copy-start.4
  61.3 1.7 %collective-permute-done.1.v2 = f32[10,16,128]{2,1,0:T(8,128)S(1)} collective-permute-done((f32[10,16,128]{2,1,0:T(8,128)}, f32[10,16,128]{2,1,0:T(8,128)S(1)}, u32[]{:S(2)}, u32[]{:S(2)}) %collective-permute-start.1) | collective-permute-done | bytes 81952 | tf_op jit(solution)/shard_map/ppermute | solution.py:379
  63.0 0.0 copy-start.5
  63.0 2.5 %collective-permute-done.2.v3 = f32[10,16,128]{2,1,0:T(8,128)S(1)} collective-permute-done((f32[10,16,128]{2,1,0:T(8,128)}, f32[10,16,128]{2,1,0:T(8,128)S(1)}, u32[]{:S(2)}, u32[]{:S(2)}) %collective-permute-start.2) | collective-permute-done | bytes 81952 | tf_op jit(solution)/shard_map/ppermute | solution.py:379
  65.4 0.0 copy-start.6
  65.5 0.0 collective-permute-done.3.m1
  65.5 0.0 copy-start.1
  65.5 0.0 collective-permute-done.4.m2
  65.5 0.0 copy-start.2
  65.5 0.0 copy-done.3
  65.5 0.0 copy-done.4
  65.5 0.0 copy-done.5
  65.5 0.6 copy-done.6
  66.1 0.2 copy-done.1
  66.3 0.2 copy-done.2
  66.5 4.6 %shard_map.143 = (f32[16,5,8,128]{3,2,1,0:T(8,128)}, f32[128,128]{1,0:T(8,128)}) custom-call(s32[1]{0:T(128)} %bitcast.z_ref, s32[1]{0:T(128)} %bitcast.35.count, f32[10,16,128]{2,1,0:T(8,128)} %copy-done.4, f32[10,16,128]{2,1,0:T(8,128)} %copy-done.5, f32[10,16,128]{2,1,0:T(8,128)} %copy-done.6, f32[75,16,128]{2,1,0:T(8,128)} %copy-done.1, ...), custom_call_target="tpu_custom_call" | custom-call | tf_op jit(solution)/shard_map/pallas_call | solution.py:380
  71.1 15.2 %all_to_all.20 = f32[128,1,128]{2,1,0:T(1,128)S(1)} all-to-all(f32[128,1,128]{2,1,0:T(1,128)} %bitcast.53), channel_id=1, replica_groups=mesh['stream'=32,'span'=4] {'stream','span'}, dimensions={0} | all-to-all | bytes 131072 | tf_op jit(solution)/shard_map/all_to_all | solution.py:387
  86.3 0.2 reduce_sum.9
  86.5 0.7 reshape.65
Async XLA Ops:
  9.8 55.7 %collective-permute-start.3 = (f32[75,16,128]{2,1,0:T(8,128)}, f32[75,16,128]{2,1,0:T(8,128)S(1)}, u32[]{:S(2)}, u32[]{:S(2)}) collective-permute-start(f32[75,16,128]{2,1,0:T(8,128)} %get-tuple-element.13), channel_id=1, source_target_pairs={{1,0},{2,1},{3,2},{5,4},{6,5},{7,6},{9,8},{10,9},{11,10},{13,12},{... | collective-permute-start | bytes 1843208 | tf_op jit(solution)/shard_map/ppermute | solution.py:364
  11.0 54.4 %collective-permute-start.4 = (f32[75,16,128]{2,1,0:T(8,128)}, f32[75,16,128]{2,1,0:T(8,128)S(1)}, u32[]{:S(2)}, u32[]{:S(2)}) collective-permute-start(f32[75,16,128]{2,1,0:T(8,128)} %get-tuple-element.13), channel_id=1, source_target_pairs={{2,0},{3,1},{1,3},{6,4},{7,5},{5,7},{10,8},{11,9},{9,11},{14,12},{... | collective-permute-start | bytes 1843208 | tf_op jit(solution)/shard_map/ppermute | solution.py:365
  12.3 18.9 %all-to-all-start = ((f32[32,24,128]{2,1,0:T(8,128)}), f32[32,24,128]{2,1,0:T(8,128)S(1)}, u32[]{:S(2)}, u32[]{:S(2)}) async-start(f32[32,24,128]{2,1,0:T(8,128)} %bitcast.50), calls=%async_computation | async-start | bytes 786432 | tf_op jit(solution)/shard_map/all_to_all | solution.py:367
  21.0 39.5 %collective-permute-start.5 = (f32[25,16,128]{2,1,0:T(8,128)}, f32[25,16,128]{2,1,0:T(8,128)S(1)}, u32[]{:S(2)}, u32[]{:S(2)}) collective-permute-start(f32[25,16,128]{2,1,0:T(8,128)} %get-tuple-element.14), channel_id=1, source_target_pairs={{3,0},{1,2},{2,3},{7,4},{5,6},{6,7},{11,8},{9,10},{10,11},{15,12},... | collective-permute-start | bytes 614408 | tf_op jit(solution)/shard_map/ppermute | solution.py:366
  31.3 0.8 copy-start
  52.3 9.0 %collective-permute-start = (f32[10,16,128]{2,1,0:T(8,128)}, f32[10,16,128]{2,1,0:T(8,128)S(1)}, u32[]{:S(2)}, u32[]{:S(2)}) collective-permute-start(f32[10,16,128]{2,1,0:T(8,128)} %get-tuple-element.12), channel_id=1, source_target_pairs={{1,0},{2,1},{3,2},{0,3},{5,4},{6,5},{7,6},{4,7},{9,8},{10,9},{11,1... | collective-permute-start | bytes 245768 | tf_op jit(solution)/shard_map/ppermute | solution.py:379
  58.0 5.0 %collective-permute-start.1 = (f32[10,16,128]{2,1,0:T(8,128)}, f32[10,16,128]{2,1,0:T(8,128)S(1)}, u32[]{:S(2)}, u32[]{:S(2)}) collective-permute-start(f32[10,16,128]{2,1,0:T(8,128)} %get-tuple-element.12), channel_id=1, source_target_pairs={{2,0},{3,1},{0,2},{1,3},{6,4},{7,5},{4,6},{5,7},{10,8},{11,9},{8,1... | collective-permute-start | bytes 245768 | tf_op jit(solution)/shard_map/ppermute | solution.py:379
  60.4 5.1 %copy-start.3 = (f32[25,16,128]{2,1,0:T(8,128)}, f32[25,16,128]{2,1,0:T(8,128)S(1)}, u32[]{:S(2)}) copy-start(f32[25,16,128]{2,1,0:T(8,128)S(1)} %collective-permute-done.5.m3) | copy-start | bytes 614404
  60.4 5.0 %collective-permute-start.2 = (f32[10,16,128]{2,1,0:T(8,128)}, f32[10,16,128]{2,1,0:T(8,128)S(1)}, u32[]{:S(2)}, u32[]{:S(2)}) collective-permute-start(f32[10,16,128]{2,1,0:T(8,128)} %get-tuple-element.12), channel_id=1, source_target_pairs={{3,0},{0,1},{1,2},{2,3},{7,4},{4,5},{5,6},{6,7},{11,8},{8,9},{9,10... | collective-permute-start | bytes 245768 | tf_op jit(solution)/shard_map/ppermute | solution.py:379
  61.3 4.2 %copy-start.4 = (f32[10,16,128]{2,1,0:T(8,128)}, f32[10,16,128]{2,1,0:T(8,128)S(1)}, u32[]{:S(2)}) copy-start(f32[10,16,128]{2,1,0:T(8,128)S(1)} %collective-permute-done.v1) | copy-start | bytes 245764
  63.0 2.5 %copy-start.5 = (f32[10,16,128]{2,1,0:T(8,128)}, f32[10,16,128]{2,1,0:T(8,128)S(1)}, u32[]{:S(2)}) copy-start(f32[10,16,128]{2,1,0:T(8,128)S(1)} %collective-permute-done.1.v2) | copy-start | bytes 245764
  65.4 0.6 copy-start.6
  65.5 0.8 copy-start.1
  65.5 1.1 %copy-start.2 = (f32[75,16,128]{2,1,0:T(8,128)}, f32[75,16,128]{2,1,0:T(8,128)S(1)}, u32[]{:S(2)}) copy-start(f32[75,16,128]{2,1,0:T(8,128)S(1)} %collective-permute-done.4.m2) | copy-start | bytes 1843204

commit v2 on v1

--- a/solution.py
+++ b/solution.py
@@ -8,7 +8,6 @@
 SX, SY, NN = 16, 8, 128
 XS = 32
 ROWS = 24
-VMEM = 56 * 1024 * 1024
 
 
 def act(m, v):
@@ -38,19 +37,31 @@
     return lax.shift_right_logical(lax.broadcasted_iota(jnp.int32, shape, 1), 5)
 
 
-def maps_kernel(z_ref, rhs, dx, lx, ux, ly, uy, msg, driven, mats, matsel, fs, gs, fy):
-    def tiles(ref, i, n=25):
-        return [ref[i, k] for k in range(n)]
-
-    def put(ref, i, vals):
-        for k, v in enumerate(vals):
-            ref[i, k] = v
-
-    d = act(tiles(dx, 0), tiles(rhs, 0, 5))
-    put(driven, 0, d)
-    put(gs, 0, d)
-    f = tiles(lx, 0)
-    put(fs, 0, f)
+def tiles(ref, i, n=25):
+    return [ref[i, k] for k in range(n)]
+
+
+def put(ref, i, vals):
+    for k, v in enumerate(vals):
+        ref[i, k] = v
+
+
+def copies(pairs, sems):
+    out = [pltpu.make_async_copy(src, dst, sems.at[k]) for k, (src, dst) in enumerate(pairs)]
+    for c in out:
+        c.start()
+    return out
+
+
+STEP = 4
+
+
+def stream_kernel(rhs_h, dx_h, lx_h, ux_h, msg, driven_h, lx, ux, rhs, dx, fs, gs, driven, sems):
+    chunks = [pl.ds(k * STEP, STEP) for k in range(SX // STEP)]
+    pairs = []
+    for c in chunks:
+        pairs += [(lx_h.at[c], lx.at[c]), (dx_h.at[c], dx.at[c]), (rhs_h.at[c], rhs.at[c])]
+    flight = copies(pairs + [(ux_h, ux)], sems)
 
     def fore(i, carry):
         g, f = carry
@@ -63,7 +74,19 @@
         put(fs, i, f)
         return g, f
 
-    g, f = lax.fori_loop(1, SX, fore, (d, f))
+    for k in range(len(chunks)):
+        for c in flight[3 * k : 3 * k + 3]:
+            c.wait()
+        if k == 0:
+            g = act(tiles(dx, 0), tiles(rhs, 0, 5))
+            put(driven, 0, g)
+            put(gs, 0, g)
+            f = tiles(lx, 0)
+            put(fs, 0, f)
+        g, f = lax.fori_loop(max(1, STEP * k), STEP * k + STEP, fore, (g, f))
+    kept = pltpu.make_async_copy(driven, driven_h, sems.at[13])
+    kept.start()
+    flight[-1].wait()
 
     def back(k, carry):
         i = SX - 2 - k
@@ -94,42 +117,50 @@
     for r in range(22, ROWS):
         for nq in range(4):
             msg[pl.ds(nq * 8 * ROWS + r, 8, ROWS), :] = zero
-
-    last = z_ref[0] == 3
-    for h in range(2):
-        def turned(ref, y):
-            return [ref[pl.ds(h * 1600 + k * 8 + y, 8, 200), :] for k in range(25)]
-
-        f = turned(ly, 0)
-        put(fy, 0, f)
+    kept.wait()
+
+
+def span_kernel(ly, uy_h, after, mats, fy, uy, sems):
+    del after
+    (flight,) = copies([(uy_h, uy)], sems)
+    def turned(ref, h, y):
+        return [ref[pl.ds(h * 1600 + k * 8 + y, 8, 200), :] for k in range(25)]
+
+    for h in range(2):
+        f = turned(ly, h, 0)
+        put(fy, 8 * h, f)
 
         def fore_y(y, f):
-            f = act_cols(turned(ly, y), f)
-            put(fy, y, f)
+            f = act_cols(turned(ly, h, y), f)
+            put(fy, 8 * h + y, f)
             return f
 
         f = lax.fori_loop(1, SY, fore_y, f)
         for k in range(25):
             mats[k, pl.ds(h * 8, 8), :] = f[k]
-
+    flight.wait()
+    for h in range(2):
         def back_y(k, c):
             y = SY - 2 - k
-            return add(tiles(fy, y), act_cols(turned(uy, y), c))
-
-        c = lax.fori_loop(0, SY - 1, back_y, f)
+            return add(tiles(fy, 8 * h + y), act_cols(turned(uy, h, y), c))
+
+        c = lax.fori_loop(0, SY - 1, back_y, tiles(fy, 8 * h + SY - 1))
         for k in range(25):
             mats[50 + k, pl.ds(h * 8, 8), :] = -c[k]
-            matsel[k, pl.ds(h * 8, 8), :] = jnp.where(last, -c[k], mats[k, pl.ds(h * 8, 8), :])
 
         def back_map_y(k, bm):
-            return act_cols(turned(uy, SY - 2 - k), bm)
-
-        bm = lax.fori_loop(0, SY - 1, back_map_y, turned(uy, SY - 1))
+            return act_cols(turned(uy, h, SY - 2 - k), bm)
+
+        bm = lax.fori_loop(0, SY - 1, back_map_y, turned(uy, h, SY - 1))
         for k in range(25):
             mats[25 + k, pl.ds(h * 8, 8), :] = bm[k]
 
 
-def solve_kernel(got, out, un, fin, sin):
+def solve_kernel(z_ref, got, mats, out, matsel, un, fin, sin, sems):
+    at = jnp.where(z_ref[0] == 3, 50, 0)
+    chosen = pltpu.make_async_copy(mats.at[pl.ds(at, 25)], matsel, sems.at[0])
+    chosen.start()
+
     un[0] = got[...]
     for q in range(1, 4):
         for p in range(XS):
@@ -145,7 +176,7 @@
             fin[p, j : j + 1, :] = f[j]
         return add(act([val(p, k) for k in range(25)], f), [val(p, 25 + j) for j in range(5)])
 
-    lax.fori_loop(0, XS, fore, zero)
+    lax.fori_loop(0, XS, fore, zero, unroll=8)
 
     def back(k, s):
         p = XS - 1 - k
@@ -155,13 +186,35 @@
         known = add(act([val(p, 60 + k) for k in range(25)], f), [val(p, 55 + j) for j in range(5)])
         return add(known, act([val(p, 30 + k) for k in range(25)], s))
 
-    lax.fori_loop(0, XS, back, zero)
+    lax.fori_loop(0, XS, back, zero, unroll=8)
     quarter = lanes_quarter((8, NN))
     for p in range(XS):
         out[p] = jnp.where(quarter == 0, fin[p], pltpu.roll(sin[p], 32, 1))
-
-
-def replay_kernel(got, driven, lx, ux, dy, ly, uy, dturn, vec, fs, sd, gt):
+    chosen.wait()
+
+
+def replay_kernel(count, got, cell, owner, weight, ly, driven_h, lx_h, ux_h, dy_h, uy_h, dturn, vec, target,
+                  spread, uy, driven, lx, ux, dy, fs, sd, gt, sems):
+    chunks = [pl.ds(k * STEP, STEP) for k in range(SX // STEP)]
+    pairs = []
+    for c in chunks:
+        pairs += [(lx_h.at[c], lx.at[c]), (driven_h.at[c], driven.at[c])]
+    for c in chunks[::-1]:
+        pairs += [(ux_h.at[c], ux.at[c]), (dy_h.at[c], dy.at[c])]
+    flight = copies(pairs + [(uy_h, uy)], sems)
+
+    row = lax.broadcasted_iota(jnp.int32, (128, 128), 0)
+    lane = lax.broadcasted_iota(jnp.int32, (128, 128), 1)
+    here = cell[...] == row
+    used = jnp.logical_and(here, lane < count[0])
+    w = jnp.sum(jnp.where(used, weight[...], 0.0), axis=1, keepdims=True)
+    who = jnp.sum(jnp.where(here, owner[...].astype(jnp.float32), 0.0), axis=1, keepdims=True)
+    who = who.astype(jnp.int32)
+    target[...] = (lax.shift_right_logical(who, 4) == lane).astype(jnp.float32).T
+    mine = jnp.logical_and(lane < 96, (lane & 15) == (who & 15))
+    spread[...] = jnp.where(mine, w, 0.0)
+
+
     quarter = lanes_quarter((SY, NN))
 
     def entering(j, at):
@@ -173,16 +226,17 @@
             out = part if out is None else jnp.where(quarter == nq, part, out)
         return out
 
-    def tiles(ref, i, n=25):
-        return [ref[i, k] for k in range(n)]
-
     def fore(i, f):
         f = sub(tiles(driven, i, 5), act(tiles(lx, i), f))
         for a in range(5):
             fs[i, a] = f[a]
         return f
 
-    lax.fori_loop(0, SX, fore, [entering(j, 0) for j in range(5)])
+    f = [entering(j, 0) for j in range(5)]
+    for k in range(len(chunks)):
+        for c in flight[2 * k : 2 * k + 2]:
+            c.wait()
+        f = lax.fori_loop(STEP * k, STEP * k + STEP, fore, f)
 
     def back(k, s):
         i = SX - 1 - k
@@ -192,8 +246,12 @@
             sd[pl.ds(pl.multiple_of((i * 5 + a) * 8, 8), 8), :] = d[a]
         return s
 
-    lax.fori_loop(0, SX, back, [entering(j, 1) for j in range(5)])
-
+    s = [entering(j, 1) for j in range(5)]
+    for k in range(len(chunks)):
+        for c in flight[2 * len(chunks) + 2 * k : 2 * len(chunks) + 2 * k + 2]:
+            c.wait()
+        s = lax.fori_loop(STEP * k, STEP * k + STEP, back, s)
+    flight[-1].wait()
     for h in range(2):
         def turned(ref, y):
             return [ref[pl.ds(h * 1600 + k * 8 + y, 8, 200), :] for k in range(25)]
@@ -215,8 +273,8 @@
             vec[5 + a, pl.ds(h * 8, 8), :] = b[a]
 
 
-def finish_kernel(z_ref, count, v1, v2, v3, m1, m2, m3, dturn, ly, uy, adjoint, metric, cell, owner,
-                  weight, new, part, fin, sin, ft, ut, pk):
+def finish_kernel(z_ref, v1, v2, v3, m1, m2, m3, dturn, ly, uy, adjoint, metric, target,
+                  spread, new, part, fin, sin, ft, ut, pk):
     z = z_ref[0]
     halves = [pl.ds(0, 8), pl.ds(8, 8)]
     zero = jnp.zeros((8, NN), jnp.float32)
@@ -312,33 +370,43 @@
                 t = t + metric[x, 5 * k + a].astype(jnp.float32) * fresh[a]
             pk[k, pl.ds(x * 8, 8), :] = t
 
-    row = lax.broadcasted_iota(jnp.int32, (128, 128), 0)
-    lane = lax.broadcasted_iota(jnp.int32, (128, 128), 1)
-    here = cell[...] == row
-    used = jnp.logical_and(here, lane < count[0])
-    w = jnp.sum(jnp.where(used, weight[...], 0.0), axis=1, keepdims=True)
-    who = jnp.sum(jnp.where(here, owner[...].astype(jnp.float32), 0.0), axis=1, keepdims=True)
-    who = who.astype(jnp.int32)
-    surface = [jnp.sum(pk[k], axis=1, keepdims=True) * w for k in range(3)]
-    which = lax.shift_right_logical(lane, 4)
-    picked = jnp.where(which == 0, surface[0], jnp.where(which == 1, surface[1], surface[2]))
-    picked = jnp.where(jnp.logical_and(lane < 48, (lane & 15) == (who & 15)), picked, 0.0)
-    target = (lax.shift_right_logical(who, 4) == lane).astype(jnp.float32)
-    part[...] = lax.dot_general(target, picked, (((0,), (0,)), ((), ())),
-                                precision=lax.Precision.HIGHEST, preferred_element_type=jnp.float32)
-
-
-def call(kernel, outs, scratch, smem=0, n_in=0):
-    f32 = jnp.float32
+    group = lax.shift_right_logical(lax.broadcasted_iota(jnp.int32, (128, 128), 1), 4)
+    value = jnp.zeros((128, 128), jnp.float32)
+    for k in range(3):
+        value = jnp.where(group % 3 == k, jnp.sum(pk[k], axis=1, keepdims=True), value)
+    value = value * spread[...]
+    high = value.astype(jnp.bfloat16).astype(jnp.float32)
+    value = jnp.where(group < 3, high, value - high).astype(jnp.bfloat16)
+    part[...] = jnp.dot(target[...].astype(jnp.bfloat16), value, preferred_element_type=jnp.float32)
+
+
+def sum_kernel(parts, out):
+    total = jnp.sum(parts[...], axis=0, keepdims=True)
+    total = total + pltpu.roll(total, 80, 1)
+    for k in range(3):
+        part = total if k == 0 else pltpu.roll(total, 128 - 16 * k, 1)
+        out[k : k + 1, :] = part[:, :16]
+
+
+def call(kernel, outs, scratch, smem=0, vmem=0, hbm=0, sems=(), cost=0, limit=16):
+    spec = pl.BlockSpec
+    out_specs = [spec(memory_space=pltpu.HBM if isinstance(s, list) else pltpu.VMEM) for s in outs]
     return pl.pallas_call(
         kernel,
-        out_shape=[jax.ShapeDtypeStruct(s, f32) for s in outs],
-        in_specs=[pl.BlockSpec(memory_space=pltpu.SMEM)] * smem
-        + [pl.BlockSpec(memory_space=pltpu.VMEM)] * (n_in - smem),
-        out_specs=[pl.BlockSpec(memory_space=pltpu.VMEM)] * len(outs),
-        scratch_shapes=[pltpu.VMEM(s, f32) for s in scratch],
-        compiler_params=pltpu.CompilerParams(vmem_limit_bytes=VMEM),
+        out_shape=[pltpu.HBM(tuple(s), jnp.float32) if isinstance(s, list) else jax.ShapeDtypeStruct(s, jnp.float32)
+                   for s in outs],
+        in_specs=[spec(memory_space=pltpu.SMEM)] * smem + [spec(memory_space=pltpu.VMEM)] * vmem
+        + [spec(memory_space=pltpu.HBM)] * hbm,
+        out_specs=out_specs,
+        scratch_shapes=[pltpu.VMEM(s, jnp.float32) for s in scratch]
+        + [pltpu.SemaphoreType.DMA((n,)) for n in sems],
+        compiler_params=pltpu.CompilerParams(vmem_limit_bytes=limit * 1024 * 1024),
+        cost_estimate=pl.CostEstimate(flops=cost, bytes_accessed=cost, transcendentals=0),
     )
+
+
+def in_hbm(x):
+    return pltpu.with_memory_space_constraint(x, pltpu.HBM)
 
 
 def shards(rhs, adjoint, diag_x, lower_x, upper_x, diag_y, lower_y, upper_y, metric, node_cell,
@@ -354,38 +422,40 @@
     metric = blocks(metric)
     z = lax.axis_index("span").astype(jnp.int32).reshape(1)
 
-    tile = (SX, 25, SY, NN)
-    msg, driven, mats, matsel = call(
-        maps_kernel,
-        [(XS * ROWS, NN), (SX, 5, SY, NN), (75, SX, NN), (25, SX, NN)],
-        [tile, (SX, 5, SY, NN), (SY, 25, 8, NN)],
-        smem=1, n_in=7,
-    )(z, rhs, dx, lx, ux, ly, uy)
+    tile, cells, msg_shape = (SX, 25, SY, NN), (SX, 5, SY, NN), (XS * ROWS, NN)
+    msg, driven = call(
+        stream_kernel,
+        [msg_shape, list(cells)],
+        [tile, tile, cells, tile, tile, cells, cells], hbm=4, sems=(14,), cost=10_000_000,
+    )(in_hbm(rhs), in_hbm(dx), in_hbm(lx), in_hbm(ux))
+    got = lax.all_to_all(msg.reshape(XS, ROWS, NN), "stream", 0, 0, tiled=True)
+    (mats,) = call(
+        span_kernel, [(75, SX, NN)], [(2 * SY, 25, 8, NN), uy.shape], vmem=1, hbm=2, sems=(1,), cost=10_000_000,
+    )(ly, in_hbm(uy), in_hbm(driven))
     m1 = lax.ppermute(mats, "span", [(1, 0), (2, 1), (3, 2)])
     m2 = lax.ppermute(mats, "span", [(2, 0), (3, 1), (1, 3)])
+    back, matsel = call(
+        solve_kernel, [(XS, 8, NN), (25, SX, NN)],
+        [(4, XS, ROWS, NN), (XS, 8, NN), (XS, 8, NN)], smem=1, vmem=1, hbm=1, sems=(1,), cost=10_000_000,
+    )(z, got, in_hbm(mats))
     m3 = lax.ppermute(matsel, "span", [(3, 0), (1, 2), (2, 3)])
-    got = lax.all_to_all(msg.reshape(XS, ROWS, NN), "stream", 0, 0, tiled=True)
-    (back,) = call(
-        solve_kernel, [(XS, 8, NN)],
-        [(4, XS, ROWS, NN), (XS, 8, NN), (XS, 8, NN)], n_in=1,
-    )(got)
     back = lax.all_to_all(back, "stream", 0, 0, tiled=True)
-    dturn, vec = call(
+    dturn, vec, target, spread, uy = call(
         replay_kernel,
-        [(SY, 5, SX, NN), (10, SX, NN)],
-        [(SX, 5, SY, NN), (SX * 5 * SY, NN), (SY, 5, 8, NN)],
-        n_in=7,
-    )(back.reshape(XS * 8, NN), driven, lx, ux, dy, ly, uy)
+        [(SY, 5, SX, NN), (10, SX, NN), (128, 128), (128, 128), uy.shape],
+        [cells, tile, tile, tile, cells, (SX * 5 * SY, NN), (SY, 5, 8, NN)],
+        smem=1, vmem=5, hbm=5, sems=(17,), cost=30_000_000,
+    )(node_count.reshape(1), back.reshape(XS * 8, NN), node_cell.reshape(1, -1), node_owner.reshape(1, -1),
+      node_weight.reshape(1, -1), ly, in_hbm(driven), in_hbm(lx), in_hbm(ux), in_hbm(dy), in_hbm(uy))
     v = [lax.ppermute(vec, "span", [((i + s) % 4, i) for i in range(4)]) for s in (1, 2, 3)]
     new, part = call(
         finish_kernel,
-        [(SX, 5, SY, NN), (128, NN)],
+        [cells, (128, NN)],
         [(5, SX, NN), (5, SX, NN), (SY, 5, SX, NN), (SY * 5 * SX, NN), (3, 128, NN)],
-        smem=2, n_in=16,
-    )(z, node_count.reshape(1), *v, m1, m2, m3, dturn, ly, uy, adjoint, metric,
-      node_cell.reshape(1, -1), node_owner.reshape(1, -1), node_weight.reshape(1, -1))
+        smem=1, vmem=13, cost=1_000_000,
+    )(z, *v, m1, m2, m3, dturn, ly, uy, adjoint, metric, target, spread)
     parts = lax.all_to_all(part, ("stream", "span"), 0, 0, tiled=True)
-    control = jnp.sum(parts, axis=0)[:48].reshape(3, 16)
+    (control,) = call(sum_kernel, [(3, 16)], [], vmem=1)(parts)
     return new.transpose(0, 2, 1, 3), control
 
 

time: 87.6 us -> 76.4 us (0.87)
  blocking collectives: 27.1 us -> 17 us
  starting transfers between devices: 20.5 us -> 26.3 us
  Pallas kernels: 22.2 us -> 17.2 us
  local copies, waits for them, and re-layouts: 2.45 us -> 0.04 us
    all_to_all x1 -> x0, blocking collectives: 11.9 us -> none  [shards(): back = lax.all_to_all(back, 'stream', 0, 0, tiled=True)]
    all_to_all x0 -> x1, waiting for transfers between devices: none -> 6.97 us  [shards(): back = lax.all_to_all(back, 'stream', 0, 0, tiled=True)]
    pallas_call x4 -> x6, Pallas kernels: 22.2 us -> 17.2 us  [the longest x1 5.17 us: shards(): call(stream_kernel, [msg_shape, list(cells)], [tile, tile, cells, tile, t...]
    all_to_all x1, waiting for transfers between devices: 9 us -> 4.78 us  [shards(): got = lax.all_to_all(msg.reshape(XS, ROWS, NN), 'stream', 0, 0, tiled=True)]
    all_to_all x0 -> x1, starting transfers between devices: none -> 3.64 us  [shards(): back = lax.all_to_all(back, 'stream', 0, 0, tiled=True)]
    ppermute x3, waiting for transfers between devices: 4.38 us -> 2.31 us  [shards(): lax.ppermute(vec, 'span', [((i + s) % 4, i) for i in range(4)])]
    ppermute x3, starting transfers between devices: 8.07 us -> 10.1 us  [shards(): lax.ppermute(vec, 'span', [((i + s) % 4, i) for i in range(4)])]
    all_to_all x1, blocking collectives: 15.2 us -> 17 us  [shards(): parts = lax.all_to_all(part, ('stream', 'span'), 0, 0, tiled=True)]
  transfers between devices with their start and end apart: 7 -> 8, of which waited for: 4 -> 3; matrix products, arithmetic and copies ran while one was open for 0% -> 0% of each run, Pallas kernels for 10% -> 11%
where the time goes in v2:
time: 76.4 us; the launch traced here: 76 us
  starting transfers between devices  26.3 us (34%)
  Pallas kernels  17.2 us (23%)
  blocking collectives  17 us (22%)
  waiting for transfers between devices  14.1 us (18%)
  between operations  1.45 us (2%)
    all_to_all x1, blocking collectives, shards(): parts = lax.all_to_all(part, ('stream', 'span'), 0, 0, tiled=True)  17 us
    ppermute x3, starting transfers between devices, shards(): lax.ppermute(vec, 'span', [((i + s) % 4, i) for i in range(4)])  10.1 us
    all_to_all x1, starting transfers between devices, shards(): got = lax.all_to_all(msg.reshape(XS, ROWS, NN), 'stream', 0, 0, tiled=True)  8.6 us
    all_to_all x1, waiting for transfers between devices, shards(): back = lax.all_to_all(back, 'stream', 0, 0, tiled=True)  6.97 us
    pallas_call x1, Pallas kernels, shards(): call(stream_kernel, [msg_shape, list(cells)], [tile, tile, cells, tile, t...  5.17 us
    all_to_all x1, waiting for transfers between devices, shards(): got = lax.all_to_all(msg.reshape(XS, ROWS, NN), 'stream', 0, 0, tiled=True)  4.78 us
    pallas_call x1, Pallas kernels, shards(): call(replay_kernel, [(SY, 5, SX, NN), (10, SX, NN), (128, 128), (128, 128...  3.83 us
    all_to_all x1, starting transfers between devices, shards(): back = lax.all_to_all(back, 'stream', 0, 0, tiled=True)  3.64 us
  transfers between devices with their start and end apart: 8, of which 3 were waited for; matrix products, arithmetic and copies ran while one was open for 0% of the time, Pallas kernels for 11%

profile of v2, /device:TPU:1, one launch (start us, length us, event | category | flops | bytes accessed | tf_op | source)
XLA Modules:
  0.0 76.0 jit_solution(5118901879301229368)
XLA Ops:
  0.6 0.0 copy-start
  0.6 5.2 %shard_map.140 = (f32[768,128]{1,0:T(8,128)}, f32[16,5,8,128]{3,2,1,0:T(8,128)}) custom-call(f32[16,5,8,128]{3,2,1,0:T(8,128)} %bitcast.55, f32[16,25,8,128]{3,2,1,0:T(8,128)} %bitcast.53, f32[16,25,8,128]{3,2,1,0:T(8,128)} %bitcast.47, f32[16,25,8,128]{3,2,1,0:T(8,128)} %bitcast.49), custom_call_target="tpu_custom_call" | custom-call | flops 10000000 | bytes 10000000 | tf_op jit(solution)/shard_map/pallas_call | solution.py:426
  5.8 8.6 %all-to-all-start = ((f32[32,24,128]{2,1,0:T(8,128)}), f32[32,24,128]{2,1,0:T(8,128)S(1)}, u32[]{:S(2)}, u32[]{:S(2)}) async-start(f32[32,24,128]{2,1,0:T(8,128)} %bitcast.9), calls=%async_computation | async-start | bytes 786432 | tf_op jit(solution)/shard_map/all_to_all | solution.py:431
  14.4 0.0 copy-done
  14.4 0.0 copy-start.4
  14.4 0.0 copy-start.5
  14.5 0.0 copy-start.6
  14.5 2.9 %shard_map.141.mats = f32[75,16,128]{2,1,0:T(8,128)S(1)} custom-call(f32[3200,128]{1,0:T(8,128)S(1)} %bitcast.36, f32[3200,128]{1,0:T(8,128)} %bitcast.51, f32[16,5,8,128]{3,2,1,0:T(8,128)} %get-tuple-element.14.after.driven_h), custom_call_target="tpu_custom_call" | custom-call | flops 10000000 | bytes 10000000 | tf_op jit(solution)/shard_map/pallas_call | solution.py:432
  17.3 0.0 copy-start.1
  17.3 1.3 %collective-permute-start.4 = (f32[75,16,128]{2,1,0:T(8,128)S(1)}, f32[75,16,128]{2,1,0:T(8,128)S(1)}, u32[]{:S(2)}, u32[]{:S(2)}) collective-permute-start(f32[75,16,128]{2,1,0:T(8,128)S(1)} %shard_map.141.mats), channel_id=1, source_target_pairs={{2,0},{3,1},{1,3},{6,4},{7,5},{5,7},{10,8},{11,9},{9,11},{14,12},{... | collective-permute-start | bytes 1843208 | tf_op jit(solution)/shard_map/ppermute | solution.py:436
  18.6 1.3 %collective-permute-start.3 = (f32[75,16,128]{2,1,0:T(8,128)S(1)}, f32[75,16,128]{2,1,0:T(8,128)}, u32[]{:S(2)}, u32[]{:S(2)}) collective-permute-start(f32[75,16,128]{2,1,0:T(8,128)S(1)} %shard_map.141.mats), channel_id=1, source_target_pairs={{1,0},{2,1},{3,2},{5,4},{6,5},{7,6},{9,8},{10,9},{11,10},{13,12},{... | collective-permute-start | bytes 1843208 | tf_op jit(solution)/shard_map/ppermute | solution.py:435
  20.0 4.8 %all-to-all-done.got = f32[32,24,128]{2,1,0:T(8,128)S(1)} async-done(((f32[32,24,128]{2,1,0:T(8,128)}), f32[32,24,128]{2,1,0:T(8,128)S(1)}, u32[]{:S(2)}, u32[]{:S(2)}) %all-to-all-start) | async-done | bytes 393248 | tf_op jit(solution)/shard_map/all_to_all | solution.py:431
  24.7 0.0 copy-done.1
  24.7 1.8 %shard_map.142 = (f32[32,8,128]{2,1,0:T(8,128)}, f32[25,16,128]{2,1,0:T(8,128)S(1)}) custom-call(s32[1]{0:T(128)} %bitcast.z_ref, f32[32,24,128]{2,1,0:T(8,128)S(1)} %all-to-all-done.got, f32[75,16,128]{2,1,0:T(8,128)} %copy-done.1), custom_call_target="tpu_custom_call" | custom-call | flops 10000000 | bytes 10000000 | tf_op jit(solution)/shard_map/pallas_call | solution.py:437
  26.6 1.3 %collective-permute-start.5 = (f32[25,16,128]{2,1,0:T(8,128)S(1)}, f32[25,16,128]{2,1,0:T(8,128)S(1)}, u32[]{:S(2)}, u32[]{:S(2)}) collective-permute-start(f32[25,16,128]{2,1,0:T(8,128)S(1)} %get-tuple-element.17), channel_id=1, source_target_pairs={{3,0},{1,2},{2,3},{7,4},{5,6},{6,7},{11,8},{9,10},{10,11},{15,12},... | collective-permute-start | bytes 614408 | tf_op jit(solution)/shard_map/ppermute | solution.py:441
  27.9 3.6 %all-to-all-start.1 = ((f32[32,8,128]{2,1,0:T(8,128)}), f32[32,8,128]{2,1,0:T(8,128)S(1)}, u32[]{:S(2)}, u32[]{:S(2)}) async-start(f32[32,8,128]{2,1,0:T(8,128)} %get-tuple-element.15), calls=%async_computation.1 | async-start | bytes 262144 | tf_op jit(solution)/shard_map/all_to_all | solution.py:442
  32.2 7.0 %all-to-all-done.1 = f32[32,8,128]{2,1,0:T(8,128)S(1)} async-done(((f32[32,8,128]{2,1,0:T(8,128)}), f32[32,8,128]{2,1,0:T(8,128)S(1)}, u32[]{:S(2)}, u32[]{:S(2)}) %all-to-all-start.1) | async-done | bytes 131104 | tf_op jit(solution)/shard_map/all_to_all | solution.py:442
  39.1 0.0 copy-done.4
  39.2 0.0 copy-done.5
  39.2 0.0 copy-done.6
  39.2 0.0 copy-start.2
  39.2 0.0 copy-start.3
  39.2 3.8 %shard_map.143 = (f32[8,5,16,128]{3,2,1,0:T(8,128)S(1)}, f32[10,16,128]{2,1,0:T(8,128)S(1)}, f32[128,128]{1,0:T(8,128)S(1)}, f32[128,128]{1,0:T(8,128)S(1)}, f32[3200,128]{1,0:T(8,128)S(1)}) custom-call(s32[1]{0:T(128)} %bitcast.35.count, f32[256,128]{1,0:T(8,128)S(1)} %bitcast.39, s32[1,128]{1,0:T(1,128)S(1)} %bitcast.44, s32[1,128]{1,0:T(1,128)S(1)} %bitcast.45, ...), custom_call_target="tpu_custom_call" | custom-call | flops 30000000 | bytes 30000000 | tf_op jit(solution)/shard_map/pallas_call | solution.py:443
  43.0 7.6 %collective-permute-start.2 = (f32[10,16,128]{2,1,0:T(8,128)S(1)}, f32[10,16,128]{2,1,0:T(8,128)S(1)}, u32[]{:S(2)}, u32[]{:S(2)}) collective-permute-start(f32[10,16,128]{2,1,0:T(8,128)S(1)} %get-tuple-element.16), channel_id=1, source_target_pairs={{3,0},{0,1},{1,2},{2,3},{7,4},{4,5},{5,6},{6,7},{11,8},{8,9},{9,10... | collective-permute-start | bytes 245768 | tf_op jit(solution)/shard_map/ppermute | solution.py:450
  50.7 0.1 collective-permute-start.1
  50.8 0.0 collective-permute-done.5.m3
  50.8 2.3 %collective-permute-start = (f32[10,16,128]{2,1,0:T(8,128)S(1)}, f32[10,16,128]{2,1,0:T(8,128)S(1)}, u32[]{:S(2)}, u32[]{:S(2)}) collective-permute-start(f32[10,16,128]{2,1,0:T(8,128)S(1)} %get-tuple-element.16), channel_id=1, source_target_pairs={{1,0},{2,1},{3,2},{0,3},{5,4},{6,5},{7,6},{4,7},{9,8},{10,9},{11,1... | collective-permute-start | bytes 245768 | tf_op jit(solution)/shard_map/ppermute | solution.py:450
  53.2 0.0 collective-permute-done.2.v3
  53.2 2.3 %collective-permute-done.1.v2 = f32[10,16,128]{2,1,0:T(8,128)S(1)} collective-permute-done((f32[10,16,128]{2,1,0:T(8,128)S(1)}, f32[10,16,128]{2,1,0:T(8,128)S(1)}, u32[]{:S(2)}, u32[]{:S(2)}) %collective-permute-start.1) | collective-permute-done | bytes 81952 | tf_op jit(solution)/shard_map/ppermute | solution.py:450
  55.5 0.0 collective-permute-done.v1
  55.5 0.0 collective-permute-done.4.m2
  55.5 0.0 collective-permute-done.3.m1
  55.5 0.0 copy-done.2
  55.5 0.0 copy-done.3
  55.5 2.8 %shard_map.144 = (f32[16,5,8,128]{3,2,1,0:T(8,128)}, f32[128,128]{1,0:T(8,128)S(1)}) custom-call(s32[1]{0:T(128)} %bitcast.z_ref, f32[10,16,128]{2,1,0:T(8,128)S(1)} %collective-permute-done.v1, f32[10,16,128]{2,1,0:T(8,128)S(1)} %collective-permute-done.1.v2, f32[10,16,128]{2,1,0:T(8,128)S(1)} %collective-permute-done.2.v3, ...), custom_call_target="tpu_custom_call" | custom-call | flops 1000000 | bytes 1000000 | tf_op jit(solution)/shard_map/pallas_call | solution.py:451
  58.3 17.0 %all_to_all.21 = f32[128,1,128]{2,1,0:T(1,128)S(1)} all-to-all(f32[128,1,128]{2,1,0:T(1,128)S(1)} %bitcast.43), channel_id=1, replica_groups=mesh['stream'=32,'span'=4] {'stream','span'}, dimensions={0} | all-to-all | bytes 131072 | tf_op jit(solution)/shard_map/all_to_all | solution.py:457
  75.3 0.7 shard_map.145
Async XLA Ops:
  0.6 13.8 %copy-start = (f32[16,8,5,5,128]{4,1,3,2,0:T(8,128)S(1)}, f32[16,8,5,5,128]{4,1,3,2,0:T(8,128)}, u32[]{:S(2)}) copy-start(f32[16,8,5,5,128]{4,1,3,2,0:T(8,128)} %param.19) | copy-start | bytes 4915204
  5.8 18.9 %all-to-all-start = ((f32[32,24,128]{2,1,0:T(8,128)}), f32[32,24,128]{2,1,0:T(8,128)S(1)}, u32[]{:S(2)}, u32[]{:S(2)}) async-start(f32[32,24,128]{2,1,0:T(8,128)} %bitcast.9), calls=%async_computation | async-start | bytes 786432 | tf_op jit(solution)/shard_map/all_to_all | solution.py:431
  14.4 24.7 %copy-start.4 = (s32[1,1,128]{2,1,0:T(1,128)S(1)}, s32[1,1,128]{2,1,0:T(1,128)}, u32[]{:S(2)}) copy-start(s32[1,1,128]{2,1,0:T(1,128)} %param.22) | copy-start | bytes 1540
  14.4 24.7 %copy-start.5 = (s32[1,1,128]{2,1,0:T(1,128)S(1)}, s32[1,1,128]{2,1,0:T(1,128)}, u32[]{:S(2)}) copy-start(s32[1,1,128]{2,1,0:T(1,128)} %param.23) | copy-start | bytes 1540
  14.5 24.7 %copy-start.6 = (f32[1,1,128]{2,1,0:T(1,128)S(1)}, f32[1,1,128]{2,1,0:T(1,128)}, u32[]{:S(2)}) copy-start(f32[1,1,128]{2,1,0:T(1,128)} %param.24) | copy-start | bytes 1540
  17.3 7.4 %copy-start.1 = (f32[75,16,128]{2,1,0:T(8,128)}, f32[75,16,128]{2,1,0:T(8,128)S(1)}, u32[]{:S(2)}) copy-start(f32[75,16,128]{2,1,0:T(8,128)S(1)} %shard_map.141.mats) | copy-start | bytes 1843204
  17.3 38.1 %collective-permute-start.4 = (f32[75,16,128]{2,1,0:T(8,128)S(1)}, f32[75,16,128]{2,1,0:T(8,128)S(1)}, u32[]{:S(2)}, u32[]{:S(2)}) collective-permute-start(f32[75,16,128]{2,1,0:T(8,128)S(1)} %shard_map.141.mats), channel_id=1, source_target_pairs={{2,0},{3,1},{1,3},{6,4},{7,5},{5,7},{10,8},{11,9},{9,11},{14,12},{... | collective-permute-start | bytes 1843208 | tf_op jit(solution)/shard_map/ppermute | solution.py:436
  18.6 36.8 %collective-permute-start.3 = (f32[75,16,128]{2,1,0:T(8,128)S(1)}, f32[75,16,128]{2,1,0:T(8,128)}, u32[]{:S(2)}, u32[]{:S(2)}) collective-permute-start(f32[75,16,128]{2,1,0:T(8,128)S(1)} %shard_map.141.mats), channel_id=1, source_target_pairs={{1,0},{2,1},{3,2},{5,4},{6,5},{7,6},{9,8},{10,9},{11,10},{13,12},{... | collective-permute-start | bytes 1843208 | tf_op jit(solution)/shard_map/ppermute | solution.py:435
  26.6 24.2 %collective-permute-start.5 = (f32[25,16,128]{2,1,0:T(8,128)S(1)}, f32[25,16,128]{2,1,0:T(8,128)S(1)}, u32[]{:S(2)}, u32[]{:S(2)}) collective-permute-start(f32[25,16,128]{2,1,0:T(8,128)S(1)} %get-tuple-element.17), channel_id=1, source_target_pairs={{3,0},{1,2},{2,3},{7,4},{5,6},{6,7},{11,8},{9,10},{10,11},{15,12},... | collective-permute-start | bytes 614408 | tf_op jit(solution)/shard_map/ppermute | solution.py:441
  27.9 11.3 %all-to-all-start.1 = ((f32[32,8,128]{2,1,0:T(8,128)}), f32[32,8,128]{2,1,0:T(8,128)S(1)}, u32[]{:S(2)}, u32[]{:S(2)}) async-start(f32[32,8,128]{2,1,0:T(8,128)} %get-tuple-element.15), calls=%async_computation.1 | async-start | bytes 262144 | tf_op jit(solution)/shard_map/all_to_all | solution.py:442
  39.2 16.3 %copy-start.2 = (bf16[16,8,3,5,128]{4,1,3,2,0:T(8,128)(2,1)S(1)}, bf16[16,8,3,5,128]{4,1,3,2,0:T(8,128)(2,1)}, u32[]{:S(2)}) copy-start(bf16[16,8,3,5,128]{4,1,3,2,0:T(8,128)(2,1)} %param.21) | copy-start | bytes 1474564
  39.2 16.3 %copy-start.3 = (f32[16,8,5,128]{3,1,2,0:T(8,128)S(1)}, f32[16,8,5,128]{3,1,2,0:T(8,128)}, u32[]{:S(2)}) copy-start(f32[16,8,5,128]{3,1,2,0:T(8,128)} %param.14) | copy-start | bytes 983044
  43.0 10.1 %collective-permute-start.2 = (f32[10,16,128]{2,1,0:T(8,128)S(1)}, f32[10,16,128]{2,1,0:T(8,128)S(1)}, u32[]{:S(2)}, u32[]{:S(2)}) collective-permute-start(f32[10,16,128]{2,1,0:T(8,128)S(1)} %get-tuple-element.16), channel_id=1, source_target_pairs={{3,0},{0,1},{1,2},{2,3},{7,4},{4,5},{5,6},{6,7},{11,8},{8,9},{9,10... | collective-permute-start | bytes 245768 | tf_op jit(solution)/shard_map/ppermute | solution.py:450
  50.7 4.8 %collective-permute-start.1 = (f32[10,16,128]{2,1,0:T(8,128)S(1)}, f32[10,16,128]{2,1,0:T(8,128)S(1)}, u32[]{:S(2)}, u32[]{:S(2)}) collective-permute-start(f32[10,16,128]{2,1,0:T(8,128)S(1)} %get-tuple-element.16), channel_id=1, source_target_pairs={{2,0},{3,1},{0,2},{1,3},{6,4},{7,5},{4,6},{5,7},{10,8},{11,9},{8,1... | collective-permute-start | bytes 245768 | tf_op jit(solution)/shard_map/ppermute | solution.py:450
  50.8 4.7 %collective-permute-start = (f32[10,16,128]{2,1,0:T(8,128)S(1)}, f32[10,16,128]{2,1,0:T(8,128)S(1)}, u32[]{:S(2)}, u32[]{:S(2)}) collective-permute-start(f32[10,16,128]{2,1,0:T(8,128)S(1)} %get-tuple-element.16), channel_id=1, source_target_pairs={{1,0},{2,1},{3,2},{0,3},{5,4},{6,5},{7,6},{4,7},{9,8},{10,9},{11,1... | collective-permute-start | bytes 245768 | tf_op jit(solution)/shard_map/ppermute | solution.py:450

commit v3 on v2

--- a/solution.py
+++ b/solution.py
@@ -83,7 +83,7 @@
             put(gs, 0, g)
             f = tiles(lx, 0)
             put(fs, 0, f)
-        g, f = lax.fori_loop(max(1, STEP * k), STEP * k + STEP, fore, (g, f))
+        g, f = lax.fori_loop(max(1, STEP * k), STEP * k + STEP, fore, (g, f), unroll=True)
     kept = pltpu.make_async_copy(driven, driven_h, sems.at[13])
     kept.start()
     flight[-1].wait()
@@ -96,12 +96,12 @@
         c = add(tiles(fs, i), act_cols(u, c))
         return b, c
 
-    b, c = lax.fori_loop(0, SX - 1, back, (g, f))
+    b, c = lax.fori_loop(0, SX - 1, back, (g, f), unroll=3)
 
     def back_map(k, bm):
         return act_cols(tiles(ux, SX - 2 - k), bm)
 
-    bm = lax.fori_loop(0, SX - 1, back_map, tiles(ux, SX - 1))
+    bm = lax.fori_loop(0, SX - 1, back_map, tiles(ux, SX - 1), unroll=3)
     zero = jnp.zeros((SY, NN), jnp.float32)
     values = f + g + bm + b + [-x for x in c] + [zero] * 3
     quarter = lanes_quarter((SY, NN))
@@ -135,7 +135,7 @@
             put(fy, 8 * h + y, f)
             return f
 
-        f = lax.fori_loop(1, SY, fore_y, f)
+        f = lax.fori_loop(1, SY, fore_y, f, unroll=True)
         for k in range(25):
             mats[k, pl.ds(h * 8, 8), :] = f[k]
     flight.wait()
@@ -144,23 +144,19 @@
             y = SY - 2 - k
             return add(tiles(fy, 8 * h + y), act_cols(turned(uy, h, y), c))
 
-        c = lax.fori_loop(0, SY - 1, back_y, tiles(fy, 8 * h + SY - 1))
+        c = lax.fori_loop(0, SY - 1, back_y, tiles(fy, 8 * h + SY - 1), unroll=True)
         for k in range(25):
             mats[50 + k, pl.ds(h * 8, 8), :] = -c[k]
 
         def back_map_y(k, bm):
             return act_cols(turned(uy, h, SY - 2 - k), bm)
 
-        bm = lax.fori_loop(0, SY - 1, back_map_y, turned(uy, h, SY - 1))
+        bm = lax.fori_loop(0, SY - 1, back_map_y, turned(uy, h, SY - 1), unroll=True)
         for k in range(25):
             mats[25 + k, pl.ds(h * 8, 8), :] = bm[k]
 
 
-def solve_kernel(z_ref, got, mats, out, matsel, un, fin, sin, sems):
-    at = jnp.where(z_ref[0] == 3, 50, 0)
-    chosen = pltpu.make_async_copy(mats.at[pl.ds(at, 25)], matsel, sems.at[0])
-    chosen.start()
-
+def solve_kernel(got, out, un, fin, sin):
     un[0] = got[...]
     for q in range(1, 4):
         for p in range(XS):
@@ -190,7 +186,6 @@
     quarter = lanes_quarter((8, NN))
     for p in range(XS):
         out[p] = jnp.where(quarter == 0, fin[p], pltpu.roll(sin[p], 32, 1))
-    chosen.wait()
 
 
 def replay_kernel(count, got, cell, owner, weight, ly, driven_h, lx_h, ux_h, dy_h, uy_h, dturn, vec, target,
@@ -273,42 +268,101 @@
             vec[5 + a, pl.ds(h * 8, 8), :] = b[a]
 
 
-def finish_kernel(z_ref, v1, v2, v3, m1, m2, m3, dturn, ly, uy, adjoint, metric, target,
+HALVES = [pl.ds(0, 8), pl.ds(8, 8)]
+
+
+def part_of(v, at, h, n=5):
+    return [v[at + k, HALVES[h], :] for k in range(n)]
+
+
+def by_side(z_ref, body):
+    @pl.when((z_ref[0] & 1) == 0)
+    def _():
+        body(0, 1)
+
+    @pl.when((z_ref[0] & 1) == 1)
+    def _():
+        body(1, 0)
+
+
+def pair_kernel(z_ref, mats, other, out):
+    m = [mats, other]
+
+    def body(lo, up):
+        for h in range(2):
+            t = act_cols(part_of(m[up], 50, h, 25), part_of(m[lo], 0, h, 25))
+            t = add(part_of(m[lo], 50, h, 25), act_cols(part_of(m[lo], 25, h, 25), t))
+            for k in range(25):
+                out[k, HALVES[h], :] = t[k]
+
+    by_side(z_ref, body)
+
+
+def join_kernel(z_ref, vec, near, mats, other, out):
+    m, v = [mats, other], [vec, near]
+
+    def body(lo, up):
+        def put_out(h, t):
+            for j in range(5):
+                out[j, HALVES[h], :] = t[j]
+
+        for h in range(2):
+            @pl.when(z_ref[0] < 2)
+            def _():
+                put_out(h, add(part_of(v[up], 0, h), act(part_of(m[up], 0, h, 25), part_of(v[lo], 0, h))))
+
+            @pl.when(z_ref[0] >= 2)
+            def _():
+                t = add(part_of(v[up], 5, h), act(part_of(m[up], 50, h, 25), part_of(v[lo], 0, h)))
+                put_out(h, add(part_of(v[lo], 5, h), act(part_of(m[lo], 25, h, 25), t)))
+
+    by_side(z_ref, body)
+
+
+def finish_kernel(z_ref, vec, near, beyond, mats, other, far, dturn, ly, uy, adjoint, metric, target,
                   spread, new, part, fin, sin, ft, ut, pk):
     z = z_ref[0]
-    halves = [pl.ds(0, 8), pl.ds(8, 8)]
-    zero = jnp.zeros((8, NN), jnp.float32)
-
-    def a_of(v, h):
-        return [v[j, halves[h], :] for j in range(5)]
-
-    def b_of(v, h):
-        return [v[5 + j, halves[h], :] for j in range(5)]
-
-    def mat(m, at, h):
-        return [m[25 * at + k, halves[h], :] for k in range(25)]
+    halves = HALVES
+    zero = [jnp.zeros((8, NN), jnp.float32)] * 5
 
     def put_in(h, f):
         for j in range(5):
             fin[j, halves[h], :] = f[j]
 
-    for h in range(2):
+    def put_back(h, s):
+        for j in range(5):
+            sin[j, halves[h], :] = s[j]
+
+    for h in range(2):
+        def lower(m1, a0, a1):
+            f2 = add(a1, act(part_of(m1, 0, h, 25), a0))
+            return add(part_of(beyond, 0, h), act(part_of(far, 0, h, 25), f2))
+
         @pl.when(z == 0)
         def _():
-            put_in(h, [zero] * 5)
+            put_in(h, zero)
+            a0 = part_of(vec, 0, h)
+            s2 = lower(other, a0, part_of(near, 0, h))
+            s1 = add(part_of(near, 5, h), act(part_of(other, 50, h, 25), a0))
+            put_back(h, add(s1, act(part_of(other, 25, h, 25), s2)))
 
         @pl.when(z == 1)
         def _():
-            put_in(h, a_of(v3, h))
+            a0 = part_of(near, 0, h)
+            put_in(h, a0)
+            put_back(h, lower(mats, a0, part_of(vec, 0, h)))
 
         @pl.when(z == 2)
         def _():
-            put_in(h, add(a_of(v3, h), act(mat(m3, 0, h), a_of(v2, h))))
+            f2 = part_of(beyond, 0, h)
+            put_in(h, f2)
+            f3 = add(part_of(vec, 0, h), act(part_of(mats, 0, h, 25), f2))
+            put_back(h, add(part_of(near, 5, h), act(part_of(other, 50, h, 25), f3)))
 
         @pl.when(z == 3)
         def _():
-            f = add(a_of(v2, h), act(mat(m2, 0, h), a_of(v1, h)))
-            put_in(h, add(a_of(v3, h), act(mat(m3, 0, h), f)))
+            put_in(h, add(part_of(near, 0, h), act(part_of(other, 0, h, 25), part_of(beyond, 0, h))))
+            put_back(h, zero)
 
     def turned(ref, y, h):
         return [ref[pl.ds(h * 1600 + k * 8 + y, 8, 200), :] for k in range(25)]
@@ -319,38 +373,6 @@
             f = sub([dturn[y, a, halves[h], :] for a in range(5)], act(turned(ly, y, h), f))
             for a in range(5):
                 ft[y, a, halves[h], :] = f[a]
-
-    def put_back(h, s):
-        for j in range(5):
-            sin[j, halves[h], :] = s[j]
-
-    for h in range(2):
-        def own(h=h):
-            return [ft[SY - 1, a, halves[h], :] for a in range(5)]
-
-        @pl.when(z == 0)
-        def _():
-            f1 = own()
-            f2 = add(a_of(v1, h), act(mat(m1, 0, h), f1))
-            f3 = add(a_of(v2, h), act(mat(m2, 0, h), f2))
-            s3 = add(b_of(v3, h), act(mat(m3, 0, h), f3))
-            s2 = add(add(b_of(v2, h), act(mat(m2, 2, h), f2)), act(mat(m2, 1, h), s3))
-            put_back(h, add(add(b_of(v1, h), act(mat(m1, 2, h), f1)), act(mat(m1, 1, h), s2)))
-
-        @pl.when(z == 1)
-        def _():
-            f2 = own()
-            f3 = add(a_of(v1, h), act(mat(m1, 0, h), f2))
-            s3 = add(b_of(v2, h), act(mat(m2, 2, h), f3))
-            put_back(h, add(add(b_of(v1, h), act(mat(m1, 2, h), f2)), act(mat(m1, 1, h), s3)))
-
-        @pl.when(z == 2)
-        def _():
-            put_back(h, add(b_of(v1, h), act(mat(m1, 2, h), own())))
-
-        @pl.when(z == 3)
-        def _():
-            put_back(h, [zero] * 5)
 
     for h in range(2):
         s = [sin[j, halves[h], :] for j in range(5)]
@@ -401,7 +423,7 @@
         scratch_shapes=[pltpu.VMEM(s, jnp.float32) for s in scratch]
         + [pltpu.SemaphoreType.DMA((n,)) for n in sems],
         compiler_params=pltpu.CompilerParams(vmem_limit_bytes=limit * 1024 * 1024),
-        cost_estimate=pl.CostEstimate(flops=cost, bytes_accessed=cost, transcendentals=0),
+        cost_estimate=pl.CostEstimate(flops=int(cost * 1e9), bytes_accessed=1000, transcendentals=0),
     )
 
 
@@ -426,34 +448,36 @@
     msg, driven = call(
         stream_kernel,
         [msg_shape, list(cells)],
-        [tile, tile, cells, tile, tile, cells, cells], hbm=4, sems=(14,), cost=10_000_000,
+        [tile, tile, cells, tile, tile, cells, cells], hbm=4, sems=(14,), cost=4,
     )(in_hbm(rhs), in_hbm(dx), in_hbm(lx), in_hbm(ux))
     got = lax.all_to_all(msg.reshape(XS, ROWS, NN), "stream", 0, 0, tiled=True)
     (mats,) = call(
-        span_kernel, [(75, SX, NN)], [(2 * SY, 25, 8, NN), uy.shape], vmem=1, hbm=2, sems=(1,), cost=10_000_000,
+        span_kernel, [(75, SX, NN)], [(2 * SY, 25, 8, NN), uy.shape], vmem=1, hbm=2, sems=(1,), cost=3,
     )(ly, in_hbm(uy), in_hbm(driven))
-    m1 = lax.ppermute(mats, "span", [(1, 0), (2, 1), (3, 2)])
-    m2 = lax.ppermute(mats, "span", [(2, 0), (3, 1), (1, 3)])
-    back, matsel = call(
-        solve_kernel, [(XS, 8, NN), (25, SX, NN)],
-        [(4, XS, ROWS, NN), (XS, 8, NN), (XS, 8, NN)], smem=1, vmem=1, hbm=1, sems=(1,), cost=10_000_000,
-    )(z, got, in_hbm(mats))
-    m3 = lax.ppermute(matsel, "span", [(3, 0), (1, 2), (2, 3)])
+    other = lax.ppermute(mats, "span", [(1, 0), (2, 3), (3, 2)])
+    (back,) = call(
+        solve_kernel, [(XS, 8, NN)],
+        [(4, XS, ROWS, NN), (XS, 8, NN), (XS, 8, NN)], vmem=1, cost=12,
+    )(got)
+    (pair,) = call(pair_kernel, [(25, SX, NN)], [], smem=1, vmem=2, cost=0.2)(z, mats, other)
+    far = lax.ppermute(pair, "span", [(2, 0), (3, 1)])
     back = lax.all_to_all(back, "stream", 0, 0, tiled=True)
     dturn, vec, target, spread, uy = call(
         replay_kernel,
         [(SY, 5, SX, NN), (10, SX, NN), (128, 128), (128, 128), uy.shape],
         [cells, tile, tile, tile, cells, (SX * 5 * SY, NN), (SY, 5, 8, NN)],
-        smem=1, vmem=5, hbm=5, sems=(17,), cost=30_000_000,
+        smem=1, vmem=5, hbm=5, sems=(17,), cost=4,
     )(node_count.reshape(1), back.reshape(XS * 8, NN), node_cell.reshape(1, -1), node_owner.reshape(1, -1),
       node_weight.reshape(1, -1), ly, in_hbm(driven), in_hbm(lx), in_hbm(ux), in_hbm(dy), in_hbm(uy))
-    v = [lax.ppermute(vec, "span", [((i + s) % 4, i) for i in range(4)]) for s in (1, 2, 3)]
+    near = lax.ppermute(vec, "span", [(i, i ^ 1) for i in range(4)])
+    (joint,) = call(join_kernel, [(5, SX, NN)], [], smem=1, vmem=4, cost=0.1)(z, vec, near, mats, other)
+    beyond = lax.ppermute(joint, "span", [(i, i ^ 2) for i in range(4)])
     new, part = call(
         finish_kernel,
         [cells, (128, NN)],
         [(5, SX, NN), (5, SX, NN), (SY, 5, SX, NN), (SY * 5 * SX, NN), (3, 128, NN)],
-        smem=1, vmem=13, cost=1_000_000,
-    )(z, *v, m1, m2, m3, dturn, ly, uy, adjoint, metric, target, spread)
+        smem=1, vmem=13, cost=2,
+    )(z, vec, near, beyond, mats, other, far, dturn, ly, uy, adjoint, metric, target, spread)
     parts = lax.all_to_all(part, ("stream", "span"), 0, 0, tiled=True)
     (control,) = call(sum_kernel, [(3, 16)], [], vmem=1)(parts)
     return new.transpose(0, 2, 1, 3), control

time: 76.4 us -> 73.1 us (0.957)
  starting transfers between devices: 26.3 us -> 20 us
  blocking collectives: 17 us -> 19.8 us
  waiting for transfers between devices: 14.1 us -> 15.5 us
  Pallas kernels: 17.2 us -> 16.1 us
    ppermute x6 -> x4, starting transfers between devices: 14 us -> 7.6 us  [the longest x1 3.3 us: shards(): beyond = lax.ppermute(joint, 'span', [(i, i ^ 2) for i in range(4)])]
    all_to_all x1, waiting for transfers between devices: 6.97 us -> 2.19 us  [shards(): back = lax.all_to_all(back, 'stream', 0, 0, tiled=True)]
    ppermute x6 -> x4, waiting for transfers between devices: 2.32 us -> 7.08 us  [the longest x1 3.32 us: shards(): other = lax.ppermute(mats, 'span', [(1, 0), (2, 3), (3, 2)])]
    all_to_all x1, blocking collectives: 17 us -> 19.8 us  [shards(): parts = lax.all_to_all(part, ('stream', 'span'), 0, 0, tiled=True)]
    all_to_all x1, waiting for transfers between devices: 4.78 us -> 6.23 us  [shards(): got = lax.all_to_all(msg.reshape(XS, ROWS, NN), 'stream', 0, 0, tiled=True)]
    pallas_call x1, Pallas kernels: 2.75 us -> 1.69 us  [shards(): call(finish_kernel, [cells, (128, NN)], [(5, SX, NN), (5, SX, NN), (SY, 5...]
    pallas_call x1 -> x3, Pallas kernels: 1.84 us -> 2.03 us  [the longest x1 1.84 us: shards(): call(solve_kernel, [(XS, 8, NN)], [(4, XS, ROWS, NN), (XS, 8, NN), (XS, 8...]
  transfers between devices with their start and end apart: 8 -> 6, of which waited for: 3 -> 5; matrix products, arithmetic and copies ran while one was open for 0% -> 0% of each run, Pallas kernels for 11% -> 12%
where the time goes in v3:
time: 73.1 us; the launch traced here: 72.7 us
  starting transfers between devices  20 us (27%)
  blocking collectives  19.8 us (27%)
  Pallas kernels  16.1 us (22%)
  waiting for transfers between devices  15.5 us (21%)
  between operations  1.4 us (2%)
    all_to_all x1, blocking collectives, shards(): parts = lax.all_to_all(part, ('stream', 'span'), 0, 0, tiled=True)  19.8 us
    all_to_all x1, starting transfers between devices, shards(): got = lax.all_to_all(msg.reshape(XS, ROWS, NN), 'stream', 0, 0, tiled=True)  8.6 us
    all_to_all x1, waiting for transfers between devices, shards(): got = lax.all_to_all(msg.reshape(XS, ROWS, NN), 'stream', 0, 0, tiled=True)  6.23 us
    pallas_call x1, Pallas kernels, shards(): call(stream_kernel, [msg_shape, list(cells)], [tile, tile, cells, tile, t...  5.02 us
    pallas_call x1, Pallas kernels, shards(): call(replay_kernel, [(SY, 5, SX, NN), (10, SX, NN), (128, 128), (128, 128...  3.83 us
    all_to_all x1, starting transfers between devices, shards(): back = lax.all_to_all(back, 'stream', 0, 0, tiled=True)  3.77 us
    ppermute x1, waiting for transfers between devices, shards(): other = lax.ppermute(mats, 'span', [(1, 0), (2, 3), (3, 2)])  3.32 us
    ppermute x1, starting transfers between devices, shards(): beyond = lax.ppermute(joint, 'span', [(i, i ^ 2) for i in range(4)])  3.3 us
  transfers between devices with their start and end apart: 6, of which 5 were waited for; matrix products, arithmetic and copies ran while one was open for 0% of the time, Pallas kernels for 12%

profile of v3, /device:TPU:1, one launch (start us, length us, event | category | flops | bytes accessed | tf_op | source)
XLA Modules:
  0.0 72.7 jit_solution(3412655288876428179)
XLA Ops:
  0.6 0.0 copy-start
  0.6 5.0 %shard_map.140 = (f32[768,128]{1,0:T(8,128)}, f32[16,5,8,128]{3,2,1,0:T(8,128)}) custom-call(f32[16,5,8,128]{3,2,1,0:T(8,128)} %bitcast.55, f32[16,25,8,128]{3,2,1,0:T(8,128)} %bitcast.47, f32[16,25,8,128]{3,2,1,0:T(8,128)} %bitcast.48, f32[16,25,8,128]{3,2,1,0:T(8,128)} %bitcast.50), custom_call_target="tpu_custom_call" | custom-call | flops 4000000000 | bytes 1000 | tf_op jit(solution)/shard_map/pallas_call | solution.py:448
  5.7 8.6 %all-to-all-start = ((f32[32,24,128]{2,1,0:T(8,128)}), f32[32,24,128]{2,1,0:T(8,128)S(1)}, u32[]{:S(2)}, u32[]{:S(2)}) async-start(f32[32,24,128]{2,1,0:T(8,128)} %bitcast.9), calls=%async_computation | async-start | bytes 786432 | tf_op jit(solution)/shard_map/all_to_all | solution.py:453
  14.3 0.0 copy-done
  14.3 2.8 %shard_map.143.mats = f32[75,16,128]{2,1,0:T(8,128)S(1)} custom-call(f32[3200,128]{1,0:T(8,128)S(1)} %bitcast.39, f32[3200,128]{1,0:T(8,128)} %bitcast.53, f32[16,5,8,128]{3,2,1,0:T(8,128)} %get-tuple-element.12.driven_h.after), custom_call_target="tpu_custom_call" | custom-call | flops 3000000000 | bytes 1000 | tf_op jit(solution)/shard_map/pallas_call | solution.py:454
  17.1 1.3 %collective-permute-start.1 = (f32[75,16,128]{2,1,0:T(8,128)S(1)}, f32[75,16,128]{2,1,0:T(8,128)S(1)}, u32[]{:S(2)}, u32[]{:S(2)}) collective-permute-start(f32[75,16,128]{2,1,0:T(8,128)S(1)} %shard_map.143.mats), channel_id=1, source_target_pairs={{1,0},{2,3},{3,2},{5,4},{6,7},{7,6},{9,8},{10,11},{11,10},{13,12},... | collective-permute-start | bytes 1843208 | tf_op jit(solution)/shard_map/ppermute | solution.py:457
  18.4 6.2 %all-to-all-done.got = f32[32,24,128]{2,1,0:T(8,128)S(1)} async-done(((f32[32,24,128]{2,1,0:T(8,128)}), f32[32,24,128]{2,1,0:T(8,128)S(1)}, u32[]{:S(2)}, u32[]{:S(2)}) %all-to-all-start) | async-done | bytes 393248 | tf_op jit(solution)/shard_map/all_to_all | solution.py:453
  24.6 1.8 %shard_map.141 = f32[32,8,128]{2,1,0:T(8,128)} custom-call(f32[32,24,128]{2,1,0:T(8,128)S(1)} %all-to-all-done.got), custom_call_target="tpu_custom_call" | custom-call | flops 12000000000 | bytes 1000 | tf_op jit(solution)/shard_map/pallas_call | solution.py:458
  26.4 0.0 copy-start.3
  26.4 0.0 copy-start.4
  26.4 0.0 copy-start.5
  26.4 3.8 %all-to-all-start.1 = ((f32[32,8,128]{2,1,0:T(8,128)}), f32[32,8,128]{2,1,0:T(8,128)S(1)}, u32[]{:S(2)}, u32[]{:S(2)}) async-start(f32[32,8,128]{2,1,0:T(8,128)} %shard_map.141), calls=%async_computation.1 | async-start | bytes 262144 | tf_op jit(solution)/shard_map/all_to_all | solution.py:464
  30.9 3.3 %collective-permute-done.1.other = f32[75,16,128]{2,1,0:T(8,128)S(1)} collective-permute-done((f32[75,16,128]{2,1,0:T(8,128)S(1)}, f32[75,16,128]{2,1,0:T(8,128)S(1)}, u32[]{:S(2)}, u32[]{:S(2)}) %collective-permute-start.1) | collective-permute-done | bytes 614432 | tf_op jit(solution)/shard_map/ppermute | solution.py:457
  34.2 0.1 shard_map.145
  34.3 1.3 %collective-permute-start.3 = (f32[25,16,128]{2,1,0:T(8,128)S(1)}, f32[25,16,128]{2,1,0:T(8,128)S(1)}, u32[]{:S(2)}, u32[]{:S(2)}) collective-permute-start(f32[25,16,128]{2,1,0:T(8,128)S(1)} %shard_map.145), channel_id=1, source_target_pairs={{2,0},{3,1},{6,4},{7,5},{10,8},{11,9},{14,12},{15,13},{18,16},{19,... | collective-permute-start | bytes 614408 | tf_op jit(solution)/shard_map/ppermute | solution.py:463
  35.6 2.2 %all-to-all-done.1 = f32[32,8,128]{2,1,0:T(8,128)S(1)} async-done(((f32[32,8,128]{2,1,0:T(8,128)}), f32[32,8,128]{2,1,0:T(8,128)S(1)}, u32[]{:S(2)}, u32[]{:S(2)}) %all-to-all-start.1) | async-done | bytes 131104 | tf_op jit(solution)/shard_map/all_to_all | solution.py:464
  37.8 0.0 copy-done.3
  37.8 0.0 copy-done.4
  37.8 0.0 copy-done.5
  37.8 0.0 copy-start.1
  37.8 0.0 copy-start.2
  37.8 3.8 %shard_map.142 = (f32[8,5,16,128]{3,2,1,0:T(8,128)S(1)}, f32[10,16,128]{2,1,0:T(8,128)S(1)}, f32[128,128]{1,0:T(8,128)S(1)}, f32[128,128]{1,0:T(8,128)S(1)}, f32[3200,128]{1,0:T(8,128)S(1)}) custom-call(s32[1]{0:T(128)} %bitcast.35.count, f32[256,128]{1,0:T(8,128)S(1)} %bitcast.37, s32[1,128]{1,0:T(1,128)S(1)} %bitcast.44, s32[1,128]{1,0:T(1,128)S(1)} %bitcast.45, ...), custom_call_target="tpu_custom_call" | custom-call | flops 4000000000 | bytes 1000 | tf_op jit(solution)/shard_map/pallas_call | solution.py:465
  41.7 1.7 %collective-permute-start = (f32[10,16,128]{2,1,0:T(8,128)S(1)}, f32[10,16,128]{2,1,0:T(8,128)S(1)}, u32[]{:S(2)}, u32[]{:S(2)}) collective-permute-start(f32[10,16,128]{2,1,0:T(8,128)S(1)} %get-tuple-element.13.vec), channel_id=1, source_target_pairs={{0,1},{1,0},{2,3},{3,2},{4,5},{5,4},{6,7},{7,6},{8,9},{9,8},{10,11... | collective-permute-start | bytes 245768 | tf_op jit(solution)/shard_map/ppermute | solution.py:472
  43.4 2.4 %collective-permute-done.near = f32[10,16,128]{2,1,0:T(8,128)S(1)} collective-permute-done((f32[10,16,128]{2,1,0:T(8,128)S(1)}, f32[10,16,128]{2,1,0:T(8,128)S(1)}, u32[]{:S(2)}, u32[]{:S(2)}) %collective-permute-start) | collective-permute-done | bytes 81952 | tf_op jit(solution)/shard_map/ppermute | solution.py:472
  45.8 0.1 shard_map.144
  45.8 3.3 %collective-permute-start.2 = (f32[5,16,128]{2,1,0:T(8,128)S(1)}, f32[5,16,128]{2,1,0:T(8,128)S(1)}, u32[]{:S(2)}, u32[]{:S(2)}) collective-permute-start(f32[5,16,128]{2,1,0:T(8,128)S(1)} %shard_map.144), channel_id=1, source_target_pairs={{0,2},{1,3},{2,0},{3,1},{4,6},{5,7},{6,4},{7,5},{8,10},{9,11},{10,... | collective-permute-start | bytes 122888 | tf_op jit(solution)/shard_map/ppermute | solution.py:474
  49.1 1.4 %collective-permute-done.2.beyond = f32[5,16,128]{2,1,0:T(8,128)S(1)} collective-permute-done((f32[5,16,128]{2,1,0:T(8,128)S(1)}, f32[5,16,128]{2,1,0:T(8,128)S(1)}, u32[]{:S(2)}, u32[]{:S(2)}) %collective-permute-start.2) | collective-permute-done | bytes 40992 | tf_op jit(solution)/shard_map/ppermute | solution.py:474
  50.5 0.0 collective-permute-done.3.far
  50.5 0.0 copy-done.1
  50.5 0.0 copy-done.2
  50.5 1.7 %shard_map.146 = (f32[16,5,8,128]{3,2,1,0:T(8,128)}, f32[128,128]{1,0:T(8,128)S(1)}) custom-call(s32[1]{0:T(128)} %bitcast.z_ref, f32[10,16,128]{2,1,0:T(8,128)S(1)} %get-tuple-element.13.vec, f32[10,16,128]{2,1,0:T(8,128)S(1)} %collective-permute-done.near, f32[5,16,128]{2,1,0:T(8,128)S(1)} %collective-permute-done.2.beyond, ...), custom_call_target="tpu_custom_call" | custom-call | flops 2000000000 | bytes 1000 | tf_op jit(solution)/shard_map/pallas_call | solution.py:475
  52.2 19.8 %all_to_all.21 = f32[128,1,128]{2,1,0:T(1,128)S(1)} all-to-all(f32[128,1,128]{2,1,0:T(1,128)S(1)} %bitcast.38), channel_id=1, replica_groups=mesh['stream'=32,'span'=4] {'stream','span'}, dimensions={0} | all-to-all | bytes 131072 | tf_op jit(solution)/shard_map/all_to_all | solution.py:481
  72.0 0.7 %shard_map.147 = f32[3,16]{1,0:T(4,128)} custom-call(f32[128,128]{1,0:T(8,128)S(1)} %bitcast.36), custom_call_target="tpu_custom_call" | custom-call | bytes 1000 | tf_op jit(solution)/shard_map/pallas_call | solution.py:482
Async XLA Ops:
  0.6 13.6 %copy-start = (f32[16,8,5,5,128]{4,1,3,2,0:T(8,128)S(1)}, f32[16,8,5,5,128]{4,1,3,2,0:T(8,128)}, u32[]{:S(2)}) copy-start(f32[16,8,5,5,128]{4,1,3,2,0:T(8,128)} %param.19) | copy-start | bytes 4915204
  5.7 18.9 %all-to-all-start = ((f32[32,24,128]{2,1,0:T(8,128)}), f32[32,24,128]{2,1,0:T(8,128)S(1)}, u32[]{:S(2)}, u32[]{:S(2)}) async-start(f32[32,24,128]{2,1,0:T(8,128)} %bitcast.9), calls=%async_computation | async-start | bytes 786432 | tf_op jit(solution)/shard_map/all_to_all | solution.py:453
  17.1 17.1 %collective-permute-start.1 = (f32[75,16,128]{2,1,0:T(8,128)S(1)}, f32[75,16,128]{2,1,0:T(8,128)S(1)}, u32[]{:S(2)}, u32[]{:S(2)}) collective-permute-start(f32[75,16,128]{2,1,0:T(8,128)S(1)} %shard_map.143.mats), channel_id=1, source_target_pairs={{1,0},{2,3},{3,2},{5,4},{6,7},{7,6},{9,8},{10,11},{11,10},{13,12},... | collective-permute-start | bytes 1843208 | tf_op jit(solution)/shard_map/ppermute | solution.py:457
  26.4 11.4 %copy-start.3 = (s32[1,1,128]{2,1,0:T(1,128)S(1)}, s32[1,1,128]{2,1,0:T(1,128)}, u32[]{:S(2)}) copy-start(s32[1,1,128]{2,1,0:T(1,128)} %param.22) | copy-start | bytes 1540
  26.4 11.4 %copy-start.4 = (s32[1,1,128]{2,1,0:T(1,128)S(1)}, s32[1,1,128]{2,1,0:T(1,128)}, u32[]{:S(2)}) copy-start(s32[1,1,128]{2,1,0:T(1,128)} %param.23) | copy-start | bytes 1540
  26.4 11.4 %copy-start.5 = (f32[1,1,128]{2,1,0:T(1,128)S(1)}, f32[1,1,128]{2,1,0:T(1,128)}, u32[]{:S(2)}) copy-start(f32[1,1,128]{2,1,0:T(1,128)} %param.24) | copy-start | bytes 1540
  26.4 11.4 %all-to-all-start.1 = ((f32[32,8,128]{2,1,0:T(8,128)}), f32[32,8,128]{2,1,0:T(8,128)S(1)}, u32[]{:S(2)}, u32[]{:S(2)}) async-start(f32[32,8,128]{2,1,0:T(8,128)} %shard_map.141), calls=%async_computation.1 | async-start | bytes 262144 | tf_op jit(solution)/shard_map/all_to_all | solution.py:464
  34.3 16.2 %collective-permute-start.3 = (f32[25,16,128]{2,1,0:T(8,128)S(1)}, f32[25,16,128]{2,1,0:T(8,128)S(1)}, u32[]{:S(2)}, u32[]{:S(2)}) collective-permute-start(f32[25,16,128]{2,1,0:T(8,128)S(1)} %shard_map.145), channel_id=1, source_target_pairs={{2,0},{3,1},{6,4},{7,5},{10,8},{11,9},{14,12},{15,13},{18,16},{19,... | collective-permute-start | bytes 614408 | tf_op jit(solution)/shard_map/ppermute | solution.py:463
  37.8 12.7 %copy-start.1 = (bf16[16,8,3,5,128]{4,1,3,2,0:T(8,128)(2,1)S(1)}, bf16[16,8,3,5,128]{4,1,3,2,0:T(8,128)(2,1)}, u32[]{:S(2)}) copy-start(bf16[16,8,3,5,128]{4,1,3,2,0:T(8,128)(2,1)} %param.21) | copy-start | bytes 1474564
  37.8 12.7 %copy-start.2 = (f32[16,8,5,128]{3,1,2,0:T(8,128)S(1)}, f32[16,8,5,128]{3,1,2,0:T(8,128)}, u32[]{:S(2)}) copy-start(f32[16,8,5,128]{3,1,2,0:T(8,128)} %param.14) | copy-start | bytes 983044
  41.7 4.1 %collective-permute-start = (f32[10,16,128]{2,1,0:T(8,128)S(1)}, f32[10,16,128]{2,1,0:T(8,128)S(1)}, u32[]{:S(2)}, u32[]{:S(2)}) collective-permute-start(f32[10,16,128]{2,1,0:T(8,128)S(1)} %get-tuple-element.13.vec), channel_id=1, source_target_pairs={{0,1},{1,0},{2,3},{3,2},{4,5},{5,4},{6,7},{7,6},{8,9},{9,8},{10,11... | collective-permute-start | bytes 245768 | tf_op jit(solution)/shard_map/ppermute | solution.py:472
  45.8 4.7 %collective-permute-start.2 = (f32[5,16,128]{2,1,0:T(8,128)S(1)}, f32[5,16,128]{2,1,0:T(8,128)S(1)}, u32[]{:S(2)}, u32[]{:S(2)}) collective-permute-start(f32[5,16,128]{2,1,0:T(8,128)S(1)} %shard_map.144), channel_id=1, source_target_pairs={{0,2},{1,3},{2,0},{3,1},{4,6},{5,7},{6,4},{7,5},{8,10},{9,11},{10,... | collective-permute-start | bytes 122888 | tf_op jit(solution)/shard_map/ppermute | solution.py:474

commit v4 on v3

--- a/solution.py
+++ b/solution.py
@@ -56,12 +56,26 @@
 STEP = 4
 
 
-def stream_kernel(rhs_h, dx_h, lx_h, ux_h, msg, driven_h, lx, ux, rhs, dx, fs, gs, driven, sems):
+def maps_kernel(rhs_h, dx_h, lx_h, ux_h, ly_h, uy_h, msg_h, driven_h, mats,
+                lx, ux, rhs, dx, fs, gs, driven, msg, ly, uy, fy, sems):
     chunks = [pl.ds(k * STEP, STEP) for k in range(SX // STEP)]
-    pairs = []
+    halves = [pl.ds(SX // 2, SX // 2), pl.ds(0, SX // 2)]
+    pairs = [(ux_h.at[c], ux.at[c]) for c in halves]
+    pairs += [(rhs_h, rhs)]
     for c in chunks:
-        pairs += [(lx_h.at[c], lx.at[c]), (dx_h.at[c], dx.at[c]), (rhs_h.at[c], rhs.at[c])]
-    flight = copies(pairs + [(ux_h, ux)], sems)
+        pairs += [(lx_h.at[c], lx.at[c]), (dx_h.at[c], dx.at[c])]
+    late = len(pairs)
+    pairs += [(ly_h, ly), (uy_h, uy)]
+    flight = copies(pairs, sems)
+    out_sem = len(pairs)
+
+    def back_map(k, bm):
+        return act_cols(tiles(ux, SX - 2 - k), bm)
+
+    flight[0].wait()
+    bm = lax.fori_loop(0, SX // 2 - 1, back_map, tiles(ux, SX - 1), unroll=True)
+    flight[1].wait()
+    bm = lax.fori_loop(SX // 2 - 1, SX - 1, back_map, bm, unroll=True)
 
     def fore(i, carry):
         g, f = carry
@@ -75,18 +89,18 @@
         return g, f
 
     for k in range(len(chunks)):
-        for c in flight[3 * k : 3 * k + 3]:
+        for c in flight[3 + 2 * k : 5 + 2 * k]:
             c.wait()
         if k == 0:
+            flight[2].wait()
             g = act(tiles(dx, 0), tiles(rhs, 0, 5))
             put(driven, 0, g)
             put(gs, 0, g)
             f = tiles(lx, 0)
             put(fs, 0, f)
         g, f = lax.fori_loop(max(1, STEP * k), STEP * k + STEP, fore, (g, f), unroll=True)
-    kept = pltpu.make_async_copy(driven, driven_h, sems.at[13])
+    kept = pltpu.make_async_copy(driven, driven_h, sems.at[out_sem])
     kept.start()
-    flight[-1].wait()
 
     def back(k, carry):
         i = SX - 2 - k
@@ -97,11 +111,6 @@
         return b, c
 
     b, c = lax.fori_loop(0, SX - 1, back, (g, f), unroll=3)
-
-    def back_map(k, bm):
-        return act_cols(tiles(ux, SX - 2 - k), bm)
-
-    bm = lax.fori_loop(0, SX - 1, back_map, tiles(ux, SX - 1), unroll=3)
     zero = jnp.zeros((SY, NN), jnp.float32)
     values = f + g + bm + b + [-x for x in c] + [zero] * 3
     quarter = lanes_quarter((SY, NN))
@@ -117,15 +126,13 @@
     for r in range(22, ROWS):
         for nq in range(4):
             msg[pl.ds(nq * 8 * ROWS + r, 8, ROWS), :] = zero
-    kept.wait()
-
-
-def span_kernel(ly, uy_h, after, mats, fy, uy, sems):
-    del after
-    (flight,) = copies([(uy_h, uy)], sems)
+    sent = pltpu.make_async_copy(msg, msg_h, sems.at[out_sem + 1])
+    sent.start()
+
     def turned(ref, h, y):
         return [ref[pl.ds(h * 1600 + k * 8 + y, 8, 200), :] for k in range(25)]
 
+    flight[late].wait()
     for h in range(2):
         f = turned(ly, h, 0)
         put(fy, 8 * h, f)
@@ -138,7 +145,7 @@
         f = lax.fori_loop(1, SY, fore_y, f, unroll=True)
         for k in range(25):
             mats[k, pl.ds(h * 8, 8), :] = f[k]
-    flight.wait()
+    flight[late + 1].wait()
     for h in range(2):
         def back_y(k, c):
             y = SY - 2 - k
@@ -154,6 +161,8 @@
         bm = lax.fori_loop(0, SY - 1, back_map_y, turned(uy, h, SY - 1), unroll=True)
         for k in range(25):
             mats[25 + k, pl.ds(h * 8, 8), :] = bm[k]
+    sent.wait()
+    kept.wait()
 
 
 def solve_kernel(got, out, un, fin, sin):
@@ -172,7 +181,7 @@
             fin[p, j : j + 1, :] = f[j]
         return add(act([val(p, k) for k in range(25)], f), [val(p, 25 + j) for j in range(5)])
 
-    lax.fori_loop(0, XS, fore, zero, unroll=8)
+    lax.fori_loop(0, XS, fore, zero, unroll=16)
 
     def back(k, s):
         p = XS - 1 - k
@@ -182,7 +191,7 @@
         known = add(act([val(p, 60 + k) for k in range(25)], f), [val(p, 55 + j) for j in range(5)])
         return add(known, act([val(p, 30 + k) for k in range(25)], s))
 
-    lax.fori_loop(0, XS, back, zero, unroll=8)
+    lax.fori_loop(0, XS, back, zero, unroll=16)
     quarter = lanes_quarter((8, NN))
     for p in range(XS):
         out[p] = jnp.where(quarter == 0, fin[p], pltpu.roll(sin[p], 32, 1))
@@ -190,11 +199,10 @@
 
 def replay_kernel(count, got, cell, owner, weight, ly, driven_h, lx_h, ux_h, dy_h, uy_h, dturn, vec, target,
                   spread, uy, driven, lx, ux, dy, fs, sd, gt, sems):
-    chunks = [pl.ds(k * STEP, STEP) for k in range(SX // STEP)]
-    pairs = []
-    for c in chunks:
-        pairs += [(lx_h.at[c], lx.at[c]), (driven_h.at[c], driven.at[c])]
-    for c in chunks[::-1]:
+    step = SX // 2
+    halves = [pl.ds(0, step), pl.ds(step, step)]
+    pairs = [(driven_h, driven)] + [(lx_h.at[c], lx.at[c]) for c in halves]
+    for c in halves[::-1]:
         pairs += [(ux_h.at[c], ux.at[c]), (dy_h.at[c], dy.at[c])]
     flight = copies(pairs + [(uy_h, uy)], sems)
 
@@ -228,10 +236,10 @@
         return f
 
     f = [entering(j, 0) for j in range(5)]
-    for k in range(len(chunks)):
-        for c in flight[2 * k : 2 * k + 2]:
-            c.wait()
-        f = lax.fori_loop(STEP * k, STEP * k + STEP, fore, f)
+    flight[0].wait()
+    for k in range(2):
+        flight[1 + k].wait()
+        f = lax.fori_loop(step * k, step * k + step, fore, f, unroll=2)
 
     def back(k, s):
         i = SX - 1 - k
@@ -242,10 +250,10 @@
         return s
 
     s = [entering(j, 1) for j in range(5)]
-    for k in range(len(chunks)):
-        for c in flight[2 * len(chunks) + 2 * k : 2 * len(chunks) + 2 * k + 2]:
-            c.wait()
-        s = lax.fori_loop(STEP * k, STEP * k + STEP, back, s)
+    for k in range(2):
+        flight[3 + 2 * k].wait()
+        flight[4 + 2 * k].wait()
+        s = lax.fori_loop(step * k, step * k + step, back, s, unroll=2)
     flight[-1].wait()
     for h in range(2):
         def turned(ref, y):
@@ -320,7 +328,7 @@
 
 
 def finish_kernel(z_ref, vec, near, beyond, mats, other, far, dturn, ly, uy, adjoint, metric, target,
-                  spread, new, part, fin, sin, ft, ut, pk):
+                  spread, new_h, part, fin, sin, ft, ut, pk, new, sems):
     z = z_ref[0]
     halves = HALVES
     zero = [jnp.zeros((8, NN), jnp.float32)] * 5
@@ -382,10 +390,12 @@
                 ut[pl.ds((y * 5 + a) * 16 + h * 8, 8), :] = s[a]
 
     for x in range(SX):
-        fresh = []
         for a in range(5):
-            fresh.append(adjoint[x, a] + ut[pl.ds(a * 16 + x, 8, 80), :])
-            new[x, a] = fresh[a]
+            new[x, a] = adjoint[x, a] + ut[pl.ds(a * 16 + x, 8, 80), :]
+    sent = pltpu.make_async_copy(new, new_h, sems.at[0])
+    sent.start()
+    for x in range(SX):
+        fresh = tiles(new, x, 5)
         for k in range(3):
             t = metric[x, 5 * k].astype(jnp.float32) * fresh[0]
             for a in range(1, 5):
@@ -400,6 +410,7 @@
     high = value.astype(jnp.bfloat16).astype(jnp.float32)
     value = jnp.where(group < 3, high, value - high).astype(jnp.bfloat16)
     part[...] = jnp.dot(target[...].astype(jnp.bfloat16), value, preferred_element_type=jnp.float32)
+    sent.wait()
 
 
 def sum_kernel(parts, out):
@@ -445,38 +456,36 @@
     z = lax.axis_index("span").astype(jnp.int32).reshape(1)
 
     tile, cells, msg_shape = (SX, 25, SY, NN), (SX, 5, SY, NN), (XS * ROWS, NN)
-    msg, driven = call(
-        stream_kernel,
-        [msg_shape, list(cells)],
-        [tile, tile, cells, tile, tile, cells, cells], hbm=4, sems=(14,), cost=4,
-    )(in_hbm(rhs), in_hbm(dx), in_hbm(lx), in_hbm(ux))
+    msg, driven, mats = call(
+        maps_kernel,
+        [list(msg_shape), list(cells), (75, SX, NN)],
+        [tile, tile, cells, tile, tile, cells, cells, msg_shape, ly.shape, uy.shape, (2 * SY, 25, 8, NN)],
+        hbm=6, sems=(15,), cost=7, limit=20,
+    )(in_hbm(rhs), in_hbm(dx), in_hbm(lx), in_hbm(ux), in_hbm(ly), in_hbm(uy))
     got = lax.all_to_all(msg.reshape(XS, ROWS, NN), "stream", 0, 0, tiled=True)
-    (mats,) = call(
-        span_kernel, [(75, SX, NN)], [(2 * SY, 25, 8, NN), uy.shape], vmem=1, hbm=2, sems=(1,), cost=3,
-    )(ly, in_hbm(uy), in_hbm(driven))
     other = lax.ppermute(mats, "span", [(1, 0), (2, 3), (3, 2)])
     (back,) = call(
         solve_kernel, [(XS, 8, NN)],
         [(4, XS, ROWS, NN), (XS, 8, NN), (XS, 8, NN)], vmem=1, cost=12,
     )(got)
     (pair,) = call(pair_kernel, [(25, SX, NN)], [], smem=1, vmem=2, cost=0.2)(z, mats, other)
-    far = lax.ppermute(pair, "span", [(2, 0), (3, 1)])
+    far = lax.ppermute(pair, "span", [(3, 0), (2, 1)])
     back = lax.all_to_all(back, "stream", 0, 0, tiled=True)
     dturn, vec, target, spread, uy = call(
         replay_kernel,
         [(SY, 5, SX, NN), (10, SX, NN), (128, 128), (128, 128), uy.shape],
         [cells, tile, tile, tile, cells, (SX * 5 * SY, NN), (SY, 5, 8, NN)],
-        smem=1, vmem=5, hbm=5, sems=(17,), cost=4,
+        smem=1, vmem=5, hbm=5, sems=(8,), cost=4,
     )(node_count.reshape(1), back.reshape(XS * 8, NN), node_cell.reshape(1, -1), node_owner.reshape(1, -1),
       node_weight.reshape(1, -1), ly, in_hbm(driven), in_hbm(lx), in_hbm(ux), in_hbm(dy), in_hbm(uy))
     near = lax.ppermute(vec, "span", [(i, i ^ 1) for i in range(4)])
     (joint,) = call(join_kernel, [(5, SX, NN)], [], smem=1, vmem=4, cost=0.1)(z, vec, near, mats, other)
-    beyond = lax.ppermute(joint, "span", [(i, i ^ 2) for i in range(4)])
+    beyond = lax.ppermute(joint, "span", [(i, 3 - i) for i in range(4)])
     new, part = call(
         finish_kernel,
-        [cells, (128, NN)],
-        [(5, SX, NN), (5, SX, NN), (SY, 5, SX, NN), (SY * 5 * SX, NN), (3, 128, NN)],
-        smem=1, vmem=13, cost=2,
+        [list(cells), (128, NN)],
+        [(5, SX, NN), (5, SX, NN), (SY, 5, SX, NN), (SY * 5 * SX, NN), (3, 128, NN), cells],
+        sems=(1,), smem=1, vmem=13, cost=2,
     )(z, vec, near, beyond, mats, other, far, dturn, ly, uy, adjoint, metric, target, spread)
     parts = lax.all_to_all(part, ("stream", "span"), 0, 0, tiled=True)
     (control,) = call(sum_kernel, [(3, 16)], [], vmem=1)(parts)

time: 73.1 us -> 71.1 us (0.973)
  blocking collectives: 19.8 us -> 17 us
  waiting for transfers between devices: 15.5 us -> 18.3 us
  Pallas kernels: 16.1 us -> 13.9 us
    ppermute x1, waiting for transfers between devices: 3.32 us -> 0.53 us  [shards(): other = lax.ppermute(mats, 'span', [(1, 0), (2, 3), (3, 2)])]
    all_to_all x1, waiting for transfers between devices: 2.19 us -> 4.98 us  [shards(): back = lax.all_to_all(back, 'stream', 0, 0, tiled=True)]
    all_to_all x1, blocking collectives: 19.8 us -> 17 us  [shards(): parts = lax.all_to_all(part, ('stream', 'span'), 0, 0, tiled=True)]
    all_to_all x1, waiting for transfers between devices: 6.23 us -> 9 us  [shards(): got = lax.all_to_all(msg.reshape(XS, ROWS, NN), 'stream', 0, 0, tiled=True)]
    pallas_call x3 -> x2, Pallas kernels: 9.46 us -> 7.41 us  [the longest x1 5.75 us: shards(): call(maps_kernel, [list(msg_shape), list(cells), (75, SX, NN)], [tile, ti...]
  transfers between devices with their start and end apart: 6 -> 6, of which waited for: 5 -> 5; matrix products, arithmetic and copies ran while one was open for 0% -> 0% of each run, Pallas kernels for 12% -> 8%
where the time goes in v4:
time: 71.1 us; the launch traced here: 70.7 us
  starting transfers between devices  20.1 us (28%)
  waiting for transfers between devices  18.3 us (26%)
  blocking collectives  17 us (24%)
  Pallas kernels  13.9 us (20%)
  between operations  1.39 us (2%)
    all_to_all x1, blocking collectives, shards(): parts = lax.all_to_all(part, ('stream', 'span'), 0, 0, tiled=True)  17 us
    all_to_all x1, waiting for transfers between devices, shards(): got = lax.all_to_all(msg.reshape(XS, ROWS, NN), 'stream', 0, 0, tiled=True)  9 us
    all_to_all x1, starting transfers between devices, shards(): got = lax.all_to_all(msg.reshape(XS, ROWS, NN), 'stream', 0, 0, tiled=True)  8.6 us
    pallas_call x1, Pallas kernels, shards(): call(maps_kernel, [list(msg_shape), list(cells), (75, SX, NN)], [tile, ti...  5.75 us
    all_to_all x1, waiting for transfers between devices, shards(): back = lax.all_to_all(back, 'stream', 0, 0, tiled=True)  4.98 us
    all_to_all x1, starting transfers between devices, shards(): back = lax.all_to_all(back, 'stream', 0, 0, tiled=True)  3.78 us
    pallas_call x1, Pallas kernels, shards(): call(replay_kernel, [(SY, 5, SX, NN), (10, SX, NN), (128, 128), (128, 128...  3.72 us
    ppermute x1, starting transfers between devices, shards(): beyond = lax.ppermute(joint, 'span', [(i, 3 - i) for i in range(4)])  3.45 us
  transfers between devices with their start and end apart: 6, of which 5 were waited for; matrix products, arithmetic and copies ran while one was open for 0% of the time, Pallas kernels for 8%

profile of v4, /device:TPU:1, one launch (start us, length us, event | category | flops | bytes accessed | tf_op | source)
XLA Modules:
  0.0 70.7 jit_solution(17772274644271609676)
XLA Ops:
  0.6 5.8 %shard_map.140 = (f32[768,128]{1,0:T(8,128)}, f32[16,5,8,128]{3,2,1,0:T(8,128)}, f32[75,16,128]{2,1,0:T(8,128)S(1)}) custom-call(f32[16,5,8,128]{3,2,1,0:T(8,128)} %bitcast.56, f32[16,25,8,128]{3,2,1,0:T(8,128)} %bitcast.48, f32[16,25,8,128]{3,2,1,0:T(8,128)} %bitcast.49, f32[16,25,8,128]{3,2,1,0:T(8,128)} %bitcast.51, f32[3200,128]{1,0:T(8,128)} %bitcast.39, ...), custom_call_target="tpu_custom_call" | custom-call | flops 7000000000 | bytes 1000 | tf_op jit(solution)/shard_map/pallas_call | solution.py:459
  6.4 8.6 %all-to-all-start = ((f32[32,24,128]{2,1,0:T(8,128)}), f32[32,24,128]{2,1,0:T(8,128)S(1)}, u32[]{:S(2)}, u32[]{:S(2)}) async-start(f32[32,24,128]{2,1,0:T(8,128)} %bitcast.47), calls=%async_computation | async-start | bytes 786432 | tf_op jit(solution)/shard_map/all_to_all | solution.py:465
  15.0 1.3 %collective-permute-start.1 = (f32[75,16,128]{2,1,0:T(8,128)S(1)}, f32[75,16,128]{2,1,0:T(8,128)S(1)}, u32[]{:S(2)}, u32[]{:S(2)}) collective-permute-start(f32[75,16,128]{2,1,0:T(8,128)S(1)} %get-tuple-element.15.mats), channel_id=1, source_target_pairs={{1,0},{2,3},{3,2},{5,4},{6,7},{7,6},{9,8},{10,11},{11,10},{13,12},... | collective-permute-start | bytes 1843208 | tf_op jit(solution)/shard_map/ppermute | solution.py:466
  16.3 9.0 %all-to-all-done.got = f32[32,24,128]{2,1,0:T(8,128)S(1)} async-done(((f32[32,24,128]{2,1,0:T(8,128)}), f32[32,24,128]{2,1,0:T(8,128)S(1)}, u32[]{:S(2)}, u32[]{:S(2)}) %all-to-all-start) | async-done | bytes 393248 | tf_op jit(solution)/shard_map/all_to_all | solution.py:465
  25.3 1.8 %shard_map.141 = f32[32,8,128]{2,1,0:T(8,128)} custom-call(f32[32,24,128]{2,1,0:T(8,128)S(1)} %all-to-all-done.got), custom_call_target="tpu_custom_call" | custom-call | flops 12000000000 | bytes 1000 | tf_op jit(solution)/shard_map/pallas_call | solution.py:467
  27.1 0.0 copy-start
  27.1 0.0 copy-start.3
  27.1 0.0 copy-start.4
  27.1 0.0 copy-start.5
  27.1 3.8 %all-to-all-start.1 = ((f32[32,8,128]{2,1,0:T(8,128)}), f32[32,8,128]{2,1,0:T(8,128)S(1)}, u32[]{:S(2)}, u32[]{:S(2)}) async-start(f32[32,8,128]{2,1,0:T(8,128)} %shard_map.141), calls=%async_computation.1 | async-start | bytes 262144 | tf_op jit(solution)/shard_map/all_to_all | solution.py:473
  31.6 0.5 collective-permute-done.1.other
  32.1 0.1 shard_map.144
  32.3 1.3 %collective-permute-start.3 = (f32[25,16,128]{2,1,0:T(8,128)S(1)}, f32[25,16,128]{2,1,0:T(8,128)S(1)}, u32[]{:S(2)}, u32[]{:S(2)}) collective-permute-start(f32[25,16,128]{2,1,0:T(8,128)S(1)} %shard_map.144), channel_id=1, source_target_pairs={{3,0},{2,1},{7,4},{6,5},{11,8},{10,9},{15,12},{14,13},{19,16},{18,... | collective-permute-start | bytes 614408 | tf_op jit(solution)/shard_map/ppermute | solution.py:472
  33.6 5.0 %all-to-all-done.1 = f32[32,8,128]{2,1,0:T(8,128)S(1)} async-done(((f32[32,8,128]{2,1,0:T(8,128)}), f32[32,8,128]{2,1,0:T(8,128)S(1)}, u32[]{:S(2)}, u32[]{:S(2)}) %all-to-all-start.1) | async-done | bytes 131104 | tf_op jit(solution)/shard_map/all_to_all | solution.py:473
  38.5 0.0 copy-done
  38.5 0.0 copy-done.3
  38.5 0.0 copy-done.4
  38.5 0.0 copy-done.5
  38.6 0.0 copy-start.1
  38.6 0.0 copy-start.2
  38.6 3.7 %shard_map.142 = (f32[8,5,16,128]{3,2,1,0:T(8,128)S(1)}, f32[10,16,128]{2,1,0:T(8,128)S(1)}, f32[128,128]{1,0:T(8,128)S(1)}, f32[128,128]{1,0:T(8,128)S(1)}, f32[3200,128]{1,0:T(8,128)S(1)}) custom-call(s32[1]{0:T(128)} %bitcast.35.count, f32[256,128]{1,0:T(8,128)S(1)} %bitcast.37, s32[1,128]{1,0:T(1,128)S(1)} %bitcast.44, s32[1,128]{1,0:T(1,128)S(1)} %bitcast.45, ...), custom_call_target="tpu_custom_call" | custom-call | flops 4000000000 | bytes 1000 | tf_op jit(solution)/shard_map/pallas_call | solution.py:474
  42.3 1.7 %collective-permute-start = (f32[10,16,128]{2,1,0:T(8,128)S(1)}, f32[10,16,128]{2,1,0:T(8,128)S(1)}, u32[]{:S(2)}, u32[]{:S(2)}) collective-permute-start(f32[10,16,128]{2,1,0:T(8,128)S(1)} %get-tuple-element.14.vec), channel_id=1, source_target_pairs={{0,1},{1,0},{2,3},{3,2},{4,5},{5,4},{6,7},{7,6},{8,9},{9,8},{10,11... | collective-permute-start | bytes 245768 | tf_op jit(solution)/shard_map/ppermute | solution.py:481
  44.0 2.4 %collective-permute-done.near = f32[10,16,128]{2,1,0:T(8,128)S(1)} collective-permute-done((f32[10,16,128]{2,1,0:T(8,128)S(1)}, f32[10,16,128]{2,1,0:T(8,128)S(1)}, u32[]{:S(2)}, u32[]{:S(2)}) %collective-permute-start) | collective-permute-done | bytes 81952 | tf_op jit(solution)/shard_map/ppermute | solution.py:481
  46.4 0.1 shard_map.143
  46.5 3.5 %collective-permute-start.2 = (f32[5,16,128]{2,1,0:T(8,128)S(1)}, f32[5,16,128]{2,1,0:T(8,128)S(1)}, u32[]{:S(2)}, u32[]{:S(2)}) collective-permute-start(f32[5,16,128]{2,1,0:T(8,128)S(1)} %shard_map.143), channel_id=1, source_target_pairs={{0,3},{1,2},{2,1},{3,0},{4,7},{5,6},{6,5},{7,4},{8,11},{9,10},{10,... | collective-permute-start | bytes 122888 | tf_op jit(solution)/shard_map/ppermute | solution.py:483
  49.9 1.4 %collective-permute-done.2.beyond = f32[5,16,128]{2,1,0:T(8,128)S(1)} collective-permute-done((f32[5,16,128]{2,1,0:T(8,128)S(1)}, f32[5,16,128]{2,1,0:T(8,128)S(1)}, u32[]{:S(2)}, u32[]{:S(2)}) %collective-permute-start.2) | collective-permute-done | bytes 40992 | tf_op jit(solution)/shard_map/ppermute | solution.py:483
  51.3 0.0 collective-permute-done.3.far
  51.3 0.0 copy-done.1
  51.3 0.0 copy-done.2
  51.3 1.7 %shard_map.145 = (f32[16,5,8,128]{3,2,1,0:T(8,128)}, f32[128,128]{1,0:T(8,128)S(1)}) custom-call(s32[1]{0:T(128)} %bitcast.z_ref, f32[10,16,128]{2,1,0:T(8,128)S(1)} %get-tuple-element.14.vec, f32[10,16,128]{2,1,0:T(8,128)S(1)} %collective-permute-done.near, f32[5,16,128]{2,1,0:T(8,128)S(1)} %collective-permute-done.2.beyond, ...), custom_call_target="tpu_custom_call" | custom-call | flops 2000000000 | bytes 1000 | tf_op jit(solution)/shard_map/pallas_call | solution.py:484
  53.0 17.0 %all_to_all.21 = f32[128,1,128]{2,1,0:T(1,128)S(1)} all-to-all(f32[128,1,128]{2,1,0:T(1,128)S(1)} %bitcast.38), channel_id=1, replica_groups=mesh['stream'=32,'span'=4] {'stream','span'}, dimensions={0} | all-to-all | bytes 131072 | tf_op jit(solution)/shard_map/all_to_all | solution.py:490
  70.0 0.7 %shard_map.146 = f32[3,16]{1,0:T(4,128)} custom-call(f32[128,128]{1,0:T(8,128)S(1)} %bitcast.36), custom_call_target="tpu_custom_call" | custom-call | bytes 1000 | tf_op jit(solution)/shard_map/pallas_call | solution.py:491
Async XLA Ops:
  6.4 18.9 %all-to-all-start = ((f32[32,24,128]{2,1,0:T(8,128)}), f32[32,24,128]{2,1,0:T(8,128)S(1)}, u32[]{:S(2)}, u32[]{:S(2)}) async-start(f32[32,24,128]{2,1,0:T(8,128)} %bitcast.47), calls=%async_computation | async-start | bytes 786432 | tf_op jit(solution)/shard_map/all_to_all | solution.py:465
  15.0 17.1 %collective-permute-start.1 = (f32[75,16,128]{2,1,0:T(8,128)S(1)}, f32[75,16,128]{2,1,0:T(8,128)S(1)}, u32[]{:S(2)}, u32[]{:S(2)}) collective-permute-start(f32[75,16,128]{2,1,0:T(8,128)S(1)} %get-tuple-element.15.mats), channel_id=1, source_target_pairs={{1,0},{2,3},{3,2},{5,4},{6,7},{7,6},{9,8},{10,11},{11,10},{13,12},... | collective-permute-start | bytes 1843208 | tf_op jit(solution)/shard_map/ppermute | solution.py:466
  27.1 11.4 %copy-start = (f32[16,8,5,5,128]{4,1,3,2,0:T(8,128)S(1)}, f32[16,8,5,5,128]{4,1,3,2,0:T(8,128)}, u32[]{:S(2)}) copy-start(f32[16,8,5,5,128]{4,1,3,2,0:T(8,128)} %param.19) | copy-start | bytes 4915204
  27.1 11.4 %copy-start.3 = (s32[1,1,128]{2,1,0:T(1,128)S(1)}, s32[1,1,128]{2,1,0:T(1,128)}, u32[]{:S(2)}) copy-start(s32[1,1,128]{2,1,0:T(1,128)} %param.22) | copy-start | bytes 1540
  27.1 11.4 %copy-start.4 = (s32[1,1,128]{2,1,0:T(1,128)S(1)}, s32[1,1,128]{2,1,0:T(1,128)}, u32[]{:S(2)}) copy-start(s32[1,1,128]{2,1,0:T(1,128)} %param.23) | copy-start | bytes 1540
  27.1 11.4 %copy-start.5 = (f32[1,1,128]{2,1,0:T(1,128)S(1)}, f32[1,1,128]{2,1,0:T(1,128)}, u32[]{:S(2)}) copy-start(f32[1,1,128]{2,1,0:T(1,128)} %param.24) | copy-start | bytes 1540
  27.1 11.4 %all-to-all-start.1 = ((f32[32,8,128]{2,1,0:T(8,128)}), f32[32,8,128]{2,1,0:T(8,128)S(1)}, u32[]{:S(2)}, u32[]{:S(2)}) async-start(f32[32,8,128]{2,1,0:T(8,128)} %shard_map.141), calls=%async_computation.1 | async-start | bytes 262144 | tf_op jit(solution)/shard_map/all_to_all | solution.py:473
  32.3 19.1 %collective-permute-start.3 = (f32[25,16,128]{2,1,0:T(8,128)S(1)}, f32[25,16,128]{2,1,0:T(8,128)S(1)}, u32[]{:S(2)}, u32[]{:S(2)}) collective-permute-start(f32[25,16,128]{2,1,0:T(8,128)S(1)} %shard_map.144), channel_id=1, source_target_pairs={{3,0},{2,1},{7,4},{6,5},{11,8},{10,9},{15,12},{14,13},{19,16},{18,... | collective-permute-start | bytes 614408 | tf_op jit(solution)/shard_map/ppermute | solution.py:472
  38.6 12.8 %copy-start.1 = (bf16[16,8,3,5,128]{4,1,3,2,0:T(8,128)(2,1)S(1)}, bf16[16,8,3,5,128]{4,1,3,2,0:T(8,128)(2,1)}, u32[]{:S(2)}) copy-start(bf16[16,8,3,5,128]{4,1,3,2,0:T(8,128)(2,1)} %param.21) | copy-start | bytes 1474564
  38.6 12.7 %copy-start.2 = (f32[16,8,5,128]{3,1,2,0:T(8,128)S(1)}, f32[16,8,5,128]{3,1,2,0:T(8,128)}, u32[]{:S(2)}) copy-start(f32[16,8,5,128]{3,1,2,0:T(8,128)} %param.14) | copy-start | bytes 983044
  42.3 4.1 %collective-permute-start = (f32[10,16,128]{2,1,0:T(8,128)S(1)}, f32[10,16,128]{2,1,0:T(8,128)S(1)}, u32[]{:S(2)}, u32[]{:S(2)}) collective-permute-start(f32[10,16,128]{2,1,0:T(8,128)S(1)} %get-tuple-element.14.vec), channel_id=1, source_target_pairs={{0,1},{1,0},{2,3},{3,2},{4,5},{5,4},{6,7},{7,6},{8,9},{9,8},{10,11... | collective-permute-start | bytes 245768 | tf_op jit(solution)/shard_map/ppermute | solution.py:481
  46.5 4.8 %collective-permute-start.2 = (f32[5,16,128]{2,1,0:T(8,128)S(1)}, f32[5,16,128]{2,1,0:T(8,128)S(1)}, u32[]{:S(2)}, u32[]{:S(2)}) collective-permute-start(f32[5,16,128]{2,1,0:T(8,128)S(1)} %shard_map.143), channel_id=1, source_target_pairs={{0,3},{1,2},{2,1},{3,0},{4,7},{5,6},{6,5},{7,4},{8,11},{9,10},{10,... | collective-permute-start | bytes 122888 | tf_op jit(solution)/shard_map/ppermute | solution.py:483

commit v5 on v4

--- a/solution.py
+++ b/solution.py
@@ -165,7 +165,7 @@
     kept.wait()
 
 
-def solve_kernel(got, out, un, fin, sin):
+def solve_kernel(got, out, un, qs):
     un[0] = got[...]
     for q in range(1, 4):
         for p in range(XS):
@@ -174,27 +174,33 @@
     def val(p, k):
         return un[k % 4, p, (k // 4) : (k // 4) + 1, :]
 
+    def keep(p, first, v):
+        for j in range(5):
+            k = first + j
+            qs[k % 4, p, (k // 4) : (k // 4) + 1, :] = v[j]
+
     zero = [jnp.zeros((1, NN), jnp.float32)] * 5
 
     def fore(p, f):
-        for j in range(5):
-            fin[p, j : j + 1, :] = f[j]
+        keep(p, 0, f)
         return add(act([val(p, k) for k in range(25)], f), [val(p, 25 + j) for j in range(5)])
 
     lax.fori_loop(0, XS, fore, zero, unroll=16)
 
     def back(k, s):
         p = XS - 1 - k
-        for j in range(5):
-            sin[p, j : j + 1, :] = s[j]
-        f = [fin[p, j : j + 1, :] for j in range(5)]
+        keep(p, 5, s)
+        f = [qs[j % 4, p, (j // 4) : (j // 4) + 1, :] for j in range(5)]
         known = add(act([val(p, 60 + k) for k in range(25)], f), [val(p, 55 + j) for j in range(5)])
         return add(known, act([val(p, 30 + k) for k in range(25)], s))
 
     lax.fori_loop(0, XS, back, zero, unroll=16)
     quarter = lanes_quarter((8, NN))
     for p in range(XS):
-        out[p] = jnp.where(quarter == 0, fin[p], pltpu.roll(sin[p], 32, 1))
+        t = qs[0, p]
+        for q in range(1, 4):
+            t = jnp.where(quarter == q, pltpu.roll(qs[q, p], 32 * q, 1), t)
+        out[p] = t[:4]
 
 
 def replay_kernel(count, got, cell, owner, weight, ly, driven_h, lx_h, ux_h, dy_h, uy_h, dturn, vec, target,
@@ -220,11 +226,11 @@
 
     quarter = lanes_quarter((SY, NN))
 
-    def entering(j, at):
+    def entering(k):
         out = None
         for nq in range(4):
-            part = got[pl.ds(nq * 64 + j, 8, 8), :]
-            shift = (32 * nq - 32 * at) % 128
+            part = got[pl.ds(nq * 32 + k // 4, 8, 4), :]
+            shift = (32 * nq - 32 * (k % 4)) % 128
             part = part if shift == 0 else pltpu.roll(part, shift, 1)
             out = part if out is None else jnp.where(quarter == nq, part, out)
         return out
@@ -235,7 +241,7 @@
             fs[i, a] = f[a]
         return f
 
-    f = [entering(j, 0) for j in range(5)]
+    f = [entering(j) for j in range(5)]
     flight[0].wait()
     for k in range(2):
         flight[1 + k].wait()
@@ -249,7 +255,7 @@
             sd[pl.ds(pl.multiple_of((i * 5 + a) * 8, 8), 8), :] = d[a]
         return s
 
-    s = [entering(j, 1) for j in range(5)]
+    s = [entering(5 + j) for j in range(5)]
     for k in range(2):
         flight[3 + 2 * k].wait()
         flight[4 + 2 * k].wait()
@@ -465,8 +471,8 @@
     got = lax.all_to_all(msg.reshape(XS, ROWS, NN), "stream", 0, 0, tiled=True)
     other = lax.ppermute(mats, "span", [(1, 0), (2, 3), (3, 2)])
     (back,) = call(
-        solve_kernel, [(XS, 8, NN)],
-        [(4, XS, ROWS, NN), (XS, 8, NN), (XS, 8, NN)], vmem=1, cost=12,
+        solve_kernel, [(XS, 4, NN)],
+        [(4, XS, ROWS, NN), (4, XS, 8, NN)], vmem=1, cost=12,
     )(got)
     (pair,) = call(pair_kernel, [(25, SX, NN)], [], smem=1, vmem=2, cost=0.2)(z, mats, other)
     far = lax.ppermute(pair, "span", [(3, 0), (2, 1)])
@@ -476,7 +482,7 @@
         [(SY, 5, SX, NN), (10, SX, NN), (128, 128), (128, 128), uy.shape],
         [cells, tile, tile, tile, cells, (SX * 5 * SY, NN), (SY, 5, 8, NN)],
         smem=1, vmem=5, hbm=5, sems=(8,), cost=4,
-    )(node_count.reshape(1), back.reshape(XS * 8, NN), node_cell.reshape(1, -1), node_owner.reshape(1, -1),
+    )(node_count.reshape(1), back.reshape(XS * 4, NN), node_cell.reshape(1, -1), node_owner.reshape(1, -1),
       node_weight.reshape(1, -1), ly, in_hbm(driven), in_hbm(lx), in_hbm(ux), in_hbm(dy), in_hbm(uy))
     near = lax.ppermute(vec, "span", [(i, i ^ 1) for i in range(4)])
     (joint,) = call(join_kernel, [(5, SX, NN)], [], smem=1, vmem=4, cost=0.1)(z, vec, near, mats, other)

time: 71.1 us -> 70.6 us (level)
  no operation moved by 1% of the time
where the time goes in v5:
time: 70.6 us; the launch traced here: 70.3 us
  starting transfers between devices  20.1 us (28%)
  waiting for transfers between devices  17.8 us (25%)
  blocking collectives  17 us (24%)
  Pallas kernels  13.9 us (20%)
  between operations  1.42 us (2%)
    all_to_all x1, blocking collectives, shards(): parts = lax.all_to_all(part, ('stream', 'span'), 0, 0, tiled=True)  17 us
    all_to_all x1, waiting for transfers between devices, shards(): got = lax.all_to_all(msg.reshape(XS, ROWS, NN), 'stream', 0, 0, tiled=True)  8.82 us
    all_to_all x1, starting transfers between devices, shards(): got = lax.all_to_all(msg.reshape(XS, ROWS, NN), 'stream', 0, 0, tiled=True)  8.6 us
    pallas_call x1, Pallas kernels, shards(): call(maps_kernel, [list(msg_shape), list(cells), (75, SX, NN)], [tile, ti...  5.75 us
    all_to_all x1, waiting for transfers between devices, shards(): back = lax.all_to_all(back, 'stream', 0, 0, tiled=True)  4.32 us
    pallas_call x1, Pallas kernels, shards(): call(replay_kernel, [(SY, 5, SX, NN), (10, SX, NN), (128, 128), (128, 128...  3.72 us
    all_to_all x1, starting transfers between devices, shards(): back = lax.all_to_all(back, 'stream', 0, 0, tiled=True)  3.64 us
    ppermute x1, starting transfers between devices, shards(): beyond = lax.ppermute(joint, 'span', [(i, 3 - i) for i in range(4)])  3.45 us
  transfers between devices with their start and end apart: 6, of which 5 were waited for; matrix products, arithmetic and copies ran while one was open for 0% of the time, Pallas kernels for 8%

profile of v5, /device:TPU:1, one launch (start us, length us, event | category | flops | bytes accessed | tf_op | source)
XLA Modules:
  0.0 70.3 jit_solution(15868958492090063358)
XLA Ops:
  0.6 5.8 %shard_map.140 = (f32[768,128]{1,0:T(8,128)}, f32[16,5,8,128]{3,2,1,0:T(8,128)}, f32[75,16,128]{2,1,0:T(8,128)S(1)}) custom-call(f32[16,5,8,128]{3,2,1,0:T(8,128)} %bitcast.56, f32[16,25,8,128]{3,2,1,0:T(8,128)} %bitcast.48, f32[16,25,8,128]{3,2,1,0:T(8,128)} %bitcast.49, f32[16,25,8,128]{3,2,1,0:T(8,128)} %bitcast.51, f32[3200,128]{1,0:T(8,128)} %bitcast.39, ...), custom_call_target="tpu_custom_call" | custom-call | flops 7000000000 | bytes 1000 | tf_op jit(solution)/shard_map/pallas_call | solution.py:465
  6.4 8.6 %all-to-all-start = ((f32[32,24,128]{2,1,0:T(8,128)}), f32[32,24,128]{2,1,0:T(8,128)S(1)}, u32[]{:S(2)}, u32[]{:S(2)}) async-start(f32[32,24,128]{2,1,0:T(8,128)} %bitcast.47), calls=%async_computation | async-start | bytes 786432 | tf_op jit(solution)/shard_map/all_to_all | solution.py:471
  15.0 0.0 copy-start
  15.0 0.0 copy-start.3
  15.0 0.0 copy-start.4
  15.0 0.0 copy-start.5
  15.0 1.4 %collective-permute-start.1 = (f32[75,16,128]{2,1,0:T(8,128)S(1)}, f32[75,16,128]{2,1,0:T(8,128)S(1)}, u32[]{:S(2)}, u32[]{:S(2)}) collective-permute-start(f32[75,16,128]{2,1,0:T(8,128)S(1)} %get-tuple-element.15.mats), channel_id=1, source_target_pairs={{1,0},{2,3},{3,2},{5,4},{6,7},{7,6},{9,8},{10,11},{11,10},{13,12},... | collective-permute-start | bytes 1843208 | tf_op jit(solution)/shard_map/ppermute | solution.py:472
  16.5 8.8 %all-to-all-done.got = f32[32,24,128]{2,1,0:T(8,128)S(1)} async-done(((f32[32,24,128]{2,1,0:T(8,128)}), f32[32,24,128]{2,1,0:T(8,128)S(1)}, u32[]{:S(2)}, u32[]{:S(2)}) %all-to-all-start) | async-done | bytes 393248 | tf_op jit(solution)/shard_map/all_to_all | solution.py:471
  25.3 1.8 %shard_map.141 = f32[32,4,128]{2,1,0:T(4,128)} custom-call(f32[32,24,128]{2,1,0:T(8,128)S(1)} %all-to-all-done.got), custom_call_target="tpu_custom_call" | custom-call | flops 12000000000 | bytes 1000 | tf_op jit(solution)/shard_map/pallas_call | solution.py:473
  27.1 3.6 %all-to-all-start.1 = ((f32[32,4,128]{2,1,0:T(4,128)}), f32[32,4,128]{2,1,0:T(4,128)S(1)}, u32[]{:S(2)}, u32[]{:S(2)}) async-start(f32[32,4,128]{2,1,0:T(4,128)} %shard_map.141), calls=%async_computation.1 | async-start | bytes 131072 | tf_op jit(solution)/shard_map/all_to_all | solution.py:479
  31.5 0.8 %collective-permute-done.1.other = f32[75,16,128]{2,1,0:T(8,128)S(1)} collective-permute-done((f32[75,16,128]{2,1,0:T(8,128)S(1)}, f32[75,16,128]{2,1,0:T(8,128)S(1)}, u32[]{:S(2)}, u32[]{:S(2)}) %collective-permute-start.1) | collective-permute-done | bytes 614432 | tf_op jit(solution)/shard_map/ppermute | solution.py:472
  32.3 0.1 shard_map.144
  32.4 1.3 %collective-permute-start.3 = (f32[25,16,128]{2,1,0:T(8,128)S(1)}, f32[25,16,128]{2,1,0:T(8,128)S(1)}, u32[]{:S(2)}, u32[]{:S(2)}) collective-permute-start(f32[25,16,128]{2,1,0:T(8,128)S(1)} %shard_map.144), channel_id=1, source_target_pairs={{3,0},{2,1},{7,4},{6,5},{11,8},{10,9},{15,12},{14,13},{19,16},{18,... | collective-permute-start | bytes 614408 | tf_op jit(solution)/shard_map/ppermute | solution.py:478
  33.7 4.3 %all-to-all-done.1 = f32[32,4,128]{2,1,0:T(4,128)S(1)} async-done(((f32[32,4,128]{2,1,0:T(4,128)}), f32[32,4,128]{2,1,0:T(4,128)S(1)}, u32[]{:S(2)}, u32[]{:S(2)}) %all-to-all-start.1) | async-done | bytes 65568 | tf_op jit(solution)/shard_map/all_to_all | solution.py:479
  38.1 0.0 copy-done
  38.1 0.0 copy-done.3
  38.1 0.0 copy-done.4
  38.1 0.0 copy-done.5
  38.1 0.0 copy-start.1
  38.1 0.0 copy-start.2
  38.1 3.7 %shard_map.142 = (f32[8,5,16,128]{3,2,1,0:T(8,128)S(1)}, f32[10,16,128]{2,1,0:T(8,128)S(1)}, f32[128,128]{1,0:T(8,128)S(1)}, f32[128,128]{1,0:T(8,128)S(1)}, f32[3200,128]{1,0:T(8,128)S(1)}) custom-call(s32[1]{0:T(128)} %bitcast.35.count, f32[128,128]{1,0:T(8,128)S(1)} %bitcast.37, s32[1,128]{1,0:T(1,128)S(1)} %bitcast.44, s32[1,128]{1,0:T(1,128)S(1)} %bitcast.45, ...), custom_call_target="tpu_custom_call" | custom-call | flops 4000000000 | bytes 1000 | tf_op jit(solution)/shard_map/pallas_call | solution.py:480
  41.8 1.7 %collective-permute-start = (f32[10,16,128]{2,1,0:T(8,128)S(1)}, f32[10,16,128]{2,1,0:T(8,128)S(1)}, u32[]{:S(2)}, u32[]{:S(2)}) collective-permute-start(f32[10,16,128]{2,1,0:T(8,128)S(1)} %get-tuple-element.14.vec), channel_id=1, source_target_pairs={{0,1},{1,0},{2,3},{3,2},{4,5},{5,4},{6,7},{7,6},{8,9},{9,8},{10,11... | collective-permute-start | bytes 245768 | tf_op jit(solution)/shard_map/ppermute | solution.py:487
  43.6 2.4 %collective-permute-done.near = f32[10,16,128]{2,1,0:T(8,128)S(1)} collective-permute-done((f32[10,16,128]{2,1,0:T(8,128)S(1)}, f32[10,16,128]{2,1,0:T(8,128)S(1)}, u32[]{:S(2)}, u32[]{:S(2)}) %collective-permute-start) | collective-permute-done | bytes 81952 | tf_op jit(solution)/shard_map/ppermute | solution.py:487
  45.9 0.1 shard_map.143
  46.0 3.5 %collective-permute-start.2 = (f32[5,16,128]{2,1,0:T(8,128)S(1)}, f32[5,16,128]{2,1,0:T(8,128)S(1)}, u32[]{:S(2)}, u32[]{:S(2)}) collective-permute-start(f32[5,16,128]{2,1,0:T(8,128)S(1)} %shard_map.143), channel_id=1, source_target_pairs={{0,3},{1,2},{2,1},{3,0},{4,7},{5,6},{6,5},{7,4},{8,11},{9,10},{10,... | collective-permute-start | bytes 122888 | tf_op jit(solution)/shard_map/ppermute | solution.py:489
  49.4 1.4 %collective-permute-done.2.beyond = f32[5,16,128]{2,1,0:T(8,128)S(1)} collective-permute-done((f32[5,16,128]{2,1,0:T(8,128)S(1)}, f32[5,16,128]{2,1,0:T(8,128)S(1)}, u32[]{:S(2)}, u32[]{:S(2)}) %collective-permute-start.2) | collective-permute-done | bytes 40992 | tf_op jit(solution)/shard_map/ppermute | solution.py:489
  50.8 0.0 collective-permute-done.3.far
  50.8 0.0 copy-done.1
  50.8 0.0 copy-done.2
  50.8 1.7 %shard_map.145 = (f32[16,5,8,128]{3,2,1,0:T(8,128)}, f32[128,128]{1,0:T(8,128)S(1)}) custom-call(s32[1]{0:T(128)} %bitcast.z_ref, f32[10,16,128]{2,1,0:T(8,128)S(1)} %get-tuple-element.14.vec, f32[10,16,128]{2,1,0:T(8,128)S(1)} %collective-permute-done.near, f32[5,16,128]{2,1,0:T(8,128)S(1)} %collective-permute-done.2.beyond, ...), custom_call_target="tpu_custom_call" | custom-call | flops 2000000000 | bytes 1000 | tf_op jit(solution)/shard_map/pallas_call | solution.py:490
  52.5 17.0 %all_to_all.21 = f32[128,1,128]{2,1,0:T(1,128)S(1)} all-to-all(f32[128,1,128]{2,1,0:T(1,128)S(1)} %bitcast.38), channel_id=1, replica_groups=mesh['stream'=32,'span'=4] {'stream','span'}, dimensions={0} | all-to-all | bytes 131072 | tf_op jit(solution)/shard_map/all_to_all | solution.py:496
  69.5 0.7 %shard_map.146 = f32[3,16]{1,0:T(4,128)} custom-call(f32[128,128]{1,0:T(8,128)S(1)} %bitcast.36), custom_call_target="tpu_custom_call" | custom-call | bytes 1000 | tf_op jit(solution)/shard_map/pallas_call | solution.py:497
Async XLA Ops:
  6.4 18.9 %all-to-all-start = ((f32[32,24,128]{2,1,0:T(8,128)}), f32[32,24,128]{2,1,0:T(8,128)S(1)}, u32[]{:S(2)}, u32[]{:S(2)}) async-start(f32[32,24,128]{2,1,0:T(8,128)} %bitcast.47), calls=%async_computation | async-start | bytes 786432 | tf_op jit(solution)/shard_map/all_to_all | solution.py:471
  15.0 23.1 %copy-start = (f32[16,8,5,5,128]{4,1,3,2,0:T(8,128)S(1)}, f32[16,8,5,5,128]{4,1,3,2,0:T(8,128)}, u32[]{:S(2)}) copy-start(f32[16,8,5,5,128]{4,1,3,2,0:T(8,128)} %param.19) | copy-start | bytes 4915204
  15.0 23.1 %copy-start.3 = (s32[1,1,128]{2,1,0:T(1,128)S(1)}, s32[1,1,128]{2,1,0:T(1,128)}, u32[]{:S(2)}) copy-start(s32[1,1,128]{2,1,0:T(1,128)} %param.22) | copy-start | bytes 1540
  15.0 23.1 %copy-start.4 = (s32[1,1,128]{2,1,0:T(1,128)S(1)}, s32[1,1,128]{2,1,0:T(1,128)}, u32[]{:S(2)}) copy-start(s32[1,1,128]{2,1,0:T(1,128)} %param.23) | copy-start | bytes 1540
  15.0 23.0 %copy-start.5 = (f32[1,1,128]{2,1,0:T(1,128)S(1)}, f32[1,1,128]{2,1,0:T(1,128)}, u32[]{:S(2)}) copy-start(f32[1,1,128]{2,1,0:T(1,128)} %param.24) | copy-start | bytes 1540
  15.0 17.2 %collective-permute-start.1 = (f32[75,16,128]{2,1,0:T(8,128)S(1)}, f32[75,16,128]{2,1,0:T(8,128)S(1)}, u32[]{:S(2)}, u32[]{:S(2)}) collective-permute-start(f32[75,16,128]{2,1,0:T(8,128)S(1)} %get-tuple-element.15.mats), channel_id=1, source_target_pairs={{1,0},{2,3},{3,2},{5,4},{6,7},{7,6},{9,8},{10,11},{11,10},{13,12},... | collective-permute-start | bytes 1843208 | tf_op jit(solution)/shard_map/ppermute | solution.py:472
  27.1 10.9 %all-to-all-start.1 = ((f32[32,4,128]{2,1,0:T(4,128)}), f32[32,4,128]{2,1,0:T(4,128)S(1)}, u32[]{:S(2)}, u32[]{:S(2)}) async-start(f32[32,4,128]{2,1,0:T(4,128)} %shard_map.141), calls=%async_computation.1 | async-start | bytes 131072 | tf_op jit(solution)/shard_map/all_to_all | solution.py:479
  32.4 18.4 %collective-permute-start.3 = (f32[25,16,128]{2,1,0:T(8,128)S(1)}, f32[25,16,128]{2,1,0:T(8,128)S(1)}, u32[]{:S(2)}, u32[]{:S(2)}) collective-permute-start(f32[25,16,128]{2,1,0:T(8,128)S(1)} %shard_map.144), channel_id=1, source_target_pairs={{3,0},{2,1},{7,4},{6,5},{11,8},{10,9},{15,12},{14,13},{19,16},{18,... | collective-permute-start | bytes 614408 | tf_op jit(solution)/shard_map/ppermute | solution.py:478
  38.1 12.8 %copy-start.1 = (bf16[16,8,3,5,128]{4,1,3,2,0:T(8,128)(2,1)S(1)}, bf16[16,8,3,5,128]{4,1,3,2,0:T(8,128)(2,1)}, u32[]{:S(2)}) copy-start(bf16[16,8,3,5,128]{4,1,3,2,0:T(8,128)(2,1)} %param.21) | copy-start | bytes 1474564
  38.1 12.7 %copy-start.2 = (f32[16,8,5,128]{3,1,2,0:T(8,128)S(1)}, f32[16,8,5,128]{3,1,2,0:T(8,128)}, u32[]{:S(2)}) copy-start(f32[16,8,5,128]{3,1,2,0:T(8,128)} %param.14) | copy-start | bytes 983044
  41.8 4.1 %collective-permute-start = (f32[10,16,128]{2,1,0:T(8,128)S(1)}, f32[10,16,128]{2,1,0:T(8,128)S(1)}, u32[]{:S(2)}, u32[]{:S(2)}) collective-permute-start(f32[10,16,128]{2,1,0:T(8,128)S(1)} %get-tuple-element.14.vec), channel_id=1, source_target_pairs={{0,1},{1,0},{2,3},{3,2},{4,5},{5,4},{6,7},{7,6},{8,9},{9,8},{10,11... | collective-permute-start | bytes 245768 | tf_op jit(solution)/shard_map/ppermute | solution.py:487
  46.0 4.8 %collective-permute-start.2 = (f32[5,16,128]{2,1,0:T(8,128)S(1)}, f32[5,16,128]{2,1,0:T(8,128)S(1)}, u32[]{:S(2)}, u32[]{:S(2)}) collective-permute-start(f32[5,16,128]{2,1,0:T(8,128)S(1)} %shard_map.143), channel_id=1, source_target_pairs={{0,3},{1,2},{2,1},{3,0},{4,7},{5,6},{6,5},{7,4},{8,11},{9,10},{10,... | collective-permute-start | bytes 122888 | tf_op jit(solution)/shard_map/ppermute | solution.py:489

commit v6 on v5

--- a/solution.py
+++ b/solution.py
@@ -185,7 +185,7 @@
         keep(p, 0, f)
         return add(act([val(p, k) for k in range(25)], f), [val(p, 25 + j) for j in range(5)])
 
-    lax.fori_loop(0, XS, fore, zero, unroll=16)
+    lax.fori_loop(0, XS, fore, zero, unroll=True)
 
     def back(k, s):
         p = XS - 1 - k
@@ -194,7 +194,7 @@
         known = add(act([val(p, 60 + k) for k in range(25)], f), [val(p, 55 + j) for j in range(5)])
         return add(known, act([val(p, 30 + k) for k in range(25)], s))
 
-    lax.fori_loop(0, XS, back, zero, unroll=16)
+    lax.fori_loop(0, XS, back, zero, unroll=True)
     quarter = lanes_quarter((8, NN))
     for p in range(XS):
         t = qs[0, p]

time: 70.6 us -> 70.6 us (level)
  no operation moved by 1% of the time
where the time goes in v6:
time: 70.6 us; the launch traced here: 70.3 us
  starting transfers between devices  20.1 us (28%)
  waiting for transfers between devices  17.8 us (25%)
  blocking collectives  17.4 us (25%)
  Pallas kernels  13.6 us (19%)
  between operations  1.42 us (2%)
    all_to_all x1, blocking collectives, shards(): parts = lax.all_to_all(part, ('stream', 'span'), 0, 0, tiled=True)  17.4 us
    all_to_all x1, waiting for transfers between devices, shards(): got = lax.all_to_all(msg.reshape(XS, ROWS, NN), 'stream', 0, 0, tiled=True)  8.82 us
    all_to_all x1, starting transfers between devices, shards(): got = lax.all_to_all(msg.reshape(XS, ROWS, NN), 'stream', 0, 0, tiled=True)  8.6 us
    pallas_call x1, Pallas kernels, shards(): call(maps_kernel, [list(msg_shape), list(cells), (75, SX, NN)], [tile, ti...  5.75 us
    all_to_all x1, waiting for transfers between devices, shards(): back = lax.all_to_all(back, 'stream', 0, 0, tiled=True)  3.97 us
    pallas_call x1, Pallas kernels, shards(): call(replay_kernel, [(SY, 5, SX, NN), (10, SX, NN), (128, 128), (128, 128...  3.72 us
    all_to_all x1, starting transfers between devices, shards(): back = lax.all_to_all(back, 'stream', 0, 0, tiled=True)  3.64 us
    ppermute x1, starting transfers between devices, shards(): beyond = lax.ppermute(joint, 'span', [(i, 3 - i) for i in range(4)])  3.45 us
  transfers between devices with their start and end apart: 6, of which 5 were waited for; matrix products, arithmetic and copies ran while one was open for 0% of the time, Pallas kernels for 8%

profile of v6, /device:TPU:1, one launch (start us, length us, event | category | flops | bytes accessed | tf_op | source)
XLA Modules:
  0.0 70.3 jit_solution(1199396860295205557)
XLA Ops:
  0.6 5.8 %shard_map.140 = (f32[768,128]{1,0:T(8,128)}, f32[16,5,8,128]{3,2,1,0:T(8,128)}, f32[75,16,128]{2,1,0:T(8,128)S(1)}) custom-call(f32[16,5,8,128]{3,2,1,0:T(8,128)} %bitcast.56, f32[16,25,8,128]{3,2,1,0:T(8,128)} %bitcast.48, f32[16,25,8,128]{3,2,1,0:T(8,128)} %bitcast.49, f32[16,25,8,128]{3,2,1,0:T(8,128)} %bitcast.51, f32[3200,128]{1,0:T(8,128)} %bitcast.39, ...), custom_call_target="tpu_custom_call" | custom-call | flops 7000000000 | bytes 1000 | tf_op jit(solution)/shard_map/pallas_call | solution.py:465
  6.4 8.6 %all-to-all-start = ((f32[32,24,128]{2,1,0:T(8,128)}), f32[32,24,128]{2,1,0:T(8,128)S(1)}, u32[]{:S(2)}, u32[]{:S(2)}) async-start(f32[32,24,128]{2,1,0:T(8,128)} %bitcast.47), calls=%async_computation | async-start | bytes 786432 | tf_op jit(solution)/shard_map/all_to_all | solution.py:471
  15.0 0.0 copy-start
  15.0 0.0 copy-start.3
  15.0 0.0 copy-start.4
  15.0 0.0 copy-start.5
  15.0 1.4 %collective-permute-start.1 = (f32[75,16,128]{2,1,0:T(8,128)S(1)}, f32[75,16,128]{2,1,0:T(8,128)S(1)}, u32[]{:S(2)}, u32[]{:S(2)}) collective-permute-start(f32[75,16,128]{2,1,0:T(8,128)S(1)} %get-tuple-element.15.mats), channel_id=1, source_target_pairs={{1,0},{2,3},{3,2},{5,4},{6,7},{7,6},{9,8},{10,11},{11,10},{13,12},... | collective-permute-start | bytes 1843208 | tf_op jit(solution)/shard_map/ppermute | solution.py:472
  16.5 8.8 %all-to-all-done.got = f32[32,24,128]{2,1,0:T(8,128)S(1)} async-done(((f32[32,24,128]{2,1,0:T(8,128)}), f32[32,24,128]{2,1,0:T(8,128)S(1)}, u32[]{:S(2)}, u32[]{:S(2)}) %all-to-all-start) | async-done | bytes 393248 | tf_op jit(solution)/shard_map/all_to_all | solution.py:471
  25.3 1.5 %shard_map.141 = f32[32,4,128]{2,1,0:T(4,128)} custom-call(f32[32,24,128]{2,1,0:T(8,128)S(1)} %all-to-all-done.got), custom_call_target="tpu_custom_call" | custom-call | flops 12000000000 | bytes 1000 | tf_op jit(solution)/shard_map/pallas_call | solution.py:473
  26.8 3.6 %all-to-all-start.1 = ((f32[32,4,128]{2,1,0:T(4,128)}), f32[32,4,128]{2,1,0:T(4,128)S(1)}, u32[]{:S(2)}, u32[]{:S(2)}) async-start(f32[32,4,128]{2,1,0:T(4,128)} %shard_map.141), calls=%async_computation.1 | async-start | bytes 131072 | tf_op jit(solution)/shard_map/all_to_all | solution.py:479
  31.1 1.2 %collective-permute-done.1.other = f32[75,16,128]{2,1,0:T(8,128)S(1)} collective-permute-done((f32[75,16,128]{2,1,0:T(8,128)S(1)}, f32[75,16,128]{2,1,0:T(8,128)S(1)}, u32[]{:S(2)}, u32[]{:S(2)}) %collective-permute-start.1) | collective-permute-done | bytes 614432 | tf_op jit(solution)/shard_map/ppermute | solution.py:472
  32.3 0.1 shard_map.144
  32.4 1.3 %collective-permute-start.3 = (f32[25,16,128]{2,1,0:T(8,128)S(1)}, f32[25,16,128]{2,1,0:T(8,128)S(1)}, u32[]{:S(2)}, u32[]{:S(2)}) collective-permute-start(f32[25,16,128]{2,1,0:T(8,128)S(1)} %shard_map.144), channel_id=1, source_target_pairs={{3,0},{2,1},{7,4},{6,5},{11,8},{10,9},{15,12},{14,13},{19,16},{18,... | collective-permute-start | bytes 614408 | tf_op jit(solution)/shard_map/ppermute | solution.py:478
  33.7 4.0 %all-to-all-done.1 = f32[32,4,128]{2,1,0:T(4,128)S(1)} async-done(((f32[32,4,128]{2,1,0:T(4,128)}), f32[32,4,128]{2,1,0:T(4,128)S(1)}, u32[]{:S(2)}, u32[]{:S(2)}) %all-to-all-start.1) | async-done | bytes 65568 | tf_op jit(solution)/shard_map/all_to_all | solution.py:479
  37.7 0.0 copy-done
  37.7 0.0 copy-done.3
  37.7 0.0 copy-done.4
  37.7 0.0 copy-done.5
  37.7 0.0 copy-start.1
  37.7 0.0 copy-start.2
  37.8 3.7 %shard_map.142 = (f32[8,5,16,128]{3,2,1,0:T(8,128)S(1)}, f32[10,16,128]{2,1,0:T(8,128)S(1)}, f32[128,128]{1,0:T(8,128)S(1)}, f32[128,128]{1,0:T(8,128)S(1)}, f32[3200,128]{1,0:T(8,128)S(1)}) custom-call(s32[1]{0:T(128)} %bitcast.35.count, f32[128,128]{1,0:T(8,128)S(1)} %bitcast.37, s32[1,128]{1,0:T(1,128)S(1)} %bitcast.44, s32[1,128]{1,0:T(1,128)S(1)} %bitcast.45, ...), custom_call_target="tpu_custom_call" | custom-call | flops 4000000000 | bytes 1000 | tf_op jit(solution)/shard_map/pallas_call | solution.py:480
  41.5 1.7 %collective-permute-start = (f32[10,16,128]{2,1,0:T(8,128)S(1)}, f32[10,16,128]{2,1,0:T(8,128)S(1)}, u32[]{:S(2)}, u32[]{:S(2)}) collective-permute-start(f32[10,16,128]{2,1,0:T(8,128)S(1)} %get-tuple-element.14.vec), channel_id=1, source_target_pairs={{0,1},{1,0},{2,3},{3,2},{4,5},{5,4},{6,7},{7,6},{8,9},{9,8},{10,11... | collective-permute-start | bytes 245768 | tf_op jit(solution)/shard_map/ppermute | solution.py:487
  43.2 2.4 %collective-permute-done.near = f32[10,16,128]{2,1,0:T(8,128)S(1)} collective-permute-done((f32[10,16,128]{2,1,0:T(8,128)S(1)}, f32[10,16,128]{2,1,0:T(8,128)S(1)}, u32[]{:S(2)}, u32[]{:S(2)}) %collective-permute-start) | collective-permute-done | bytes 81952 | tf_op jit(solution)/shard_map/ppermute | solution.py:487
  45.6 0.1 shard_map.143
  45.6 3.5 %collective-permute-start.2 = (f32[5,16,128]{2,1,0:T(8,128)S(1)}, f32[5,16,128]{2,1,0:T(8,128)S(1)}, u32[]{:S(2)}, u32[]{:S(2)}) collective-permute-start(f32[5,16,128]{2,1,0:T(8,128)S(1)} %shard_map.143), channel_id=1, source_target_pairs={{0,3},{1,2},{2,1},{3,0},{4,7},{5,6},{6,5},{7,4},{8,11},{9,10},{10,... | collective-permute-start | bytes 122888 | tf_op jit(solution)/shard_map/ppermute | solution.py:489
  49.1 1.4 %collective-permute-done.2.beyond = f32[5,16,128]{2,1,0:T(8,128)S(1)} collective-permute-done((f32[5,16,128]{2,1,0:T(8,128)S(1)}, f32[5,16,128]{2,1,0:T(8,128)S(1)}, u32[]{:S(2)}, u32[]{:S(2)}) %collective-permute-start.2) | collective-permute-done | bytes 40992 | tf_op jit(solution)/shard_map/ppermute | solution.py:489
  50.5 0.0 collective-permute-done.3.far
  50.5 0.0 copy-done.1
  50.5 0.0 copy-done.2
  50.5 1.7 %shard_map.145 = (f32[16,5,8,128]{3,2,1,0:T(8,128)}, f32[128,128]{1,0:T(8,128)S(1)}) custom-call(s32[1]{0:T(128)} %bitcast.z_ref, f32[10,16,128]{2,1,0:T(8,128)S(1)} %get-tuple-element.14.vec, f32[10,16,128]{2,1,0:T(8,128)S(1)} %collective-permute-done.near, f32[5,16,128]{2,1,0:T(8,128)S(1)} %collective-permute-done.2.beyond, ...), custom_call_target="tpu_custom_call" | custom-call | flops 2000000000 | bytes 1000 | tf_op jit(solution)/shard_map/pallas_call | solution.py:490
  52.2 17.4 %all_to_all.21 = f32[128,1,128]{2,1,0:T(1,128)S(1)} all-to-all(f32[128,1,128]{2,1,0:T(1,128)S(1)} %bitcast.38), channel_id=1, replica_groups=mesh['stream'=32,'span'=4] {'stream','span'}, dimensions={0} | all-to-all | bytes 131072 | tf_op jit(solution)/shard_map/all_to_all | solution.py:496
  69.5 0.7 %shard_map.146 = f32[3,16]{1,0:T(4,128)} custom-call(f32[128,128]{1,0:T(8,128)S(1)} %bitcast.36), custom_call_target="tpu_custom_call" | custom-call | bytes 1000 | tf_op jit(solution)/shard_map/pallas_call | solution.py:497
Async XLA Ops:
  6.4 18.9 %all-to-all-start = ((f32[32,24,128]{2,1,0:T(8,128)}), f32[32,24,128]{2,1,0:T(8,128)S(1)}, u32[]{:S(2)}, u32[]{:S(2)}) async-start(f32[32,24,128]{2,1,0:T(8,128)} %bitcast.47), calls=%async_computation | async-start | bytes 786432 | tf_op jit(solution)/shard_map/all_to_all | solution.py:471
  15.0 22.7 %copy-start = (f32[16,8,5,5,128]{4,1,3,2,0:T(8,128)S(1)}, f32[16,8,5,5,128]{4,1,3,2,0:T(8,128)}, u32[]{:S(2)}) copy-start(f32[16,8,5,5,128]{4,1,3,2,0:T(8,128)} %param.19) | copy-start | bytes 4915204
  15.0 22.7 %copy-start.3 = (s32[1,1,128]{2,1,0:T(1,128)S(1)}, s32[1,1,128]{2,1,0:T(1,128)}, u32[]{:S(2)}) copy-start(s32[1,1,128]{2,1,0:T(1,128)} %param.22) | copy-start | bytes 1540
  15.0 22.7 %copy-start.4 = (s32[1,1,128]{2,1,0:T(1,128)S(1)}, s32[1,1,128]{2,1,0:T(1,128)}, u32[]{:S(2)}) copy-start(s32[1,1,128]{2,1,0:T(1,128)} %param.23) | copy-start | bytes 1540
  15.0 22.7 %copy-start.5 = (f32[1,1,128]{2,1,0:T(1,128)S(1)}, f32[1,1,128]{2,1,0:T(1,128)}, u32[]{:S(2)}) copy-start(f32[1,1,128]{2,1,0:T(1,128)} %param.24) | copy-start | bytes 1540
  15.0 17.2 %collective-permute-start.1 = (f32[75,16,128]{2,1,0:T(8,128)S(1)}, f32[75,16,128]{2,1,0:T(8,128)S(1)}, u32[]{:S(2)}, u32[]{:S(2)}) collective-permute-start(f32[75,16,128]{2,1,0:T(8,128)S(1)} %get-tuple-element.15.mats), channel_id=1, source_target_pairs={{1,0},{2,3},{3,2},{5,4},{6,7},{7,6},{9,8},{10,11},{11,10},{13,12},... | collective-permute-start | bytes 1843208 | tf_op jit(solution)/shard_map/ppermute | solution.py:472
  26.8 10.9 %all-to-all-start.1 = ((f32[32,4,128]{2,1,0:T(4,128)}), f32[32,4,128]{2,1,0:T(4,128)S(1)}, u32[]{:S(2)}, u32[]{:S(2)}) async-start(f32[32,4,128]{2,1,0:T(4,128)} %shard_map.141), calls=%async_computation.1 | async-start | bytes 131072 | tf_op jit(solution)/shard_map/all_to_all | solution.py:479
  32.4 18.0 %collective-permute-start.3 = (f32[25,16,128]{2,1,0:T(8,128)S(1)}, f32[25,16,128]{2,1,0:T(8,128)S(1)}, u32[]{:S(2)}, u32[]{:S(2)}) collective-permute-start(f32[25,16,128]{2,1,0:T(8,128)S(1)} %shard_map.144), channel_id=1, source_target_pairs={{3,0},{2,1},{7,4},{6,5},{11,8},{10,9},{15,12},{14,13},{19,16},{18,... | collective-permute-start | bytes 614408 | tf_op jit(solution)/shard_map/ppermute | solution.py:478
  37.7 12.8 %copy-start.1 = (bf16[16,8,3,5,128]{4,1,3,2,0:T(8,128)(2,1)S(1)}, bf16[16,8,3,5,128]{4,1,3,2,0:T(8,128)(2,1)}, u32[]{:S(2)}) copy-start(bf16[16,8,3,5,128]{4,1,3,2,0:T(8,128)(2,1)} %param.21) | copy-start | bytes 1474564
  37.7 12.7 %copy-start.2 = (f32[16,8,5,128]{3,1,2,0:T(8,128)S(1)}, f32[16,8,5,128]{3,1,2,0:T(8,128)}, u32[]{:S(2)}) copy-start(f32[16,8,5,128]{3,1,2,0:T(8,128)} %param.14) | copy-start | bytes 983044
  41.5 4.1 %collective-permute-start = (f32[10,16,128]{2,1,0:T(8,128)S(1)}, f32[10,16,128]{2,1,0:T(8,128)S(1)}, u32[]{:S(2)}, u32[]{:S(2)}) collective-permute-start(f32[10,16,128]{2,1,0:T(8,128)S(1)} %get-tuple-element.14.vec), channel_id=1, source_target_pairs={{0,1},{1,0},{2,3},{3,2},{4,5},{5,4},{6,7},{7,6},{8,9},{9,8},{10,11... | collective-permute-start | bytes 245768 | tf_op jit(solution)/shard_map/ppermute | solution.py:487
  45.6 4.8 %collective-permute-start.2 = (f32[5,16,128]{2,1,0:T(8,128)S(1)}, f32[5,16,128]{2,1,0:T(8,128)S(1)}, u32[]{:S(2)}, u32[]{:S(2)}) collective-permute-start(f32[5,16,128]{2,1,0:T(8,128)S(1)} %shard_map.143), channel_id=1, source_target_pairs={{0,3},{1,2},{2,1},{3,0},{4,7},{5,6},{6,5},{7,4},{8,11},{9,10},{10,... | collective-permute-start | bytes 122888 | tf_op jit(solution)/shard_map/ppermute | solution.py:489
